TPU v7x, 32 devices: a whole 2x2x4 slice. The times are simulated.
32 devices in a mesh: row: 8 (over y, x, core), col: 4 (over z).
Axes of the slice: x: 2, y: 2, z: 4, core: 2. Of those that a mesh axis runs over, the one named last changes fastest.
Arguments:
- prior_voltage: float32 [4, 1024, 2048], P(None, 'row', 'col'), may hold values from 0.5 to 1.5
- baseline_admittance: float32 [4, 1024, 2048], P(None, 'row', 'col'), may hold values from 0.5 to 2
- block_warmth: float32 [4, 256, 512], P(None, 'row', 'col'), may hold values from 0 to 2
- interlayer_indicator: int32 [3, 1024, 2048], P(None, 'row', 'col'), may hold values 0 or 1
- feeder_indicator: int32 [4, 1024, 2048], P(None, 'row', 'col'), may hold values 0 or 1
- injected_amperes: float32 [4, 1024, 2048], P(None, 'row', 'col'), may hold values from 0.5 to 4
Outputs:
- revised_voltage: float32 [4, 1024, 2048], P(None, 'row', 'col')
- revised_warmth: float32 [4, 256, 512], P(None, 'row', 'col')
All inputs are finite; a program needn't handle non-finite values. No bound on the sum of `interlayer_indicator` or of `feeder_indicator` on one device may be relied on, other than what follows from the above.
Results may differ from a plain program's by a relative error of at most 0.00002.
Values sent between devices are 32-bit elements; how exact they have to be, the bound alone decides.
No kernel may reach another device: no remote copies, remote signals or barrier semaphores. Data moves between devices by JAX's collectives and lax.ppermute only.
A program may use at most 128 MiB of HBM per device.

v0:
```python
import jax
import jax.numpy as jnp
from jax import lax
from jax.sharding import PartitionSpec as P

BLOCK_REFINE = 4
SWEEPS = 3
HEAT_SWEEPS = 4


warmth_sensitivity = 0.5
via_cond = 1.0
leak_cond = 0.2
spectrum_low = 0.05
spectrum_high = 1.95
warming_weight = 0.3
layer_admittance = 1.0
drain_admittance = 1.0
heat_gain = 0.0625
interval_length = 0.12


def padded(x, sides, width):
    for axis, dim in sides:
        size, length = (lax.axis_size(axis), x.shape[dim])
        up = [(i, (i + 1) % size) for i in range(size - 1)]
        down = [(j, i) for i, j in up]
        last = lax.slice_in_dim(x, length - width, length, axis=dim)
        leading = lax.slice_in_dim(x, 0, width, axis=dim)
        before = lax.ppermute(last, axis, up)
        after = lax.ppermute(leading, axis, down)
        x = jnp.concatenate([before, x, after], axis=dim)
    return x


def cropped_array(voltage_grid, margin):
    if margin == 0:
        return voltage_grid
    return voltage_grid[
        :, margin : voltage_grid.shape[1] - margin, margin : voltage_grid.shape[2] - margin
    ]


def neighbours(voltage_grid):
    return (
        voltage_grid[:, :-2, 1:-1],
        voltage_grid[:, 2:, 1:-1],
        voltage_grid[:, 1:-1, :-2],
        voltage_grid[:, 1:-1, 2:],
    )


def planar_edges(cond_pad):
    center = cond_pad[:, 1:-1, 1:-1]
    return tuple((jnp.sqrt(center * other) for other in neighbours(cond_pad)))


def vertical(voltage_grid, vias):
    nought_value = jnp.zeros_like(voltage_grid[:1])
    return jnp.concatenate([vias * voltage_grid[1:], nought_value], 0) + jnp.concatenate(
        [nought_value, vias * voltage_grid[:-1]], 0
    )


def via_total(vias):
    nought_value = jnp.zeros_like(vias[:1])
    return jnp.concatenate([vias, nought_value], 0) + jnp.concatenate([nought_value, vias], 0)


def operate(field_pad, edges, vias, diag):
    center = field_pad[:, 1:-1, 1:-1]
    near = jnp.zeros_like(center)
    for edge, other in zip(edges, neighbours(field_pad)):
        near = near + edge * other
    return diag * center - near - vertical(center, vias)


def joule_power(field_pad, edges, vias):
    center = field_pad[:, 1:-1, 1:-1]
    total = leak_cond * center * center
    for edge, other in zip(edges, neighbours(field_pad)):
        total = total + 0.5 * edge * (center - other) ** 2
    drop = vias * (center[:-1] - center[1:]) ** 2
    nought_value = jnp.zeros_like(center[:1])
    return total + 0.5 * (
        jnp.concatenate([drop, nought_value], 0) + jnp.concatenate([nought_value, drop], 0)
    )


def warming_increment(warmth_excess, diffusivity, warmth_border, diffusivity_border, warming_load):
    energy_flow = jnp.zeros_like(warmth_excess)
    for partner_warmth, partner_diffusivity in zip(
        neighbours(warmth_border), neighbours(diffusivity_border)
    ):
        energy_flow = energy_flow + jnp.sqrt(diffusivity * partner_diffusivity) * (
            partner_warmth - warmth_excess
        )
    nought_value = jnp.zeros_like(warmth_excess[:1])
    upright_flow = layer_admittance * (
        jnp.concatenate([warmth_excess[1:] - warmth_excess[:-1], nought_value], 0)
        + jnp.concatenate([nought_value, warmth_excess[:-1] - warmth_excess[1:]], 0)
    )
    layer_total = warmth_excess.shape[0]
    upper_layer = (
        lax.broadcasted_iota(jnp.int32, (layer_total, 1, 1), 0) == layer_total - 1
    ).astype(jnp.float32)
    return warmth_excess + interval_length * (
        energy_flow + upright_flow + warming_load - drain_admittance * upper_layer * warmth_excess
    )


def inside_mask(rows, cols, row_first, col_first, row_total, col_total):
    row_ids = lax.broadcasted_iota(jnp.int32, (1, rows, cols), 1) + row_first
    col_ids = lax.broadcasted_iota(jnp.int32, (1, rows, cols), 2) + col_first
    inside = (row_ids >= 0) & (row_ids < row_total) & (col_ids >= 0) & (col_ids < col_total)
    return inside.astype(jnp.float32)


def masked_kappa(warmth_border, inside):
    return jnp.exp(-warming_weight * warmth_border) * inside


def rim(voltage_grid):
    return padded(voltage_grid, (("row", 1), ("col", 2)), 1)


def on_device(
    prior_voltage,
    baseline_admittance,
    block_warmth,
    interlayer_indicator,
    feeder_indicator,
    injected_amperes,
):
    warmth_on_points = jnp.repeat(
        jnp.repeat(block_warmth, BLOCK_REFINE, axis=1), BLOCK_REFINE, axis=2
    )
    admittance = baseline_admittance * jnp.exp(-warmth_sensitivity * warmth_on_points)
    vias = via_cond * interlayer_indicator.astype(jnp.float32)
    inject = feeder_indicator.astype(jnp.float32) * injected_amperes
    width = 1
    field_pad, cond_pad = (
        padded(prior_voltage, (("row", 1), ("col", 2)), 1),
        padded(admittance, (("row", 1), ("col", 2)), 1),
    )
    inject_pad, vias_pad = (inject, vias)
    side_margin = 0
    edge_margin = width - 1
    edges_all = planar_edges(cond_pad)
    diag_all = (
        leak_cond
        + edges_all[0]
        + edges_all[1]
        + edges_all[2]
        + edges_all[3]
        + via_total(cropped_array(vias_pad, side_margin - edge_margin))
    )

    def pieces(want):
        edges = tuple((cropped_array(edge, edge_margin - want) for edge in edges_all))
        return (
            edges,
            cropped_array(vias_pad, side_margin - want),
            cropped_array(diag_all, edge_margin - want),
            cropped_array(inject_pad, side_margin - want),
        )

    center_c = 0.5 * (spectrum_high + spectrum_low)
    half = 0.5 * (spectrum_high - spectrum_low)
    sigma = center_c / half
    rho = 1.0 / sigma
    field_margin = width
    out_margin = field_margin - 1
    edges, vias_m, diag_m, inject_m = pieces(out_margin)
    resid = inject_m - operate(field_pad, edges, vias_m, diag_m)
    step = resid / (diag_m * center_c)
    step_margin = out_margin
    voltage_grid = field_pad
    for sweep in range(SWEEPS):
        voltage_grid = cropped_array(voltage_grid, field_margin - step_margin) + step
        field_margin = step_margin
        if sweep < SWEEPS - 1:
            voltage_grid = rim(voltage_grid)
            field_margin = 1
            out_margin = field_margin - 1
            edges, vias_m, diag_m, inject_m = pieces(out_margin)
            resid = inject_m - operate(voltage_grid, edges, vias_m, diag_m)
            rho_new = 1.0 / (2.0 * sigma - rho)
            step = rho_new * rho * cropped_array(
                step, step_margin - out_margin
            ) + 2.0 * rho_new / half * (resid / diag_m)
            step_margin = out_margin
            rho = rho_new
    revised_voltage = cropped_array(voltage_grid, field_margin)
    voltage_grid = rim(voltage_grid)
    field_margin = 1
    edges, vias_m, diag_m, inject_m = pieces(0)
    power = joule_power(cropped_array(voltage_grid, field_margin - 1), edges, vias_m)
    layer_total, rows, cols = power.shape
    warming_load = (
        power.reshape(
            layer_total, rows // BLOCK_REFINE, BLOCK_REFINE, cols // BLOCK_REFINE, BLOCK_REFINE
        ).sum(axis=(2, 4))
        * heat_gain
    )
    heated_heightwise = block_warmth.shape[1]
    heated_widthwise = block_warmth.shape[2]
    row_total = heated_heightwise * lax.axis_size("row")
    col_total = heated_widthwise * lax.axis_size("col")
    leading_line_offset = lax.axis_index("row") * heated_heightwise
    col_start = lax.axis_index("col") * heated_widthwise
    depth = HEAT_SWEEPS
    warmth_border, heat_pad = (
        padded(block_warmth, (("row", 1), ("col", 2)), depth),
        padded(warming_load, (("row", 1), ("col", 2)), depth),
    )
    inside_all = inside_mask(
        heated_heightwise + 2 * depth,
        heated_widthwise + 2 * depth,
        leading_line_offset - depth,
        col_start - depth,
        row_total,
        col_total,
    )
    warmth_excess = warmth_border
    for sweep in range(depth):
        diffusivity_border = masked_kappa(warmth_excess, cropped_array(inside_all, sweep))
        warmth_excess = warming_increment(
            cropped_array(warmth_excess, 1),
            cropped_array(diffusivity_border, 1),
            warmth_excess,
            diffusivity_border,
            cropped_array(heat_pad, sweep + 1),
        )
    return (revised_voltage, warmth_excess)


def solution(mesh):
    placed = (
        P(None, "row", "col"),
        P(None, "row", "col"),
        P(None, "row", "col"),
        P(None, "row", "col"),
        P(None, "row", "col"),
        P(None, "row", "col"),
    )
    return jax.shard_map(
        on_device,
        mesh=mesh,
        in_specs=placed,
        out_specs=(P(None, "row", "col"), P(None, "row", "col")),
        check_vma=False,
    )
```

profile of v0, /device:TPU:0, one launch (start us, length us, event | category | flops | bytes accessed | tf_op | source)
XLA Modules:
  0.0 219.1 jit_solution(11264072095372323271)
XLA Ops:
  1.7 1.6 copy.43
  4.3 2.4 %collective-permute-start = (f32[4,1,512]{2,0,1:T(4,128)S(1)}, f32[4,1,512]{2,0,1:T(4,128)S(1)}, u32[]{:S(2)}, u32[]{:S(2)}) collective-permute-start(f32[4,1,512]{2,0,1:T(4,128)S(1)} %copy.44), channel_id=1, source_target_pairs={{0,4},{4,8},{8,12},{12,16},{16,20},{20,24},{24,28},{1,5},{5,9},{9,... | collective-permute-start | bytes 24584 | tf_op jit(solution)/shard_map/ppermute | solution.py:30
  7.0 1.3 collective-permute-start.1
  8.3 0.9 fusion.137
  9.2 5.1 %collective-permute-start.4 = (f32[4,1,512]{2,0,1:T(4,128)S(1)}, f32[4,1,512]{2,0,1:T(4,128)S(1)}, u32[]{:S(2)}, u32[]{:S(2)}) collective-permute-start(f32[4,1,512]{2,0,1:T(4,128)S(1)} %copy.84), channel_id=1, source_target_pairs={{0,4},{4,8},{8,12},{12,16},{16,20},{20,24},{24,28},{1,5},{5,9},{9,... | collective-permute-start | bytes 24584 | tf_op jit(solution)/shard_map/ppermute | solution.py:30
  14.3 1.3 collective-permute-start.5
  16.4 4.3 %collective-permute-start.16 = (f32[4,4,128]{2,1,0:T(4,128)S(1)}, f32[4,4,128]{2,1,0:T(4,128)S(1)}, u32[]{:S(2)}, u32[]{:S(2)}) collective-permute-start(f32[4,4,128]{2,1,0:T(4,128)S(1)} %get-tuple-element.62), channel_id=1, source_target_pairs={{0,4},{4,8},{8,12},{12,16},{16,20},{20,24},{24,28},{1,5},{5,9},{9,... | collective-permute-start | bytes 24584 | tf_op jit(solution)/shard_map/ppermute | solution.py:30
  20.6 1.6 copy.63
  22.5 1.5 copy.50
  24.0 1.3 slice_multiply_fusion.5
  25.3 1.3 copy.45
  26.7 1.4 copy.47
  28.0 0.9 pad_maximum_fusion.56
  28.9 3.5 %collective-permute-start.2 = (f32[4,130,1]{1,2,0:T(1,128)S(1)}, f32[4,130,1]{1,2,0:T(1,128)S(1)}, u32[]{:S(2)}, u32[]{:S(2)}) collective-permute-start(f32[4,130,1]{1,2,0:T(1,128)S(1)} %get-tuple-element.31), channel_id=1, source_target_pairs={{0,1},{1,2},{2,3},{4,5},{5,6},{6,7},{8,9},{9,10},{10,11},{12,13},{... | collective-permute-start | bytes 6248 | tf_op jit(solution)/shard_map/ppermute | solution.py:30
  32.4 1.3 collective-permute-start.3
  33.7 1.4 copy.53
  35.2 1.4 copy.57
  37.4 4.5 %collective-permute-start.6 = (f32[4,130,1]{1,2,0:T(1,128)S(1)}, f32[4,130,1]{1,2,0:T(1,128)S(1)}, u32[]{:S(2)}, u32[]{:S(2)}) collective-permute-start(f32[4,130,1]{1,2,0:T(1,128)S(1)} %get-tuple-element.32), channel_id=1, source_target_pairs={{0,1},{1,2},{2,3},{4,5},{5,6},{6,7},{8,9},{9,10},{10,11},{12,13},{... | collective-permute-start | bytes 6248 | tf_op jit(solution)/shard_map/ppermute | solution.py:30
  41.9 1.3 collective-permute-start.7
  43.3 1.0 convert_element_type.38
  44.3 2.5 %copy.40 = s32[4,128,512]{1,2,0:T(8,128)} copy(s32[4,128,512]{2,1,0:T(8,128)} %param.10) | data formatting | bytes 2097152 | tf_op args[4]
  46.8 2.5 %copy.41 = f32[4,128,512]{1,2,0:T(8,128)} copy(f32[4,128,512]{2,1,0:T(8,128)} %param.11) | data formatting | bytes 2097152 | tf_op args[5]
  49.4 1.3 collective-permute-start.17
  50.7 10.6 %fusion.127 = (f32[4,128,512]{1,2,0:T(8,128)S(1)}, f32[4,128,512]{1,2,0:T(8,128)}, f32[4,128,512]{1,2,0:T(8,128)}, f32[4,128,512]{1,2,0:T(8,128)}, f32[4,128,512]{1,2,0:T(8,128)}, /*index=5*/f32[4,128,512]{1,2,0:T(8,128)}) fusion(f32[4,128,512]{1,2,0:T(8,128)} %copy-done, f32[3,128,512]{1,2,0:T(8,128)} %get-tuple-element.39, ...), kind=kLoop, calls=%fused_computation.252 | loop fusion | flops 11010048 | bytes 12886144 | tf_op jit(solution)/shard_map/add | solution.py:180
  61.4 1.3 fusion.135
  62.7 1.5 copy.64
  64.2 3.4 %collective-permute-start.8 = (f32[4,1,512]{2,0,1:T(4,128)S(1)}, f32[4,1,512]{2,0,1:T(4,128)S(1)}, u32[]{:S(2)}, u32[]{:S(2)}) collective-permute-start(f32[4,1,512]{2,0,1:T(4,128)S(1)} %copy.64), channel_id=1, source_target_pairs={{0,4},{4,8},{8,12},{12,16},{16,20},{20,24},{24,28},{1,5},{5,9},{9,... | collective-permute-start | bytes 24584 | tf_op jit(solution)/shard_map/ppermute | solution.py:30
  68.0 1.3 collective-permute-start.9
  70.2 2.1 collective-permute-done.9
  72.3 1.3 copy.67
  74.5 4.4 %collective-permute-start.10 = (f32[4,130,1]{1,2,0:T(1,128)S(1)}, f32[4,130,1]{1,2,0:T(1,128)S(1)}, u32[]{:S(2)}, u32[]{:S(2)}) collective-permute-start(f32[4,130,1]{1,2,0:T(1,128)S(1)} %get-tuple-element.28), channel_id=1, source_target_pairs={{0,1},{1,2},{2,3},{4,5},{5,6},{6,7},{8,9},{9,10},{10,11},{12,13},{... | collective-permute-start | bytes 6248 | tf_op jit(solution)/shard_map/ppermute | solution.py:30
  78.9 1.3 collective-permute-start.11
  80.3 4.1 %collective-permute-done.11 = f32[4,130,1]{1,2,0:T(1,128)S(1)} collective-permute-done((f32[4,130,1]{1,2,0:T(1,128)S(1)}, f32[4,130,1]{1,2,0:T(1,128)S(1)}, u32[]{:S(2)}, u32[]{:S(2)}) %collective-permute-start.11) | collective-permute-done | bytes 2112 | tf_op jit(solution)/shard_map/ppermute | solution.py:31
  84.4 6.9 %fusion.126 = (f32[4,128,512]{1,2,0:T(8,128)S(1)}, f32[4,128,512]{1,2,0:T(8,128)}) fusion(f32[4,128,512]{1,2,0:T(8,128)S(1)} %get-tuple-element.18, f32[3,128,512]{1,2,0:T(8,128)S(1)} %get-tuple-element.37, f32[3,128,512]{1,2,0:T(8,128)S(1)} %get-tuple-element.36, f32[4,128,512]{1,2,0:T(8,128)} %get-tuple-element.23, ...), kind=kLoop, calls=%fused_computation.251 | loop fusion | flops 8650752 | bytes 12865600 | tf_op jit(solution)/shard_map/add | solution.py:180
  91.3 1.3 fusion.134
  92.6 1.5 copy.70
  94.2 2.9 %collective-permute-start.12 = (f32[4,1,512]{2,0,1:T(4,128)S(1)}, f32[4,1,512]{2,0,1:T(4,128)S(1)}, u32[]{:S(2)}, u32[]{:S(2)}) collective-permute-start(f32[4,1,512]{2,0,1:T(4,128)S(1)} %copy.70), channel_id=1, source_target_pairs={{0,4},{4,8},{8,12},{12,16},{16,20},{20,24},{24,28},{1,5},{5,9},{9,... | collective-permute-start | bytes 24584 | tf_op jit(solution)/shard_map/ppermute | solution.py:30
  97.4 1.3 collective-permute-start.13
  99.1 4.0 %collective-permute-done.13 = f32[4,1,512]{2,0,1:T(4,128)S(1)} collective-permute-done((f32[4,1,512]{2,0,1:T(4,128)S(1)}, f32[4,1,512]{2,0,1:T(4,128)S(1)}, u32[]{:S(2)}, u32[]{:S(2)}) %collective-permute-start.13) | collective-permute-done | bytes 8224 | tf_op jit(solution)/shard_map/ppermute | solution.py:31
  103.1 1.3 copy.73
  105.3 3.5 %collective-permute-start.14 = (f32[4,130,1]{1,2,0:T(1,128)S(1)}, f32[4,130,1]{1,2,0:T(1,128)S(1)}, u32[]{:S(2)}, u32[]{:S(2)}) collective-permute-start(f32[4,130,1]{1,2,0:T(1,128)S(1)} %get-tuple-element.26), channel_id=1, source_target_pairs={{0,1},{1,2},{2,3},{4,5},{5,6},{6,7},{8,9},{9,10},{10,11},{12,13},{... | collective-permute-start | bytes 6248 | tf_op jit(solution)/shard_map/ppermute | solution.py:30
  108.8 1.5 collective-permute-start.15
  110.4 3.9 %collective-permute-done.15 = f32[4,130,1]{1,2,0:T(1,128)S(1)} collective-permute-done((f32[4,130,1]{1,2,0:T(1,128)S(1)}, f32[4,130,1]{1,2,0:T(1,128)S(1)}, u32[]{:S(2)}, u32[]{:S(2)}) %collective-permute-start.15) | collective-permute-done | bytes 2112 | tf_op jit(solution)/shard_map/ppermute | solution.py:31
  114.3 6.1 %add_add_fusion = f32[4,128,512]{1,2,0:T(8,128)S(1)} fusion(f32[4,128,512]{1,2,0:T(8,128)S(1)} %get-tuple-element.16, f32[4,128,512]{1,2,0:T(8,128)} %get-tuple-element.23, f32[4,130,1]{1,2,0:T(1,128)S(1)} %collective-permute-done.15, f32[4,1,512]{1,2,0:T(8,128)} %copy.73, f32[4,1,512]{1,2,0:T(8,128)} %copy-done.1, f32[4,128,512]{1,2,0:T(8,128)} %get-tuple-element.22, ...), kind=kLoop, calls=%fused_computation.99 | loop fusion | flops 8650752 | bytes 11817024 | tf_op jit(solution)/shard_map/add | solution.py:180
  120.4 1.3 fusion.133
  121.7 1.5 copy.76
  123.3 3.0 %collective-permute-start.20 = (f32[4,1,512]{2,0,1:T(4,128)S(1)}, f32[4,1,512]{2,0,1:T(4,128)S(1)}, u32[]{:S(2)}, u32[]{:S(2)}) collective-permute-start(f32[4,1,512]{2,0,1:T(4,128)S(1)} %copy.76), channel_id=1, source_target_pairs={{0,4},{4,8},{8,12},{12,16},{16,20},{20,24},{24,28},{1,5},{5,9},{9,... | collective-permute-start | bytes 24584 | tf_op jit(solution)/shard_map/ppermute | solution.py:30
  126.6 1.3 collective-permute-start.21
  128.6 3.5 %collective-permute-start.18 = (f32[4,40,4]{2,1,0:T(8,128)}, f32[4,40,4]{2,1,0:T(8,128)S(1)}, u32[]{:S(2)}, u32[]{:S(2)}) collective-permute-start(f32[4,40,4]{2,1,0:T(8,128)} %get-tuple-element.58), channel_id=1, source_target_pairs={{0,1},{1,2},{2,3},{4,5},{5,6},{6,7},{8,9},{9,10},{10,11},{12,13},{... | collective-permute-start | bytes 7688 | tf_op jit(solution)/shard_map/ppermute | solution.py:30
  132.1 1.3 collective-permute-start.19
  133.8 1.3 copy.79
  136.0 4.5 %collective-permute-start.22 = (f32[4,130,1]{1,2,0:T(1,128)S(1)}, f32[4,130,1]{1,2,0:T(1,128)S(1)}, u32[]{:S(2)}, u32[]{:S(2)}) collective-permute-start(f32[4,130,1]{1,2,0:T(1,128)S(1)} %get-tuple-element.24), channel_id=1, source_target_pairs={{0,1},{1,2},{2,3},{4,5},{5,6},{6,7},{8,9},{9,10},{10,11},{12,13},{... | collective-permute-start | bytes 6248 | tf_op jit(solution)/shard_map/ppermute | solution.py:30
  140.5 1.3 collective-permute-start.23
  142.0 4.1 %collective-permute-done.23 = f32[4,130,1]{1,2,0:T(1,128)S(1)} collective-permute-done((f32[4,130,1]{1,2,0:T(1,128)S(1)}, f32[4,130,1]{1,2,0:T(1,128)S(1)}, u32[]{:S(2)}, u32[]{:S(2)}) %collective-permute-start.23) | collective-permute-done | bytes 2112 | tf_op jit(solution)/shard_map/ppermute | solution.py:31
  146.0 3.8 %fusion.4 = f32[4,128,512]{1,2,0:T(8,128)S(1)} fusion(f32[4,128,512]{1,2,0:T(8,128)S(1)} %add_add_fusion, f32[4,130,1]{1,2,0:T(1,128)S(1)} %collective-permute-done.23, f32[4,1,512]{1,2,0:T(8,128)} %copy.79, f32[4,1,512]{1,2,0:T(8,128)S(1)} %copy.77, f32[4,130,1]{1,2,0:T(1,128)S(1)} %collective-permute-done.22, f32[3,128,512]{1,2,0:T(8,128)S(1)} %fusion.59, ...), kind=kLoop, calls=%fused_computation.5 | loop fusion | flops 8650752 | bytes 7098432 | tf_op jit(solution)/shard_map/add | solution.py:85
  150.2 36.0 %reshape.106 = f32[4,32,4,128,4]{4,3,2,1,0:T(8,128)} reshape(f32[4,128,512]{2,1,0:T(8,128)S(1)} %copy.82) | data formatting | bytes 2097152 | tf_op jit(solution)/shard_map/reshape | solution.py:201
  186.1 12.2 %reduce_sum.9 = f32[4,32,128]{2,1,0:T(8,128)S(1)} reduce(f32[4,32,4,128,4]{4,3,2,1,0:T(8,128)} %reshape.106, f32[]{:T(128)} %constant.23.clone.1), dimensions={2,4}, to_apply=%region_0.0 | reduce | flops 245760 | bytes 1114116 | tf_op jit(solution)/shard_map/reduce_sum | solution.py:203
  198.4 2.8 %collective-permute-start.24 = (f32[4,4,128]{2,1,0:T(4,128)S(1)}, f32[4,4,128]{2,1,0:T(4,128)S(1)}, u32[]{:S(2)}, u32[]{:S(2)}) collective-permute-start(f32[4,4,128]{2,1,0:T(4,128)S(1)} %get-tuple-element.64), channel_id=1, source_target_pairs={{0,4},{4,8},{8,12},{12,16},{16,20},{20,24},{24,28},{1,5},{5,9},{9,... | collective-permute-start | bytes 24584 | tf_op jit(solution)/shard_map/ppermute | solution.py:30
  201.2 1.3 collective-permute-start.25
  202.6 4.9 %collective-permute-done.25 = f32[4,4,128]{2,1,0:T(4,128)S(1)} collective-permute-done((f32[4,4,128]{2,1,0:T(4,128)S(1)}, f32[4,4,128]{2,1,0:T(4,128)S(1)}, u32[]{:S(2)}, u32[]{:S(2)}) %collective-permute-start.25) | collective-permute-done | bytes 8224 | tf_op jit(solution)/shard_map/ppermute | solution.py:31
  207.7 2.2 %collective-permute-start.26 = (f32[4,40,4]{2,1,0:T(8,128)S(1)}, f32[4,40,4]{2,1,0:T(8,128)S(1)}, u32[]{:S(2)}, u32[]{:S(2)}) collective-permute-start(f32[4,40,4]{2,1,0:T(8,128)S(1)} %get-tuple-element.60), channel_id=1, source_target_pairs={{0,1},{1,2},{2,3},{4,5},{5,6},{6,7},{8,9},{9,10},{10,11},{12,13},{... | collective-permute-start | bytes 7688 | tf_op jit(solution)/shard_map/ppermute | solution.py:30
  209.9 1.3 collective-permute-start.27
  211.3 1.3 copy.83
  212.6 3.6 %collective-permute-done.27 = f32[4,40,4]{2,1,0:T(8,128)S(1)} collective-permute-done((f32[4,40,4]{2,1,0:T(8,128)S(1)}, f32[4,40,4]{2,1,0:T(8,128)S(1)}, u32[]{:S(2)}, u32[]{:S(2)}) %collective-permute-start.27) | collective-permute-done | bytes 2592 | tf_op jit(solution)/shard_map/ppermute | solution.py:31
  (80 shorter events, 14.1 us)
Async XLA Ops:
  4.3 21.1 %collective-permute-start = (f32[4,1,512]{2,0,1:T(4,128)S(1)}, f32[4,1,512]{2,0,1:T(4,128)S(1)}, u32[]{:S(2)}, u32[]{:S(2)}) collective-permute-start(f32[4,1,512]{2,0,1:T(4,128)S(1)} %copy.44), channel_id=1, source_target_pairs={{0,4},{4,8},{8,12},{12,16},{16,20},{20,24},{24,28},{1,5},{5,9},{9,... | collective-permute-start | bytes 24584 | tf_op jit(solution)/shard_map/ppermute | solution.py:30
  7.0 19.7 %collective-permute-start.1 = (f32[4,1,512]{2,0,1:T(4,128)S(1)}, f32[4,1,512]{2,0,1:T(4,128)S(1)}, u32[]{:S(2)}, u32[]{:S(2)}) collective-permute-start(f32[4,1,512]{2,0,1:T(4,128)S(1)} %copy.46), channel_id=1, source_target_pairs={{4,0},{8,4},{12,8},{16,12},{20,16},{24,20},{28,24},{5,1},{9,5},{13... | collective-permute-start | bytes 24584 | tf_op jit(solution)/shard_map/ppermute | solution.py:31
  9.2 24.6 %collective-permute-start.4 = (f32[4,1,512]{2,0,1:T(4,128)S(1)}, f32[4,1,512]{2,0,1:T(4,128)S(1)}, u32[]{:S(2)}, u32[]{:S(2)}) collective-permute-start(f32[4,1,512]{2,0,1:T(4,128)S(1)} %copy.84), channel_id=1, source_target_pairs={{0,4},{4,8},{8,12},{12,16},{16,20},{20,24},{24,28},{1,5},{5,9},{9,... | collective-permute-start | bytes 24584 | tf_op jit(solution)/shard_map/ppermute | solution.py:30
  14.3 20.8 %collective-permute-start.5 = (f32[4,1,512]{2,0,1:T(4,128)S(1)}, f32[4,1,512]{2,0,1:T(4,128)S(1)}, u32[]{:S(2)}, u32[]{:S(2)}) collective-permute-start(f32[4,1,512]{2,0,1:T(4,128)S(1)} %copy.85), channel_id=1, source_target_pairs={{4,0},{8,4},{12,8},{16,12},{20,16},{24,20},{28,24},{5,1},{9,5},{13... | collective-permute-start | bytes 24584 | tf_op jit(solution)/shard_map/ppermute | solution.py:31
  16.4 82.3 %collective-permute-start.16 = (f32[4,4,128]{2,1,0:T(4,128)S(1)}, f32[4,4,128]{2,1,0:T(4,128)S(1)}, u32[]{:S(2)}, u32[]{:S(2)}) collective-permute-start(f32[4,4,128]{2,1,0:T(4,128)S(1)} %get-tuple-element.62), channel_id=1, source_target_pairs={{0,4},{4,8},{8,12},{12,16},{16,20},{20,24},{24,28},{1,5},{5,9},{9,... | collective-permute-start | bytes 24584 | tf_op jit(solution)/shard_map/ppermute | solution.py:30
  22.2 28.5 %copy-start = (f32[4,128,512]{1,2,0:T(8,128)}, f32[4,128,512]{1,2,0:T(8,128)S(1)}, u32[]{:S(2)}) copy-start(f32[4,128,512]{1,2,0:T(8,128)S(1)} %copy.63) | copy-start | bytes 3145732
  28.0 70.7 %copy-start.3 = (f32[4,32,128]{2,1,0:T(8,128)S(1)}, f32[4,32,128]{2,1,0:T(8,128)}, u32[]{:S(2)}) copy-start(f32[4,32,128]{2,1,0:T(8,128)} %param.8) | copy-start | bytes 196612
  28.9 20.5 %collective-permute-start.2 = (f32[4,130,1]{1,2,0:T(1,128)S(1)}, f32[4,130,1]{1,2,0:T(1,128)S(1)}, u32[]{:S(2)}, u32[]{:S(2)}) collective-permute-start(f32[4,130,1]{1,2,0:T(1,128)S(1)} %get-tuple-element.31), channel_id=1, source_target_pairs={{0,1},{1,2},{2,3},{4,5},{5,6},{6,7},{8,9},{9,10},{10,11},{12,13},{... | collective-permute-start | bytes 6248 | tf_op jit(solution)/shard_map/ppermute | solution.py:30
  32.4 18.3 %collective-permute-start.3 = (f32[4,130,1]{1,2,0:T(1,128)S(1)}, f32[4,130,1]{1,2,0:T(1,128)S(1)}, u32[]{:S(2)}, u32[]{:S(2)}) collective-permute-start(f32[4,130,1]{1,2,0:T(1,128)S(1)} %get-tuple-element.30), channel_id=1, source_target_pairs={{1,0},{2,1},{3,2},{5,4},{6,5},{7,6},{9,8},{10,9},{11,10},{13,12},{... | collective-permute-start | bytes 6248 | tf_op jit(solution)/shard_map/ppermute | solution.py:31
  37.4 13.3 %collective-permute-start.6 = (f32[4,130,1]{1,2,0:T(1,128)S(1)}, f32[4,130,1]{1,2,0:T(1,128)S(1)}, u32[]{:S(2)}, u32[]{:S(2)}) collective-permute-start(f32[4,130,1]{1,2,0:T(1,128)S(1)} %get-tuple-element.32), channel_id=1, source_target_pairs={{0,1},{1,2},{2,3},{4,5},{5,6},{6,7},{8,9},{9,10},{10,11},{12,13},{... | collective-permute-start | bytes 6248 | tf_op jit(solution)/shard_map/ppermute | solution.py:30
  41.9 8.8 %collective-permute-start.7 = (f32[4,130,1]{1,2,0:T(1,128)S(1)}, f32[4,130,1]{1,2,0:T(1,128)S(1)}, u32[]{:S(2)}, u32[]{:S(2)}) collective-permute-start(f32[4,130,1]{1,2,0:T(1,128)S(1)} %get-tuple-element.33), channel_id=1, source_target_pairs={{1,0},{2,1},{3,2},{5,4},{6,5},{7,6},{9,8},{10,9},{11,10},{13,12},{... | collective-permute-start | bytes 6248 | tf_op jit(solution)/shard_map/ppermute | solution.py:31
  49.4 49.3 %collective-permute-start.17 = (f32[4,4,128]{2,1,0:T(4,128)S(1)}, f32[4,4,128]{2,1,0:T(4,128)S(1)}, u32[]{:S(2)}, u32[]{:S(2)}) collective-permute-start(f32[4,4,128]{2,1,0:T(4,128)S(1)} %get-tuple-element.63), channel_id=1, source_target_pairs={{4,0},{8,4},{12,8},{16,12},{20,16},{24,20},{28,24},{5,1},{9,5},{13... | collective-permute-start | bytes 24584 | tf_op jit(solution)/shard_map/ppermute | solution.py:31
  64.2 5.6 %collective-permute-start.8 = (f32[4,1,512]{2,0,1:T(4,128)S(1)}, f32[4,1,512]{2,0,1:T(4,128)S(1)}, u32[]{:S(2)}, u32[]{:S(2)}) collective-permute-start(f32[4,1,512]{2,0,1:T(4,128)S(1)} %copy.64), channel_id=1, source_target_pairs={{0,4},{4,8},{8,12},{12,16},{16,20},{20,24},{24,28},{1,5},{5,9},{9,... | collective-permute-start | bytes 24584 | tf_op jit(solution)/shard_map/ppermute | solution.py:30
  68.0 4.3 %collective-permute-start.9 = (f32[4,1,512]{2,0,1:T(4,128)S(1)}, f32[4,1,512]{2,0,1:T(4,128)S(1)}, u32[]{:S(2)}, u32[]{:S(2)}) collective-permute-start(f32[4,1,512]{2,0,1:T(4,128)S(1)} %copy.66), channel_id=1, source_target_pairs={{4,0},{8,4},{12,8},{16,12},{20,16},{24,20},{28,24},{5,1},{9,5},{13... | collective-permute-start | bytes 24584 | tf_op jit(solution)/shard_map/ppermute | solution.py:31
  70.2 14.2 %copy-start.2 = (f32[4,1,512]{1,2,0:T(8,128)}, f32[4,1,512]{1,2,0:T(8,128)S(1)}, u32[]{:S(2)}) copy-start(f32[4,1,512]{1,2,0:T(8,128)S(1)} %copy.65) | copy-start | bytes 24580
  74.5 5.9 %collective-permute-start.10 = (f32[4,130,1]{1,2,0:T(1,128)S(1)}, f32[4,130,1]{1,2,0:T(1,128)S(1)}, u32[]{:S(2)}, u32[]{:S(2)}) collective-permute-start(f32[4,130,1]{1,2,0:T(1,128)S(1)} %get-tuple-element.28), channel_id=1, source_target_pairs={{0,1},{1,2},{2,3},{4,5},{5,6},{6,7},{8,9},{9,10},{10,11},{12,13},{... | collective-permute-start | bytes 6248 | tf_op jit(solution)/shard_map/ppermute | solution.py:30
  78.9 5.5 %collective-permute-start.11 = (f32[4,130,1]{1,2,0:T(1,128)S(1)}, f32[4,130,1]{1,2,0:T(1,128)S(1)}, u32[]{:S(2)}, u32[]{:S(2)}) collective-permute-start(f32[4,130,1]{1,2,0:T(1,128)S(1)} %get-tuple-element.29), channel_id=1, source_target_pairs={{1,0},{2,1},{3,2},{5,4},{6,5},{7,6},{9,8},{10,9},{11,10},{13,12},{... | collective-permute-start | bytes 6248 | tf_op jit(solution)/shard_map/ppermute | solution.py:31
  94.2 4.6 %collective-permute-start.12 = (f32[4,1,512]{2,0,1:T(4,128)S(1)}, f32[4,1,512]{2,0,1:T(4,128)S(1)}, u32[]{:S(2)}, u32[]{:S(2)}) collective-permute-start(f32[4,1,512]{2,0,1:T(4,128)S(1)} %copy.70), channel_id=1, source_target_pairs={{0,4},{4,8},{8,12},{12,16},{16,20},{20,24},{24,28},{1,5},{5,9},{9,... | collective-permute-start | bytes 24584 | tf_op jit(solution)/shard_map/ppermute | solution.py:30
  97.4 5.7 %collective-permute-start.13 = (f32[4,1,512]{2,0,1:T(4,128)S(1)}, f32[4,1,512]{2,0,1:T(4,128)S(1)}, u32[]{:S(2)}, u32[]{:S(2)}) collective-permute-start(f32[4,1,512]{2,0,1:T(4,128)S(1)} %copy.72), channel_id=1, source_target_pairs={{4,0},{8,4},{12,8},{16,12},{20,16},{24,20},{28,24},{5,1},{9,5},{13... | collective-permute-start | bytes 24584 | tf_op jit(solution)/shard_map/ppermute | solution.py:31
  99.1 15.2 %copy-start.1 = (f32[4,1,512]{1,2,0:T(8,128)}, f32[4,1,512]{1,2,0:T(8,128)S(1)}, u32[]{:S(2)}) copy-start(f32[4,1,512]{1,2,0:T(8,128)S(1)} %copy.71) | copy-start | bytes 24580
  105.3 5.1 %collective-permute-start.14 = (f32[4,130,1]{1,2,0:T(1,128)S(1)}, f32[4,130,1]{1,2,0:T(1,128)S(1)}, u32[]{:S(2)}, u32[]{:S(2)}) collective-permute-start(f32[4,130,1]{1,2,0:T(1,128)S(1)} %get-tuple-element.26), channel_id=1, source_target_pairs={{0,1},{1,2},{2,3},{4,5},{5,6},{6,7},{8,9},{9,10},{10,11},{12,13},{... | collective-permute-start | bytes 6248 | tf_op jit(solution)/shard_map/ppermute | solution.py:30
  108.8 5.5 %collective-permute-start.15 = (f32[4,130,1]{1,2,0:T(1,128)S(1)}, f32[4,130,1]{1,2,0:T(1,128)S(1)}, u32[]{:S(2)}, u32[]{:S(2)}) collective-permute-start(f32[4,130,1]{1,2,0:T(1,128)S(1)} %get-tuple-element.27), channel_id=1, source_target_pairs={{1,0},{2,1},{3,2},{5,4},{6,5},{7,6},{9,8},{10,9},{11,10},{13,12},{... | collective-permute-start | bytes 6248 | tf_op jit(solution)/shard_map/ppermute | solution.py:31
  123.3 10.2 %collective-permute-start.20 = (f32[4,1,512]{2,0,1:T(4,128)S(1)}, f32[4,1,512]{2,0,1:T(4,128)S(1)}, u32[]{:S(2)}, u32[]{:S(2)}) collective-permute-start(f32[4,1,512]{2,0,1:T(4,128)S(1)} %copy.76), channel_id=1, source_target_pairs={{0,4},{4,8},{8,12},{12,16},{16,20},{20,24},{24,28},{1,5},{5,9},{9,... | collective-permute-start | bytes 24584 | tf_op jit(solution)/shard_map/ppermute | solution.py:30
  126.6 7.2 %collective-permute-start.21 = (f32[4,1,512]{2,0,1:T(4,128)S(1)}, f32[4,1,512]{2,0,1:T(4,128)S(1)}, u32[]{:S(2)}, u32[]{:S(2)}) collective-permute-start(f32[4,1,512]{2,0,1:T(4,128)S(1)} %copy.78), channel_id=1, source_target_pairs={{4,0},{8,4},{12,8},{16,12},{20,16},{24,20},{28,24},{5,1},{9,5},{13... | collective-permute-start | bytes 24584 | tf_op jit(solution)/shard_map/ppermute | solution.py:31
  128.6 73.8 %collective-permute-start.18 = (f32[4,40,4]{2,1,0:T(8,128)}, f32[4,40,4]{2,1,0:T(8,128)S(1)}, u32[]{:S(2)}, u32[]{:S(2)}) collective-permute-start(f32[4,40,4]{2,1,0:T(8,128)} %get-tuple-element.58), channel_id=1, source_target_pairs={{0,1},{1,2},{2,3},{4,5},{5,6},{6,7},{8,9},{9,10},{10,11},{12,13},{... | collective-permute-start | bytes 7688 | tf_op jit(solution)/shard_map/ppermute | solution.py:30
  132.1 70.4 %collective-permute-start.19 = (f32[4,40,4]{2,1,0:T(8,128)}, f32[4,40,4]{2,1,0:T(8,128)S(1)}, u32[]{:S(2)}, u32[]{:S(2)}) collective-permute-start(f32[4,40,4]{2,1,0:T(8,128)} %get-tuple-element.59), channel_id=1, source_target_pairs={{1,0},{2,1},{3,2},{5,4},{6,5},{7,6},{9,8},{10,9},{11,10},{13,12},{... | collective-permute-start | bytes 7688 | tf_op jit(solution)/shard_map/ppermute | solution.py:31
  136.0 6.0 %collective-permute-start.22 = (f32[4,130,1]{1,2,0:T(1,128)S(1)}, f32[4,130,1]{1,2,0:T(1,128)S(1)}, u32[]{:S(2)}, u32[]{:S(2)}) collective-permute-start(f32[4,130,1]{1,2,0:T(1,128)S(1)} %get-tuple-element.24), channel_id=1, source_target_pairs={{0,1},{1,2},{2,3},{4,5},{5,6},{6,7},{8,9},{9,10},{10,11},{12,13},{... | collective-permute-start | bytes 6248 | tf_op jit(solution)/shard_map/ppermute | solution.py:30
  140.5 5.5 %collective-permute-start.23 = (f32[4,130,1]{1,2,0:T(1,128)S(1)}, f32[4,130,1]{1,2,0:T(1,128)S(1)}, u32[]{:S(2)}, u32[]{:S(2)}) collective-permute-start(f32[4,130,1]{1,2,0:T(1,128)S(1)} %get-tuple-element.25), channel_id=1, source_target_pairs={{1,0},{2,1},{3,2},{5,4},{6,5},{7,6},{9,8},{10,9},{11,10},{13,12},{... | collective-permute-start | bytes 6248 | tf_op jit(solution)/shard_map/ppermute | solution.py:31
  150.2 66.2 %copy-start.4 = (f32[4]{0:T(128)S(1)}, f32[4]{0:T(128)}, u32[]{:S(2)}) copy-start(f32[4]{0:T(128)} %compare_convert_fusion) | copy-start | bytes 52
  198.4 4.3 %collective-permute-start.24 = (f32[4,4,128]{2,1,0:T(4,128)S(1)}, f32[4,4,128]{2,1,0:T(4,128)S(1)}, u32[]{:S(2)}, u32[]{:S(2)}) collective-permute-start(f32[4,4,128]{2,1,0:T(4,128)S(1)} %get-tuple-element.64), channel_id=1, source_target_pairs={{0,4},{4,8},{8,12},{12,16},{16,20},{20,24},{24,28},{1,5},{5,9},{9,... | collective-permute-start | bytes 24584 | tf_op jit(solution)/shard_map/ppermute | solution.py:30
  201.2 6.4 %collective-permute-start.25 = (f32[4,4,128]{2,1,0:T(4,128)S(1)}, f32[4,4,128]{2,1,0:T(4,128)S(1)}, u32[]{:S(2)}, u32[]{:S(2)}) collective-permute-start(f32[4,4,128]{2,1,0:T(4,128)S(1)} %get-tuple-element.65), channel_id=1, source_target_pairs={{4,0},{8,4},{12,8},{16,12},{20,16},{24,20},{28,24},{5,1},{9,5},{13... | collective-permute-start | bytes 24584 | tf_op jit(solution)/shard_map/ppermute | solution.py:31
  207.7 5.0 %collective-permute-start.26 = (f32[4,40,4]{2,1,0:T(8,128)S(1)}, f32[4,40,4]{2,1,0:T(8,128)S(1)}, u32[]{:S(2)}, u32[]{:S(2)}) collective-permute-start(f32[4,40,4]{2,1,0:T(8,128)S(1)} %get-tuple-element.60), channel_id=1, source_target_pairs={{0,1},{1,2},{2,3},{4,5},{5,6},{6,7},{8,9},{9,10},{10,11},{12,13},{... | collective-permute-start | bytes 7688 | tf_op jit(solution)/shard_map/ppermute | solution.py:30
  209.9 6.3 %collective-permute-start.27 = (f32[4,40,4]{2,1,0:T(8,128)S(1)}, f32[4,40,4]{2,1,0:T(8,128)S(1)}, u32[]{:S(2)}, u32[]{:S(2)}) collective-permute-start(f32[4,40,4]{2,1,0:T(8,128)S(1)} %get-tuple-element.61), channel_id=1, source_target_pairs={{1,0},{2,1},{3,2},{5,4},{6,5},{7,6},{9,8},{10,9},{11,10},{13,12},{... | collective-permute-start | bytes 7688 | tf_op jit(solution)/shard_map/ppermute | solution.py:31
where the time goes:
time: 224 us; the launch traced here: 219 us
  local copies, waits for them, and re-layouts  71.5 us (32%)
  starting transfers between devices  68.3 us (30%)
  other arithmetic  51.2 us (23%)
  waiting for transfers between devices  26.7 us (12%)
    ppermute x14, starting transfers between devices, padded(): before = lax.ppermute(last, axis, up)  50 us
    reshape x1, local copies, waits for them, and re-layouts, on_device(): power.reshape(layer_total, rows // BLOCK_REFINE, BLOCK_REFINE, cols // BL...  36 us
    ppermute x14, waiting for transfers between devices, padded(): after = lax.ppermute(leading, axis, down)  26.7 us
    add x3, other arithmetic, on_device(): cropped_array(voltage_grid, field_margin - step_margin) + step  23.6 us
    ppermute x14, starting transfers between devices, padded(): after = lax.ppermute(leading, axis, down)  18.3 us
    reduce_sum x1, other arithmetic, on_device(): warming_load = power.reshape(layer_total, rows // BLOCK_REFINE, BLOCK_REF...  12.2 us
    slice x12, local copies, waits for them, and re-layouts, padded(): last = lax.slice_in_dim(x, length - width, length, axis=dim)  11.4 us
    unnamed x18, local copies, waits for them, and re-layouts  11 us
  transfers between devices with their start and end apart: 28, of which 7 were waited for; matrix products, arithmetic and copies ran while one was open for 48% of the time, Pallas kernels for 0%

commit v1 on v0

v1 whole, which is shorter than its diff:
```python
import jax
import jax.numpy as jnp
from jax import lax
from jax.experimental import pallas as pl
from jax.experimental.pallas import tpu as pltpu
from jax.sharding import PartitionSpec as P

REFINE = 4
SWEEPS = 3
HEAT_SWEEPS = 4

warmth_sensitivity = 0.5
leak_cond = 0.2
spectrum_low = 0.05
spectrum_high = 1.95
warming_weight = 0.3
heat_gain = 0.0625
interval_length = 0.12

SUB = 8
LANE = 128
REACH = 4
BOTH = ("row", "col")
HIGHEST = lax.Precision.HIGHEST


def row_swaps(rows, cols, first):
    pairs = []
    for r in range(rows):
        for c in range(cols):
            p = r + 1 if (r - first) % 2 == 0 else r - 1
            if 0 <= p < rows:
                pairs.append((r * cols + c, p * cols + c))
            elif c ^ 1 < cols:
                pairs.append((r * cols + c, r * cols + (c ^ 1)))
    return pairs


def col_swaps(rows, cols, first):
    pairs = []
    for r in range(rows):
        for c in range(cols):
            p = c + 1 if (c - first) % 2 == 0 else c - 1
            if 0 <= p < cols:
                pairs.append((r * cols + c, r * cols + p))
            elif r ^ 1 < rows:
                pairs.append((r * cols + c, (r ^ 1) * cols + c))
    return pairs


def iota(shape, dim):
    return lax.broadcasted_iota(jnp.int32, shape, dim)


def uniform(flag, shape):
    return jnp.full(shape, flag.astype(jnp.int32), jnp.int32) == 1


def place(axis):
    at = lax.axis_index(axis)
    return at % 2 == 0, at > 0, at < lax.axis_size(axis) - 1


def dot(a, b):
    return jnp.dot(a, b, precision=HIGHEST, preferred_element_type=jnp.float32)


def spread_lanes(cells, nodes):
    same = lax.shift_right_logical(iota((cells, nodes), 1), 2) == iota((cells, nodes), 0)
    return same.astype(jnp.float32)


def gather_lanes(nodes, cells):
    same = lax.shift_right_logical(iota((nodes, cells), 0), 2) == iota((nodes, cells), 1)
    return same.astype(jnp.float32)


def pack_rows_kernel(x_t, x_b, b_t, b_b, w_t, w_b, v_t, v_b, f_t, f_b, a_t, a_b, e_ref, o_ref):
    layers, _, cols = x_t.shape
    cells = w_t.shape[2]
    even, _, _ = place("row")
    low = iota((SUB, cols), 0) < REACH
    spread = spread_lanes(cells, cols)

    def planes(x, b, w, v, f, a, cell_row):
        warm = jnp.concatenate([w[l, cell_row : cell_row + 1, :] for l in range(layers)] * 2, 0)
        warm = dot(jnp.exp(-0.5 * warmth_sensitivity * warm), spread)
        xs = [x[l] for l in range(layers)]
        gs = [jnp.sqrt(b[l]) * warm[l : l + 1] for l in range(layers)]
        js = [f[l].astype(jnp.float32) * a[l] for l in range(layers)]
        vs = [v[l].astype(jnp.float32) for l in range(layers - 1)]
        ws = [jnp.concatenate([w[l] for l in range(layers)], axis=1)]
        return xs + gs, js + vs + ws

    top_a, top_b = planes(x_t, b_t, w_t, v_t, f_t, a_t, 0)
    bot_a, bot_b = planes(x_b, b_b, w_b, v_b, f_b, a_b, SUB - 1)
    pick = uniform(even, (SUB, cols))
    for k in range(2 * layers):
        top = jnp.where(low, top_a[k], pltpu.roll(top_b[k], REACH, 0))
        bot = jnp.where(low, pltpu.roll(bot_a[k], REACH, 0), bot_b[k])
        e_ref[k] = jnp.where(pick, bot, top)
        o_ref[k] = jnp.where(pick, top, bot)


def row_margin(e_ref, o_ref, plane, cols, half):
    even, above, below = place("row")
    k = plane % half
    e, o = e_ref[k, :, cols], o_ref[k, :, cols]
    pick = uniform(even, e.shape)
    top, bot = jnp.where(pick, o, e), jnp.where(pick, e, o)
    if plane < half:
        top = pltpu.roll(top, REACH, 0)
    else:
        bot = pltpu.roll(bot, REACH, 0)
    return (
        jnp.where(uniform(above, top.shape), top, 0.0),
        jnp.where(uniform(below, bot.shape), bot, 0.0),
    )


def fields_kernel(b_ref, w_ref, f_ref, a_ref, g_ref, j_ref):
    _, rows, cols = b_ref.shape
    _, cell_rows, cells = w_ref.shape
    warm = jnp.exp(-0.5 * warmth_sensitivity * w_ref[0])
    warm = dot(gather_lanes(rows, cell_rows), dot(warm, spread_lanes(cells, cols)))
    g_ref[0] = jnp.sqrt(b_ref[0]) * warm
    j_ref[0] = f_ref[0].astype(jnp.float32) * a_ref[0]


def pack_cols_kernel(
    x_l, x_r, g_l, g_r, j_l, j_r, v_l, v_r, w_ref, re_ref, ro_ref, e_ref, o_ref
):
    layers, rows, _ = x_l.shape
    cols = re_ref.shape[2]
    half = 2 * layers
    cell_rows, cells = w_ref.shape[1:]
    height, cell_height = rows + 2 * SUB, cell_rows + 2 * SUB
    even, _, _ = place("col")
    lane = iota((height, LANE), 1)
    slot, low = lax.shift_right_logical(lane, 3), lane % 8 < REACH
    cell_lane = iota((cell_height, LANE), 1)
    cell_slot, cell_high = lax.shift_right_logical(cell_lane, 3), cell_lane % 8 >= REACH
    sides = []
    for side, refs in enumerate(((x_l, g_l, j_l, v_l), (x_r, g_r, j_r, v_r))):
        tile = slice(0, LANE) if side == 0 else slice(cols - LANE, cols)
        own = [ref[l] for ref in refs for l in range(ref.shape[0])]
        out = jnp.zeros((height, LANE), jnp.float32)
        for p, value in enumerate(own):
            top, bot = row_margin(re_ref, ro_ref, p, tile, half)
            value = jnp.concatenate([top, value.astype(jnp.float32), bot], axis=0)
            value = pltpu.roll(value, (8 * p + REACH * side) % LANE, 1)
            out = jnp.where((slot == p) & low, value, out)
        head = out[:cell_height]
        for l in range(layers):
            tile = slice(l * cells, (l + 1) * cells)
            top, bot = row_margin(re_ref, ro_ref, 2 * half - 1, tile, half)
            value = jnp.concatenate([top, w_ref[l], bot], axis=0)
            value = pltpu.roll(value, (8 * l + REACH + REACH * side) % LANE, 1)
            head = jnp.where((cell_slot == l) & cell_high, value, head)
        sides.append(jnp.concatenate([head, out[cell_height:]], axis=0))
    left, right = sides
    pick = uniform(even, (height, LANE))
    e_ref[...] = jnp.where(pick, right, left)
    o_ref[...] = jnp.where(pick, left, right)


def col_margin(e, o, high):
    even, before, after = place("col")
    lane = iota(e.shape, 1)
    pick = uniform(even, e.shape)
    right, left = jnp.where(pick, e, o), jnp.where(pick, o, e)
    right = jnp.where(uniform(after, e.shape), right, 0.0)
    left = jnp.where(uniform(before, e.shape), left, 0.0)
    own_half = lane % 8 >= REACH if high else lane % 8 < REACH
    return jnp.where(own_half, right, pltpu.roll(left, LANE - REACH, 1))


def margin_tile(mixed, shift):
    lane = iota(mixed.shape, 1)
    value = mixed if shift == 0 else pltpu.roll(mixed, LANE - shift, 1)
    return jnp.where((lane < REACH) | (lane >= LANE - REACH), value, 0.0)


def rows_of(i):
    return pl.ds(pl.multiple_of(i * SUB, SUB), SUB)


def above_below(before, here, after):
    sub = iota(here.shape, 0)
    up = jnp.where(sub == 0, pltpu.roll(before, 1, 0), pltpu.roll(here, 1, 0))
    down = jnp.where(sub == SUB - 1, pltpu.roll(after, SUB - 1, 0), pltpu.roll(here, SUB - 1, 0))
    return up, down


def around(ref, l, i):
    here = ref[l, rows_of(i + 1), :]
    up, down = above_below(ref[l, rows_of(i), :], here, ref[l, rows_of(i + 2), :])
    width = here.shape[1]
    return (up + down) + (pltpu.roll(here, 1, 1) + pltpu.roll(here, width - 1, 1))


def sweeps_kernel(
    x_ref, g_ref, j_ref, v_ref, re_ref, ro_ref, ce_ref, co_ref,
    xo_ref, h_ref, he_ref, ho_ref,
    X, G, J, V, W0, W1, D, DI, GD, PW,
):
    layers, rows, cols = x_ref.shape
    half = 2 * layers
    groups = rows // SUB + 2
    own_rows = pl.ds(2 * SUB, rows)
    mixed = col_margin(ce_ref[...], co_ref[...], False)
    plane = 0
    for ref, pad in ((x_ref, X), (g_ref, G), (j_ref, J), (v_ref, V)):
        for l in range(ref.shape[0]):
            top, bot = row_margin(re_ref, ro_ref, plane, slice(0, cols), half)
            pad[l, SUB : 2 * SUB, 0:cols] = top
            pad[l, rows + 2 * SUB : rows + 3 * SUB, 0:cols] = bot
            pad[l, own_rows, 0:cols] = ref[l].astype(jnp.float32)
            pad[l, SUB : rows + 3 * SUB, cols : cols + LANE] = margin_tile(mixed, 8 * plane)
            plane += 1

    def each(body, first, last, unroll):
        lax.fori_loop(first, last, lambda i, c: (body(i), c)[1], 0, unroll=unroll)

    def start(i):
        r = rows_of(i + 1)
        for l in range(layers):
            W0[l, r, :] = G[l, r, :] * X[l, r, :]

    each(start, 0, groups, 3)

    center_c = 0.5 * (spectrum_high + spectrum_low)
    half_c = 0.5 * (spectrum_high - spectrum_low)
    sigma = center_c / half_c
    rho = 1.0 / sigma

    def upright(l, xs, vs):
        if l == 0:
            return vs[0] * xs[1]
        if l == layers - 1:
            return vs[l - 1] * xs[l - 1]
        return vs[l] * xs[l + 1] + vs[l - 1] * xs[l - 1]

    def first(i):
        r = rows_of(i + 1)
        xs = [X[l, r, :] for l in range(layers)]
        vs = [V[l, r, :] for l in range(layers - 1)]
        for l in range(layers):
            g = G[l, r, :]
            diag = leak_cond + g * around(G, l, i)
            if l < layers - 1:
                diag = diag + vs[l]
            if l > 0:
                diag = diag + vs[l - 1]
            inverse = 1.0 / diag
            gd = g * inverse
            jd = J[l, r, :] * inverse
            d = (jd + gd * around(W0, l, i) + inverse * upright(l, xs, vs) - xs[l]) / center_c
            x = xs[l] + d
            DI[l, r, :] = inverse
            GD[l, r, :] = gd
            J[l, r, :] = jd
            D[l, r, :] = d
            X[l, r, :] = x
            W1[l, r, :] = g * x

    each(first, 0, groups, 3)

    source, target = W1, W0
    for sweep in range(SWEEPS - 1):
        rho_new = 1.0 / (2.0 * sigma - rho)
        keep, gain = rho_new * rho, 2.0 * rho_new / half_c
        rho = rho_new
        last = sweep == SWEEPS - 2

        def later(i, source=source, target=target, keep=keep, gain=gain, last=last):
            r = rows_of(i + 1)
            xs = [X[l, r, :] for l in range(layers)]
            vs = [V[l, r, :] for l in range(layers - 1)]
            for l in range(layers):
                resid = (
                    J[l, r, :]
                    + GD[l, r, :] * around(source, l, i)
                    + DI[l, r, :] * upright(l, xs, vs)
                    - xs[l]
                )
                d = keep * D[l, r, :] + gain * resid
                x = xs[l] + d
                X[l, r, :] = x
                if not last:
                    D[l, r, :] = d
                    target[l, r, :] = G[l, r, :] * x

        each(later, 0, groups, 3)
        source, target = target, source

    def power(i):
        r = rows_of(i + 1)
        width = cols + LANE
        xs = [X[l, r, :] for l in range(layers)]
        drops = [
            V[l, r, 0:cols] * (xs[l][:, :cols] - xs[l + 1][:, :cols]) ** 2
            for l in range(layers - 1)
        ]
        for l in range(layers):
            x, g = xs[l], G[l, r, :]
            step = x - pltpu.roll(x, width - 1, 1)
            edge = (g * pltpu.roll(g, width - 1, 1)) * (step * step)
            flat = (edge + pltpu.roll(edge, 1, 1))[:, :cols]
            x, g = x[:, :cols], g[:, :cols]
            x_up, x_down = above_below(X[l, rows_of(i), 0:cols], x, X[l, rows_of(i + 2), 0:cols])
            g_up, g_down = above_below(G[l, rows_of(i), 0:cols], g, G[l, rows_of(i + 2), 0:cols])
            total = flat + g * (g_up * (x - x_up) ** 2 + g_down * (x - x_down) ** 2)
            if l < layers - 1:
                total = total + drops[l]
            if l > 0:
                total = total + drops[l - 1]
            PW[l, rows_of(i - 1), :] = leak_cond * (x * x) + 0.5 * total

    each(power, 1, groups - 1, 3)
    even, _, _ = place("row")
    cell_rows, cells = h_ref.shape[1:]
    fold_rows = spread_lanes(cell_rows, rows)
    fold_cols = gather_lanes(cols, cells)
    pick = uniform(even, (SUB, cells))
    for l in range(layers):
        xo_ref[l] = X[l, own_rows, 0:cols]
        heat = dot(dot(fold_rows, PW[l]), fold_cols) * heat_gain
        h_ref[l] = heat
        top, bot = heat[:SUB], heat[cell_rows - SUB :]
        he_ref[l] = jnp.where(pick, bot, top)
        ho_ref[l] = jnp.where(pick, top, bot)


def heat_rows(h_ref, e_ref, o_ref, l):
    even, above, below = place("row")
    e, o = e_ref[l], o_ref[l]
    pick = uniform(even, e.shape)
    top = jnp.where(uniform(above, e.shape), jnp.where(pick, o, e), 0.0)
    bot = jnp.where(uniform(below, e.shape), jnp.where(pick, e, o), 0.0)
    return jnp.concatenate([top, h_ref[l], bot], axis=0)


def pack_heat_kernel(h_ref, re_ref, ro_ref, e_ref, o_ref):
    layers, cell_rows, cells = h_ref.shape
    height = cell_rows + 2 * SUB
    even, _, _ = place("col")
    lane = iota((height, LANE), 1)
    slot, low = lax.shift_right_logical(lane, 3), lane % 8 < REACH
    left = right = jnp.zeros((height, LANE), jnp.float32)
    for l in range(layers):
        value = heat_rows(h_ref, re_ref, ro_ref, l)
        mine = (slot == l) & low
        left = jnp.where(mine, pltpu.roll(value[:, :LANE], 8 * l, 1) if l else value[:, :LANE], left)
        right = jnp.where(mine, pltpu.roll(value[:, cells - LANE :], 8 * l + REACH, 1), right)
    pick = uniform(even, (height, LANE))
    e_ref[...] = jnp.where(pick, right, left)
    o_ref[...] = jnp.where(pick, left, right)


def warm_kernel(
    w_ref, h_ref, re_ref, ro_ref, ce_ref, co_ref, hre_ref, hro_ref, hce_ref, hco_ref, out_ref
):
    layers, cell_rows, cells = w_ref.shape
    half = 2 * layers
    height, width = cell_rows + 2 * SUB, cells + LANE
    warm_mixed = col_margin(ce_ref[0:height, :], co_ref[0:height, :], True)
    heat_mixed = col_margin(hce_ref[...], hco_ref[...], False)
    theta, heat = [], []
    for l in range(layers):
        top, bot = row_margin(
            re_ref, ro_ref, 2 * half - 1, slice(l * cells, (l + 1) * cells), half
        )
        own = jnp.concatenate([top, w_ref[l], bot], axis=0)
        theta.append(jnp.concatenate([own, margin_tile(warm_mixed, 8 * l + REACH)], axis=1))
        own = heat_rows(h_ref, hre_ref, hro_ref, l)
        heat.append(jnp.concatenate([own, margin_tile(heat_mixed, 8 * l)], axis=1))
    _, above, below = place("row")
    _, before, after = place("col")
    shape = (height, width)
    r, c = iota(shape, 0), iota(shape, 1)
    inside = (uniform(above, shape) | (r >= SUB)) & (uniform(below, shape) | (r < height - SUB))
    inside = inside & (uniform(after, shape) | (c < cells) | (c >= cells + LANE // 2))
    inside = inside & (uniform(before, shape) | (c < cells + LANE // 2))

    def around_cells(v):
        return (pltpu.roll(v, 1, 0) + pltpu.roll(v, height - 1, 0)) + (
            pltpu.roll(v, 1, 1) + pltpu.roll(v, width - 1, 1)
        )

    for _ in range(HEAT_SWEEPS):
        later = []
        for l in range(layers):
            t = theta[l]
            q = jnp.where(inside, jnp.exp(-0.5 * warming_weight * t), 0.0)
            change = q * (around_cells(q * t) - t * around_cells(q)) + heat[l]
            if l < layers - 1:
                change = change + (theta[l + 1] - t)
            if l > 0:
                change = change + (theta[l - 1] - t)
            if l == layers - 1:
                change = change - t
            later.append(t + interval_length * change)
        theta = later
    for l in range(layers):
        out_ref[l] = theta[l][SUB : SUB + cell_rows, :cells]


def on_device(x, base, warm, via, feeder, amps):
    layers, rows, cols = x.shape
    _, cell_rows, cells = warm.shape
    f32 = jnp.float32
    mesh_rows, mesh_cols = lax.axis_size("row"), lax.axis_size("col")
    last_row, last_cell_row, last_col = rows // SUB - 1, cell_rows // SUB - 1, cols // LANE - 1

    def shape(*dims):
        return jax.ShapeDtypeStruct(dims, f32)

    def edge_rows(a, at):
        return pl.BlockSpec((a.shape[0], SUB, a.shape[2]), lambda _, at=at: (0, at, 0))

    def edge_cols(a, at):
        return pl.BlockSpec((a.shape[0], a.shape[1], LANE), lambda _, at=at: (0, 0, at))

    def full(a):
        return pl.BlockSpec(a.shape, lambda _, n=len(a.shape): (0,) * n)

    def swap(e, o, tables):
        return tuple(
            lax.ppermute(m, BOTH, tables(mesh_rows, mesh_cols, first)) for first, m in enumerate((e, o))
        )

    params = pltpu.CompilerParams(vmem_limit_bytes=40 * 1024 * 1024)
    row_args, row_specs = [], []
    for a in (x, base, warm, via, feeder, amps):
        end = last_cell_row if a is warm else last_row
        row_args += [a, a]
        row_specs += [edge_rows(a, 0), edge_rows(a, end)]
    message = shape(2 * layers, SUB, cols)
    e, o = pl.pallas_call(
        pack_rows_kernel,
        grid=(1,),
        in_specs=row_specs,
        out_specs=(full(message), full(message)),
        out_shape=(message, message),
        compiler_params=pltpu.CompilerParams(vmem_limit_bytes=60 * 1024 * 1024),
        name="pack_rows",
    )(*row_args)
    row_e, row_o = swap(e, o, row_swaps)

    fine = pl.BlockSpec((1, rows, cols), lambda l: (l, 0, 0))
    coarse = pl.BlockSpec((1, cell_rows, cells), lambda l: (l, 0, 0))
    g, inject = pl.pallas_call(
        fields_kernel,
        grid=(layers,),
        in_specs=[fine, coarse, fine, fine],
        out_specs=(fine, fine),
        out_shape=(shape(layers, rows, cols),) * 2,
        compiler_params=params,
        name="fields",
        cost_estimate=pl.CostEstimate(flops=8 * x.size, bytes_accessed=20 * x.size, transcendentals=x.size),
    )(base, warm, feeder, amps)

    col_args, col_specs = [], []
    for a in (x, g, inject, via):
        col_args += [a, a]
        col_specs += [edge_cols(a, 0), edge_cols(a, last_col)]
    message = shape(rows + 2 * SUB, LANE)
    e, o = pl.pallas_call(
        pack_cols_kernel,
        grid=(1,),
        in_specs=col_specs + [full(warm), full(row_e), full(row_o)],
        out_specs=(full(message), full(message)),
        out_shape=(message, message),
        compiler_params=params,
        name="pack_cols",
    )(*col_args, warm, row_e, row_o)
    col_e, col_o = swap(e, o, col_swaps)

    pad = pltpu.VMEM((layers, rows + 4 * SUB, cols + LANE), f32)
    pad_via = pltpu.VMEM((layers - 1, rows + 4 * SUB, cols + LANE), f32)
    edge = shape(layers, SUB, cells)
    voltage, heat, e, o = pl.pallas_call(
        sweeps_kernel,
        out_shape=(shape(layers, rows, cols), shape(layers, cell_rows, cells), edge, edge),
        scratch_shapes=[pad, pad, pad, pad_via, pad, pad, pad, pad, pad, pltpu.VMEM((layers, rows, cols), f32)],
        compiler_params=params,
        name="sweeps",
    )(x, g, inject, via, row_e, row_o, col_e, col_o)
    heat_row_e, heat_row_o = swap(e, o, row_swaps)

    message = shape(cell_rows + 2 * SUB, LANE)
    e, o = pl.pallas_call(
        pack_heat_kernel,
        out_shape=(message, message),
        compiler_params=params,
        name="pack_heat",
    )(heat, heat_row_e, heat_row_o)
    heat_col_e, heat_col_o = swap(e, o, col_swaps)

    warmth = pl.pallas_call(
        warm_kernel,
        out_shape=shape(layers, cell_rows, cells),
        compiler_params=params,
        name="warm",
    )(warm, heat, row_e, row_o, col_e, col_o, heat_row_e, heat_row_o, heat_col_e, heat_col_o)
    return voltage, warmth


def solution(mesh):
    placed = P(None, "row", "col")
    return jax.shard_map(
        on_device,
        mesh=mesh,
        in_specs=(placed,) * 6,
        out_specs=(placed, placed),
        check_vma=False,
    )
```

time: 224 us -> 37.5 us (0.17); the launches traced: 219 us -> 37 us
  local copies, waits for them, and re-layouts: 71.5 us -> 0.02 us
  starting transfers between devices: 68.3 us -> 11.5 us
  other arithmetic: 51.2 us -> 0 us
  waiting for transfers between devices: 26.7 us -> 6.49 us
  Pallas kernels: 0 us -> 18.2 us
    ppermute x28 -> x8, starting transfers between devices: 68.3 us -> 11.5 us  [swap(): lax.ppermute(m, BOTH, tables(mesh_rows, mesh_cols, first))]
    reshape x1 -> x0, local copies, waits for them, and re-layouts: 36 us -> none  [on_device(): power.reshape(layer_total, rows // BLOCK_REFINE, BLOCK_REFINE, cols // BL...]
    add x5 -> x0, other arithmetic: 28.2 us -> none  [the longest x3 23.6 us: on_device(): cropped_array(voltage_grid, field_margin - step_margin) + step]
    ppermute x28 -> x8, waiting for transfers between devices: 26.7 us -> 6.49 us  [swap(): lax.ppermute(m, BOTH, tables(mesh_rows, mesh_cols, first))]
    pallas_call x0 -> x6, Pallas kernels: none -> 18.2 us  [the longest x1 11.3 us: on_device(): pl.pallas_call(sweeps_kernel, out_shape=(shape(layers, rows, cols), shape...]
    slice x17 -> x0, local copies, waits for them, and re-layouts: 13 us -> none  [the longest x12 11.4 us: padded(): last = lax.slice_in_dim(x, length - width, length, axis=dim)]
    reduce_sum x1 -> x0, other arithmetic: 12.2 us -> none  [on_device(): warming_load = power.reshape(layer_total, rows // BLOCK_REFINE, BLOCK_REF...]
    unnamed x18 -> x12, local copies, waits for them, and re-layouts: 11 us -> 0.02 us
  transfers between devices with their start and end apart: 28 -> 8, of which waited for: 7 -> 4; matrix products, arithmetic and copies ran while one was open for 48% -> 0% of each run, Pallas kernels for 0% -> 6%
where the time goes in v1:
time: 37.5 us; the launch traced here: 37 us
  Pallas kernels  18.2 us (49%)
  starting transfers between devices  11.5 us (31%)
  waiting for transfers between devices  6.49 us (17%)
  between operations  0.71 us (2%)
    ppermute x8, starting transfers between devices, swap(): lax.ppermute(m, BOTH, tables(mesh_rows, mesh_cols, first))  11.5 us
    pallas_call x1, Pallas kernels, on_device(): pl.pallas_call(sweeps_kernel, out_shape=(shape(layers, rows, cols), shape...  11.3 us
    ppermute x8, waiting for transfers between devices, swap(): lax.ppermute(m, BOTH, tables(mesh_rows, mesh_cols, first))  6.49 us
    pallas_call x1, Pallas kernels, on_device(): pl.pallas_call(pack_rows_kernel, grid=(1,), in_specs=row_specs, out_specs...  2.29 us
    pallas_call x1, Pallas kernels, on_device(): pl.pallas_call(fields_kernel, grid=(layers,), in_specs=[fine, coarse, fin...  2.26 us
    pallas_call x1, Pallas kernels, on_device(): pl.pallas_call(warm_kernel, out_shape=shape(layers, cell_rows, cells), co...  1.62 us
  transfers between devices with their start and end apart: 8, of which 4 were waited for; matrix products, arithmetic and copies ran while one was open for 0% of the time, Pallas kernels for 6%

profile of v1, /device:TPU:0, one launch (start us, length us, event | category | flops | bytes accessed | tf_op | source)
XLA Modules:
  0.0 37.0 jit_solution(5561213317249971152)
XLA Ops:
  0.6 0.0 copy-start.5
  0.6 0.0 copy-start.4
  0.7 0.0 copy-start.3
  0.7 0.0 copy-start.2
  0.7 2.3 %pack_rows.1 = (f32[8,8,512]{2,1,0:T(8,128)}, f32[8,8,512]{2,1,0:T(8,128)}) custom-call(f32[4,128,512]{2,1,0:T(8,128)} %x_ref.1, f32[4,128,512]{2,1,0:T(8,128)} %x_ref.1, f32[4,128,512]{2,1,0:T(8,128)} %b_b.1, f32[4,128,512]{2,1,0:T(8,128)} %b_b.1, f32[4,32,128]{2,1,0:T(8,128)} %w_ref.5, f32[4,32,128]{2,1,0:T(8,128)} %w_ref.5, s32[3,128,512]{2,1,0:T(8,128)} %v_ref.1, ...), custom_call_target="tpu_custom_call" | custom-call | tf_op jit(solution)/shard_map/pack_rows/pallas_call | solution.py:440
  3.0 0.5 %collective-permute-start = (f32[8,8,512]{2,1,0:T(8,128)}, f32[8,8,512]{2,1,0:T(8,128)S(1)}, u32[]{:S(2)}, u32[]{:S(2)}) collective-permute-start(f32[8,8,512]{2,1,0:T(8,128)} %get-tuple-element.16), channel_id=1, source_target_pairs={{0,4},{1,5},{2,6},{3,7},{4,0},{5,1},{6,2},{7,3},{8,12},{9,13},{10,... | collective-permute-start | bytes 393224 | tf_op jit(solution)/shard_map/ppermute | solution.py:430
  3.4 0.0 copy-start
  3.4 0.0 copy-start.1
  3.4 2.7 %collective-permute-start.1 = (f32[8,8,512]{2,1,0:T(8,128)}, f32[8,8,512]{2,1,0:T(8,128)S(1)}, u32[]{:S(2)}, u32[]{:S(2)}) collective-permute-start(f32[8,8,512]{2,1,0:T(8,128)} %get-tuple-element.17), channel_id=1, source_target_pairs={{0,1},{1,0},{2,3},{3,2},{4,8},{5,9},{6,10},{7,11},{8,4},{9,5},{10,... | collective-permute-start | bytes 393224 | tf_op jit(solution)/shard_map/ppermute | solution.py:430
  6.1 0.0 copy-done.5
  6.1 0.0 copy-done.4
  6.1 0.0 copy-done.3
  6.1 0.0 copy-done.2
  6.1 2.3 %fields.1 = (f32[4,128,512]{2,1,0:T(8,128)S(1)}, f32[4,128,512]{2,1,0:T(8,128)S(1)}) custom-call(f32[4,128,512]{2,1,0:T(8,128)S(1)} %copy-done.2, f32[4,32,128]{2,1,0:T(8,128)S(1)} %copy-done.5, s32[4,128,512]{2,1,0:T(8,128)S(1)} %copy-done.3, f32[4,128,512]{2,1,0:T(8,128)S(1)} %copy-done.4), custom_call_target="tpu_custom_call" | custom-call | flops 2097152 | bytes 5242880 | tf_op jit(solution)/shard_map/fields/pallas_call | solution.py:453
  8.3 0.0 collective-permute-done.re_ref
  8.4 0.9 %collective-permute-done.1.ro_ref = f32[8,8,512]{2,1,0:T(8,128)S(1)} collective-permute-done((f32[8,8,512]{2,1,0:T(8,128)}, f32[8,8,512]{2,1,0:T(8,128)S(1)}, u32[]{:S(2)}, u32[]{:S(2)}) %collective-permute-start.1) | collective-permute-done | bytes 131104 | tf_op jit(solution)/shard_map/ppermute | solution.py:430
  9.2 0.0 copy-done
  9.2 0.0 copy-done.1
  9.2 0.7 %pack_cols.1 = (f32[144,128]{1,0:T(8,128)S(1)}, f32[144,128]{1,0:T(8,128)S(1)}) custom-call(f32[4,128,512]{2,1,0:T(8,128)S(1)} %copy-done, f32[4,128,512]{2,1,0:T(8,128)S(1)} %copy-done, f32[4,128,512]{2,1,0:T(8,128)S(1)} %get-tuple-element.14.g_l.g_r.g_ref, f32[4,128,512]{2,1,0:T(8,128)S(1)} %get-tuple-element.14.g_l.g_r.g_ref, ...), custom_call_target="tpu_custom_call" | custom-call | tf_op jit(solution)/shard_map/pack_cols/pallas_call | solution.py:469
  9.9 2.1 %collective-permute-start.2 = (f32[144,128]{1,0:T(8,128)S(1)}, f32[144,128]{1,0:T(8,128)S(1)}, u32[]{:S(2)}, u32[]{:S(2)}) collective-permute-start(f32[144,128]{1,0:T(8,128)S(1)} %get-tuple-element.18), channel_id=1, source_target_pairs={{0,1},{1,0},{2,3},{3,2},{4,5},{5,4},{6,7},{7,6},{8,9},{9,8},{10,11... | collective-permute-start | bytes 221192 | tf_op jit(solution)/shard_map/ppermute | solution.py:430
  12.0 0.7 %collective-permute-start.3 = (f32[144,128]{1,0:T(8,128)S(1)}, f32[144,128]{1,0:T(8,128)S(1)}, u32[]{:S(2)}, u32[]{:S(2)}) collective-permute-start(f32[144,128]{1,0:T(8,128)S(1)} %get-tuple-element.19), channel_id=1, source_target_pairs={{0,4},{1,2},{2,1},{3,7},{4,0},{5,6},{6,5},{7,3},{8,12},{9,10},{10,... | collective-permute-start | bytes 221192 | tf_op jit(solution)/shard_map/ppermute | solution.py:430
  12.7 2.1 %collective-permute-done.2.ce_ref = f32[144,128]{1,0:T(8,128)S(1)} collective-permute-done((f32[144,128]{1,0:T(8,128)S(1)}, f32[144,128]{1,0:T(8,128)S(1)}, u32[]{:S(2)}, u32[]{:S(2)}) %collective-permute-start.2) | collective-permute-done | bytes 73760 | tf_op jit(solution)/shard_map/ppermute | solution.py:430
  14.8 0.0 collective-permute-done.3.co_ref
  14.8 11.3 %sweeps.1 = (f32[4,128,512]{2,1,0:T(8,128)}, f32[4,32,128]{2,1,0:T(8,128)S(1)}, f32[4,8,128]{2,1,0:T(8,128)S(1)}, f32[4,8,128]{2,1,0:T(8,128)S(1)}) custom-call(f32[4,128,512]{2,1,0:T(8,128)S(1)} %copy-done, f32[4,128,512]{2,1,0:T(8,128)S(1)} %get-tuple-element.14.g_l.g_r.g_ref, f32[4,128,512]{2,1,0:T(8,128)S(1)} %get-tuple-element.15.j_l.j_r.j_ref, ...), custom_call_target="tpu_custom_call" | custom-call | tf_op jit(solution)/shard_map/sweeps/pallas_call | solution.py:483
  26.1 0.1 collective-permute-start.4
  26.2 3.4 %collective-permute-start.5 = (f32[4,8,128]{2,1,0:T(8,128)S(1)}, f32[4,8,128]{2,1,0:T(8,128)S(1)}, u32[]{:S(2)}, u32[]{:S(2)}) collective-permute-start(f32[4,8,128]{2,1,0:T(8,128)S(1)} %get-tuple-element.23), channel_id=1, source_target_pairs={{0,1},{1,0},{2,3},{3,2},{4,8},{5,9},{6,10},{7,11},{8,4},{9,5},{10,... | collective-permute-start | bytes 49160 | tf_op jit(solution)/shard_map/ppermute | solution.py:430
  29.6 0.0 collective-permute-done.4.re_ref.hre_ref
  29.6 1.7 %collective-permute-done.5.ro_ref.hro_ref = f32[4,8,128]{2,1,0:T(8,128)S(1)} collective-permute-done((f32[4,8,128]{2,1,0:T(8,128)S(1)}, f32[4,8,128]{2,1,0:T(8,128)S(1)}, u32[]{:S(2)}, u32[]{:S(2)}) %collective-permute-start.5) | collective-permute-done | bytes 16416 | tf_op jit(solution)/shard_map/ppermute | solution.py:430
  31.4 0.1 pack_heat.1
  31.5 2.1 %collective-permute-start.6 = (f32[48,128]{1,0:T(8,128)S(1)}, f32[48,128]{1,0:T(8,128)S(1)}, u32[]{:S(2)}, u32[]{:S(2)}) collective-permute-start(f32[48,128]{1,0:T(8,128)S(1)} %get-tuple-element.24), channel_id=1, source_target_pairs={{0,1},{1,0},{2,3},{3,2},{4,5},{5,4},{6,7},{7,6},{8,9},{9,8},{10,11... | collective-permute-start | bytes 73736 | tf_op jit(solution)/shard_map/ppermute | solution.py:430
  33.6 0.0 collective-permute-start.7
  33.6 1.8 %collective-permute-done.6.hce_ref = f32[48,128]{1,0:T(8,128)S(1)} collective-permute-done((f32[48,128]{1,0:T(8,128)S(1)}, f32[48,128]{1,0:T(8,128)S(1)}, u32[]{:S(2)}, u32[]{:S(2)}) %collective-permute-start.6) | collective-permute-done | bytes 24608 | tf_op jit(solution)/shard_map/ppermute | solution.py:430
  35.4 0.0 collective-permute-done.7.hco_ref
  35.4 1.6 %warm.1 = f32[4,32,128]{2,1,0:T(8,128)} custom-call(f32[4,32,128]{2,1,0:T(8,128)S(1)} %copy-done.5, f32[4,32,128]{2,1,0:T(8,128)S(1)} %get-tuple-element.21.h_ref, f32[8,8,512]{2,1,0:T(8,128)S(1)} %collective-permute-done.re_ref, f32[8,8,512]{2,1,0:T(8,128)S(1)} %collective-permute-done.1.ro_ref, f32[144,128]{1,0:T(8,128)S(1)} %collective-permute-done.2.ce_ref, ...), custom_call_target="tpu_custom_call" | custom-call | tf_op jit(solution)/shard_map/warm/pallas_call | solution.py:501
Async XLA Ops:
  0.6 5.4 %copy-start.5 = (f32[4,32,128]{2,1,0:T(8,128)S(1)}, f32[4,32,128]{2,1,0:T(8,128)}, u32[]{:S(2)}) copy-start(f32[4,32,128]{2,1,0:T(8,128)} %w_ref.5) | copy-start | bytes 196612
  0.6 5.4 %copy-start.4 = (f32[4,128,512]{2,1,0:T(8,128)S(1)}, f32[4,128,512]{2,1,0:T(8,128)}, u32[]{:S(2)}) copy-start(f32[4,128,512]{2,1,0:T(8,128)} %a_b.1) | copy-start | bytes 3145732
  0.7 5.4 %copy-start.3 = (s32[4,128,512]{2,1,0:T(8,128)S(1)}, s32[4,128,512]{2,1,0:T(8,128)}, u32[]{:S(2)}) copy-start(s32[4,128,512]{2,1,0:T(8,128)} %f_b.1) | copy-start | bytes 3145732
  0.7 5.4 %copy-start.2 = (f32[4,128,512]{2,1,0:T(8,128)S(1)}, f32[4,128,512]{2,1,0:T(8,128)}, u32[]{:S(2)}) copy-start(f32[4,128,512]{2,1,0:T(8,128)} %b_b.1) | copy-start | bytes 3145732
  3.0 5.4 %collective-permute-start = (f32[8,8,512]{2,1,0:T(8,128)}, f32[8,8,512]{2,1,0:T(8,128)S(1)}, u32[]{:S(2)}, u32[]{:S(2)}) collective-permute-start(f32[8,8,512]{2,1,0:T(8,128)} %get-tuple-element.16), channel_id=1, source_target_pairs={{0,4},{1,5},{2,6},{3,7},{4,0},{5,1},{6,2},{7,3},{8,12},{9,13},{10,... | collective-permute-start | bytes 393224 | tf_op jit(solution)/shard_map/ppermute | solution.py:430
  3.4 5.8 %copy-start = (f32[4,128,512]{2,1,0:T(8,128)S(1)}, f32[4,128,512]{2,1,0:T(8,128)}, u32[]{:S(2)}) copy-start(f32[4,128,512]{2,1,0:T(8,128)} %x_ref.1) | copy-start | bytes 3145732
  3.4 5.8 %copy-start.1 = (s32[3,128,512]{2,1,0:T(8,128)S(1)}, s32[3,128,512]{2,1,0:T(8,128)}, u32[]{:S(2)}) copy-start(s32[3,128,512]{2,1,0:T(8,128)} %v_ref.1) | copy-start | bytes 2359300
  3.4 5.8 %collective-permute-start.1 = (f32[8,8,512]{2,1,0:T(8,128)}, f32[8,8,512]{2,1,0:T(8,128)S(1)}, u32[]{:S(2)}, u32[]{:S(2)}) collective-permute-start(f32[8,8,512]{2,1,0:T(8,128)} %get-tuple-element.17), channel_id=1, source_target_pairs={{0,1},{1,0},{2,3},{3,2},{4,8},{5,9},{6,10},{7,11},{8,4},{9,5},{10,... | collective-permute-start | bytes 393224 | tf_op jit(solution)/shard_map/ppermute | solution.py:430
  9.9 4.9 %collective-permute-start.2 = (f32[144,128]{1,0:T(8,128)S(1)}, f32[144,128]{1,0:T(8,128)S(1)}, u32[]{:S(2)}, u32[]{:S(2)}) collective-permute-start(f32[144,128]{1,0:T(8,128)S(1)} %get-tuple-element.18), channel_id=1, source_target_pairs={{0,1},{1,0},{2,3},{3,2},{4,5},{5,4},{6,7},{7,6},{8,9},{9,8},{10,11... | collective-permute-start | bytes 221192 | tf_op jit(solution)/shard_map/ppermute | solution.py:430
  12.0 2.8 %collective-permute-start.3 = (f32[144,128]{1,0:T(8,128)S(1)}, f32[144,128]{1,0:T(8,128)S(1)}, u32[]{:S(2)}, u32[]{:S(2)}) collective-permute-start(f32[144,128]{1,0:T(8,128)S(1)} %get-tuple-element.19), channel_id=1, source_target_pairs={{0,4},{1,2},{2,1},{3,7},{4,0},{5,6},{6,5},{7,3},{8,12},{9,10},{10,... | collective-permute-start | bytes 221192 | tf_op jit(solution)/shard_map/ppermute | solution.py:430
  26.1 3.5 %collective-permute-start.4 = (f32[4,8,128]{2,1,0:T(8,128)S(1)}, f32[4,8,128]{2,1,0:T(8,128)S(1)}, u32[]{:S(2)}, u32[]{:S(2)}) collective-permute-start(f32[4,8,128]{2,1,0:T(8,128)S(1)} %get-tuple-element.22), channel_id=1, source_target_pairs={{0,4},{1,5},{2,6},{3,7},{4,0},{5,1},{6,2},{7,3},{8,12},{9,13},{10,... | collective-permute-start | bytes 49160 | tf_op jit(solution)/shard_map/ppermute | solution.py:430
  26.2 5.1 %collective-permute-start.5 = (f32[4,8,128]{2,1,0:T(8,128)S(1)}, f32[4,8,128]{2,1,0:T(8,128)S(1)}, u32[]{:S(2)}, u32[]{:S(2)}) collective-permute-start(f32[4,8,128]{2,1,0:T(8,128)S(1)} %get-tuple-element.23), channel_id=1, source_target_pairs={{0,1},{1,0},{2,3},{3,2},{4,8},{5,9},{6,10},{7,11},{8,4},{9,5},{10,... | collective-permute-start | bytes 49160 | tf_op jit(solution)/shard_map/ppermute | solution.py:430
  31.5 3.9 %collective-permute-start.6 = (f32[48,128]{1,0:T(8,128)S(1)}, f32[48,128]{1,0:T(8,128)S(1)}, u32[]{:S(2)}, u32[]{:S(2)}) collective-permute-start(f32[48,128]{1,0:T(8,128)S(1)} %get-tuple-element.24), channel_id=1, source_target_pairs={{0,1},{1,0},{2,3},{3,2},{4,5},{5,4},{6,7},{7,6},{8,9},{9,8},{10,11... | collective-permute-start | bytes 73736 | tf_op jit(solution)/shard_map/ppermute | solution.py:430
  33.6 1.8 %collective-permute-start.7 = (f32[48,128]{1,0:T(8,128)S(1)}, f32[48,128]{1,0:T(8,128)S(1)}, u32[]{:S(2)}, u32[]{:S(2)}) collective-permute-start(f32[48,128]{1,0:T(8,128)S(1)} %get-tuple-element.25), channel_id=1, source_target_pairs={{0,4},{1,2},{2,1},{3,7},{4,0},{5,6},{6,5},{7,3},{8,12},{9,10},{10,... | collective-permute-start | bytes 73736 | tf_op jit(solution)/shard_map/ppermute | solution.py:430

commit v2 on v1

--- a/solution.py
+++ b/solution.py
@@ -116,15 +116,6 @@
         jnp.where(uniform(above, top.shape), top, 0.0),
         jnp.where(uniform(below, bot.shape), bot, 0.0),
     )
-
-
-def fields_kernel(b_ref, w_ref, f_ref, a_ref, g_ref, j_ref):
-    _, rows, cols = b_ref.shape
-    _, cell_rows, cells = w_ref.shape
-    warm = jnp.exp(-0.5 * warmth_sensitivity * w_ref[0])
-    warm = dot(gather_lanes(rows, cell_rows), dot(warm, spread_lanes(cells, cols)))
-    g_ref[0] = jnp.sqrt(b_ref[0]) * warm
-    j_ref[0] = f_ref[0].astype(jnp.float32) * a_ref[0]
 
 
 def pack_cols_kernel(
@@ -164,7 +155,7 @@
     o_ref[...] = jnp.where(pick, left, right)
 
 
-def col_margin(e, o, high):
+def col_margin(e, o, high, back):
     even, before, after = place("col")
     lane = iota(e.shape, 1)
     pick = uniform(even, e.shape)
@@ -172,7 +163,7 @@
     right = jnp.where(uniform(after, e.shape), right, 0.0)
     left = jnp.where(uniform(before, e.shape), left, 0.0)
     own_half = lane % 8 >= REACH if high else lane % 8 < REACH
-    return jnp.where(own_half, right, pltpu.roll(left, LANE - REACH, 1))
+    return jnp.where(own_half, right, pltpu.roll(left, LANE - back, 1))
 
 
 def margin_tile(mixed, shift):
@@ -181,167 +172,350 @@
     return jnp.where((lane < REACH) | (lane >= LANE - REACH), value, 0.0)
 
 
-def rows_of(i):
+CENTER = 0.5 * (spectrum_high + spectrum_low)
+HALF = 0.5 * (spectrum_high - spectrum_low)
+SIGMA = CENTER / HALF
+
+
+def sweep_gains():
+    rho, gains = 1.0 / SIGMA, []
+    for _ in range(SWEEPS - 1):
+        rho_new = 1.0 / (2.0 * SIGMA - rho)
+        gains.append((rho_new * rho, 2.0 * rho_new / HALF))
+        rho = rho_new
+    return gains
+
+
+def tile_rows(i):
     return pl.ds(pl.multiple_of(i * SUB, SUB), SUB)
 
 
-def above_below(before, here, after):
-    sub = iota(here.shape, 0)
-    up = jnp.where(sub == 0, pltpu.roll(before, 1, 0), pltpu.roll(here, 1, 0))
-    down = jnp.where(sub == SUB - 1, pltpu.roll(after, SUB - 1, 0), pltpu.roll(here, SUB - 1, 0))
-    return up, down
-
-
-def around(ref, l, i):
-    here = ref[l, rows_of(i + 1), :]
-    up, down = above_below(ref[l, rows_of(i), :], here, ref[l, rows_of(i + 2), :])
+def each(first, last, unroll, body):
+    if unroll >= last - first:
+        for i in range(first, last):
+            body(i)
+    else:
+        lax.fori_loop(first, last, lambda i, c: (body(i), c)[1], 0, unroll=unroll)
+
+
+def before(i):
+    return max(i - 1, 0) if isinstance(i, int) else jnp.maximum(i - 1, 0)
+
+
+def after(i, groups):
+    return min(i + 1, groups - 1) if isinstance(i, int) else jnp.minimum(i + 1, groups - 1)
+
+
+def shifted_down(here, nxt):
+    return jnp.where(
+        iota(here.shape, 0) == SUB - 1, pltpu.roll(nxt, SUB - 1, 0), pltpu.roll(here, SUB - 1, 0)
+    )
+
+
+def shifted_up(prev, here):
+    return jnp.where(iota(here.shape, 0) == 0, pltpu.roll(prev, 1, 0), pltpu.roll(here, 1, 0))
+
+
+def around(ref, l, i, groups):
+    here = ref[l, tile_rows(i), :]
     width = here.shape[1]
-    return (up + down) + (pltpu.roll(here, 1, 1) + pltpu.roll(here, width - 1, 1))
-
-
-def sweeps_kernel(
-    x_ref, g_ref, j_ref, v_ref, re_ref, ro_ref, ce_ref, co_ref,
-    xo_ref, h_ref, he_ref, ho_ref,
-    X, G, J, V, W0, W1, D, DI, GD, PW,
-):
-    layers, rows, cols = x_ref.shape
-    half = 2 * layers
-    groups = rows // SUB + 2
-    own_rows = pl.ds(2 * SUB, rows)
-    mixed = col_margin(ce_ref[...], co_ref[...], False)
-    plane = 0
-    for ref, pad in ((x_ref, X), (g_ref, G), (j_ref, J), (v_ref, V)):
-        for l in range(ref.shape[0]):
-            top, bot = row_margin(re_ref, ro_ref, plane, slice(0, cols), half)
-            pad[l, SUB : 2 * SUB, 0:cols] = top
-            pad[l, rows + 2 * SUB : rows + 3 * SUB, 0:cols] = bot
-            pad[l, own_rows, 0:cols] = ref[l].astype(jnp.float32)
-            pad[l, SUB : rows + 3 * SUB, cols : cols + LANE] = margin_tile(mixed, 8 * plane)
-            plane += 1
-
-    def each(body, first, last, unroll):
-        lax.fori_loop(first, last, lambda i, c: (body(i), c)[1], 0, unroll=unroll)
+    up = shifted_up(ref[l, tile_rows(before(i)), :], here)
+    down = shifted_down(here, ref[l, tile_rows(after(i, groups)), :])
+    return up, down, pltpu.roll(here, 1, 1), pltpu.roll(here, width - 1, 1)
+
+
+def added(four):
+    return (four[0] + four[1]) + (four[2] + four[3])
+
+
+def upright(l, xs, vs):
+    layers = len(xs)
+    if l == 0:
+        return vs[0] * xs[1]
+    if l == layers - 1:
+        return vs[l - 1] * xs[l - 1]
+    return vs[l] * xs[l + 1] + vs[l - 1] * xs[l - 1]
+
+
+def load_vias(V, r):
+    return [V[l, r, :].astype(jnp.float32) for l in range(V.shape[0])]
+
+
+def first_sweep(unroll, X, G, J, V, W0, XN, WN, D, DI, GD, JD, EH, EV):
+    layers, height, _ = X.shape
+    groups = height // SUB
 
     def start(i):
-        r = rows_of(i + 1)
+        r = tile_rows(i)
         for l in range(layers):
             W0[l, r, :] = G[l, r, :] * X[l, r, :]
 
-    each(start, 0, groups, 3)
-
-    center_c = 0.5 * (spectrum_high + spectrum_low)
-    half_c = 0.5 * (spectrum_high - spectrum_low)
-    sigma = center_c / half_c
-    rho = 1.0 / sigma
-
-    def upright(l, xs, vs):
-        if l == 0:
-            return vs[0] * xs[1]
-        if l == layers - 1:
-            return vs[l - 1] * xs[l - 1]
-        return vs[l] * xs[l + 1] + vs[l - 1] * xs[l - 1]
-
-    def first(i):
-        r = rows_of(i + 1)
+    each(0, groups, unroll, start)
+
+    def body(i):
+        r = tile_rows(i)
         xs = [X[l, r, :] for l in range(layers)]
-        vs = [V[l, r, :] for l in range(layers - 1)]
+        vs = load_vias(V, r)
         for l in range(layers):
             g = G[l, r, :]
-            diag = leak_cond + g * around(G, l, i)
+            four = around(G, l, i, groups)
+            diag = leak_cond + g * added(four)
+            EV[l, r, :] = g * four[1]
+            EH[l, r, :] = g * four[3]
             if l < layers - 1:
                 diag = diag + vs[l]
             if l > 0:
                 diag = diag + vs[l - 1]
             inverse = 1.0 / diag
-            gd = g * inverse
-            jd = J[l, r, :] * inverse
-            d = (jd + gd * around(W0, l, i) + inverse * upright(l, xs, vs) - xs[l]) / center_c
+            gd, jd = g * inverse, J[l, r, :] * inverse
+            near = added(around(W0, l, i, groups))
+            d = (jd + gd * near + inverse * upright(l, xs, vs) - xs[l]) / CENTER
             x = xs[l] + d
-            DI[l, r, :] = inverse
-            GD[l, r, :] = gd
-            J[l, r, :] = jd
-            D[l, r, :] = d
-            X[l, r, :] = x
-            W1[l, r, :] = g * x
-
-    each(first, 0, groups, 3)
-
-    source, target = W1, W0
-    for sweep in range(SWEEPS - 1):
-        rho_new = 1.0 / (2.0 * sigma - rho)
-        keep, gain = rho_new * rho, 2.0 * rho_new / half_c
-        rho = rho_new
-        last = sweep == SWEEPS - 2
-
-        def later(i, source=source, target=target, keep=keep, gain=gain, last=last):
-            r = rows_of(i + 1)
-            xs = [X[l, r, :] for l in range(layers)]
-            vs = [V[l, r, :] for l in range(layers - 1)]
-            for l in range(layers):
-                resid = (
-                    J[l, r, :]
-                    + GD[l, r, :] * around(source, l, i)
-                    + DI[l, r, :] * upright(l, xs, vs)
-                    - xs[l]
-                )
-                d = keep * D[l, r, :] + gain * resid
-                x = xs[l] + d
-                X[l, r, :] = x
-                if not last:
-                    D[l, r, :] = d
-                    target[l, r, :] = G[l, r, :] * x
-
-        each(later, 0, groups, 3)
-        source, target = target, source
-
-    def power(i):
-        r = rows_of(i + 1)
-        width = cols + LANE
+            DI[l, r, :], GD[l, r, :], JD[l, r, :], D[l, r, :] = inverse, gd, jd, d
+            XN[l, r, :] = x
+            WN[l, r, :] = g * x
+
+    each(0, groups, unroll, body)
+
+
+def next_sweep(unroll, keep, gain, X, V, W, D, DI, GD, JD, G, XN, WN=None, DN=None):
+    layers, height, _ = X.shape
+    groups = height // SUB
+
+    def body(i):
+        r = tile_rows(i)
         xs = [X[l, r, :] for l in range(layers)]
-        drops = [
-            V[l, r, 0:cols] * (xs[l][:, :cols] - xs[l + 1][:, :cols]) ** 2
-            for l in range(layers - 1)
-        ]
+        vs = load_vias(V, r)
         for l in range(layers):
-            x, g = xs[l], G[l, r, :]
-            step = x - pltpu.roll(x, width - 1, 1)
-            edge = (g * pltpu.roll(g, width - 1, 1)) * (step * step)
-            flat = (edge + pltpu.roll(edge, 1, 1))[:, :cols]
-            x, g = x[:, :cols], g[:, :cols]
-            x_up, x_down = above_below(X[l, rows_of(i), 0:cols], x, X[l, rows_of(i + 2), 0:cols])
-            g_up, g_down = above_below(G[l, rows_of(i), 0:cols], g, G[l, rows_of(i + 2), 0:cols])
-            total = flat + g * (g_up * (x - x_up) ** 2 + g_down * (x - x_down) ** 2)
+            near = added(around(W, l, i, groups))
+            resid = (
+                JD[l, r, :] + GD[l, r, :] * near + DI[l, r, :] * upright(l, xs, vs) - xs[l]
+            )
+            d = keep * D[l, r, :] + gain * resid
+            x = xs[l] + d
+            XN[l, r, :] = x
+            if WN is not None:
+                DN[l, r, :] = d
+                WN[l, r, :] = G[l, r, :] * x
+
+    each(0, groups, unroll, body)
+
+
+def later_sweeps(unroll, X, V, W, D, DI, GD, JD, G, WN, XN, DN):
+    gains = sweep_gains()
+    x, w, d, other = X, W, D, WN
+    for at, (keep, gain) in enumerate(gains):
+        if at == len(gains) - 1:
+            next_sweep(unroll, keep, gain, x, V, w, d, DI, GD, JD, G, XN)
+        else:
+            next_sweep(unroll, keep, gain, x, V, w, d, DI, GD, JD, G, XN, other, DN)
+            assert len(gains) <= 2
+            x, w, d = XN, other, DN
+
+
+def power_rows(first, last, unroll, X, V, EH, EV, PA, PB, PD):
+    layers, height, width = X.shape
+    groups = height // SUB
+    share = jnp.where(iota((SUB, width), 0) % REFINE == REFINE - 1, 0.5, 1.0)
+    lane_share = jnp.where(iota((SUB, width), 1) % REFINE == REFINE - 1, 1.0, 2.0)
+
+    def fold(v):
+        v = v + pltpu.roll(v, SUB - 1, 0)
+        return v + pltpu.roll(v, SUB - 2, 0)
+
+    def body(i):
+        r = tile_rows(i)
+        out = tile_rows(i + 1)
+        xs = [X[l, r, :] for l in range(layers)]
+        vs = load_vias(V, r)
+        drops = [0.5 * vs[l] * (xs[l] - xs[l + 1]) ** 2 for l in range(layers - 1)]
+        for l in range(layers):
+            x = xs[l]
+            across = x - pltpu.roll(x, width - 1, 1)
+            down = x - shifted_down(x, X[l, tile_rows(after(i, groups)), :])
+            across = 0.5 * EH[l, r, :] * (across * across)
+            down = EV[l, r, :] * (down * down)
+            total = leak_cond * (x * x) + share * down + lane_share * across
             if l < layers - 1:
                 total = total + drops[l]
             if l > 0:
                 total = total + drops[l - 1]
-            PW[l, rows_of(i - 1), :] = leak_cond * (x * x) + 0.5 * total
-
-    each(power, 1, groups - 1, 3)
-    even, _, _ = place("row")
+            total, across = fold(total), fold(across)
+            for t in range(width // LANE):
+                tile = slice(t * LANE, (t + 1) * LANE)
+                PA[l, t, out, :] = total[:, tile]
+                PB[l, t, out, :] = across[:, tile]
+                PD[l, t, out, :] = down[:, tile]
+
+    each(first, last, unroll, body)
+
+
+def fold_power(row, cells, PA, PB, PD, same, left):
+    layers = PA.shape[0]
+    at = pl.ds(row + SUB, cells, stride=REFINE)
+    up = pl.ds(row + SUB - 1, cells, stride=REFINE)
+    tiles = range(PA.shape[1])
+    a = [
+        jnp.concatenate([PA[l, t, at, :] + 0.5 * PD[l, t, up, :] for t in tiles], 1)
+        for l in range(layers)
+    ]
+    b = [jnp.concatenate([PB[l, t, at, :] for t in tiles], 1) for l in range(layers)]
+    a, b = jnp.concatenate(a, 0), jnp.concatenate(b, 0)
+    heat = (dot(a, same) + dot(b, left)) * heat_gain
+    return [heat[l * cells : (l + 1) * cells] for l in range(layers)]
+
+
+def fold_matrices(nodes, cells):
+    n, c = iota((nodes, cells), 0), iota((nodes, cells), 1)
+    same = lax.shift_right_logical(n, 2) == c
+    return same.astype(jnp.float32), (n == REFINE * c - 1).astype(jnp.float32)
+
+
+def bulk_first_kernel(
+    x_ref, b_ref, w_ref, v_ref, f_ref, a_ref,
+    g_ref, j_ref, XN, WN, D, DI, GD, JD, EH, EV,
+    W0,
+):
+    layers, rows, cols = x_ref.shape
+    _, cell_rows, cells = w_ref.shape
+    spread_rows = gather_lanes(rows, cell_rows)
+    spread = spread_lanes(cells, cols)
+    for l in range(layers):
+        warm = jnp.exp(-0.5 * warmth_sensitivity * w_ref[l])
+        g_ref[l] = jnp.sqrt(b_ref[l]) * dot(spread_rows, dot(warm, spread))
+        j_ref[l] = f_ref[l].astype(jnp.float32) * a_ref[l]
+    first_sweep(2, x_ref, g_ref, j_ref, v_ref, W0, XN, WN, D, DI, GD, JD, EH, EV)
+
+
+def bulk_mid_kernel(X, V, W, D, DI, GD, JD, G, XN, WN, DN):
+    keep, gain = sweep_gains()[0]
+    next_sweep(2, keep, gain, X, V, W, D, DI, GD, JD, G, XN, WN, DN)
+
+
+def bulk_last_kernel(
+    X, V, W, D, DI, GD, JD, EH, EV, xr_ref, xc_ref,
+    x_hbm, h_ref,
+    XN, PA, PB, PD, out, sem,
+):
+    layers, rows, cols = X.shape
     cell_rows, cells = h_ref.shape[1:]
-    fold_rows = spread_lanes(cell_rows, rows)
-    fold_cols = gather_lanes(cols, cells)
-    pick = uniform(even, (SUB, cells))
+    groups = rows // SUB
+    keep, gain = sweep_gains()[-1]
+    next_sweep(2, keep, gain, X, V, W, D, DI, GD, JD, None, XN)
+    lane = iota((rows, LANE), 1)
     for l in range(layers):
-        xo_ref[l] = X[l, own_rows, 0:cols]
-        heat = dot(dot(fold_rows, PW[l]), fold_cols) * heat_gain
-        h_ref[l] = heat
-        top, bot = heat[:SUB], heat[cell_rows - SUB :]
-        he_ref[l] = jnp.where(pick, bot, top)
-        ho_ref[l] = jnp.where(pick, top, bot)
-
-
-def heat_rows(h_ref, e_ref, o_ref, l):
+        for t in range(cols // LANE):
+            tile = slice(t * LANE, (t + 1) * LANE)
+            x = jnp.concatenate(
+                [xr_ref[l, 0:SUB, tile], XN[l, SUB : rows - SUB, tile], xr_ref[l, SUB : 2 * SUB, tile]], 0
+            )
+            if t == 0:
+                x = jnp.where(lane < SUB, xc_ref[l], x)
+            if t == cols // LANE - 1:
+                x = jnp.where(lane >= LANE - SUB, xc_ref[l], x)
+            out[l, :, tile] = x
+    copy = pltpu.make_async_copy(out, x_hbm, sem)
+    copy.start()
+    PD[:, :, 0:SUB, :] = jnp.zeros((layers, cols // LANE, SUB, LANE), jnp.float32)
+    power_rows(0, groups, 2, XN, V, EH, EV, PA, PB, PD)
+    heat = fold_power(0, cell_rows, PA, PB, PD, *fold_matrices(cols, cells))
+    for l in range(layers):
+        h_ref[l] = heat[l]
+    copy.wait()
+
+
+def row_strip_kernel(
+    x_t, x_b, g_t, g_b, j_t, j_b, v_t, v_b,
+    x_l, x_r, g_l, g_r, j_l, j_r, v_l, v_r,
+    re_ref, ro_ref,
+    xr_ref, h_ref, strip_ref,
+    X, G, J, V, W0, XN, WN, D, DI, GD, JD, EH, EV, PA, PB, PD, DN, XL,
+):
+    layers, deep, cols = x_t.shape
+    rows = x_l.shape[1]
+    cells = h_ref.shape[2]
+    half = 2 * layers
+    height = 2 * (SUB + deep)
+    plane = 0
+    lane = iota((rows + 2 * SUB, LANE), 1)
+    for top_ref, bot_ref, left_ref, right_ref, pad in (
+        (x_t, x_b, x_l, x_r, X), (g_t, g_b, g_l, g_r, G), (j_t, j_b, j_l, j_r, J), (v_t, v_b, v_l, v_r, V),
+    ):
+        for l in range(top_ref.shape[0]):
+            top, bot = row_margin(re_ref, ro_ref, plane, slice(0, cols), half)
+            pad[l, 0:SUB, :] = top
+            pad[l, SUB : SUB + deep, :] = top_ref[l].astype(jnp.float32)
+            pad[l, SUB + deep : SUB + 2 * deep, :] = bot_ref[l].astype(jnp.float32)
+            pad[l, SUB + 2 * deep : height, :] = bot
+            left = jnp.concatenate([top[:, :LANE], left_ref[l].astype(jnp.float32), bot[:, :LANE]], 0)
+            right = jnp.concatenate(
+                [top[:, cols - LANE :], right_ref[l].astype(jnp.float32), bot[:, cols - LANE :]], 0
+            )
+            strip_ref[plane] = jnp.where(lane < LANE // 4, left, pltpu.roll(right, LANE // 2, 1))
+            plane += 1
+    first_sweep(6, X, G, J, V, W0, XN, WN, D, DI, GD, JD, EH, EV)
+    later_sweeps(6, XN, V, WN, D, DI, GD, JD, G, W0, XL, DN)
+    groups = height // SUB
+    power_rows(0, groups - 1, 6, XL, V, EH, EV, PA, PB, PD)
+    heat = fold_power(SUB, 2 * SUB // 2, PA, PB, PD, *fold_matrices(cols, cells))
+    for l in range(layers):
+        h_ref[l] = heat[l]
+        xr_ref[l, 0:SUB, :] = XL[l, SUB : 2 * SUB, :]
+        xr_ref[l, SUB : 2 * SUB, :] = XL[l, height - 2 * SUB : height - SUB, :]
+
+
+def col_strip_kernel(
+    strip_ref, ce_ref, co_ref, hr_ref,
+    xc_ref, hc_ref, hm_ref,
+    X, G, J, V, W0, XN, WN, D, DI, GD, JD, EH, EV, PA, PB, PD, DN, XL,
+):
+    layers, rows, _ = xc_ref.shape
+    cell_rows, cells = hc_ref.shape[1:]
+    height = rows + 2 * SUB
+    mixed = col_margin(ce_ref[...], co_ref[...], False, LANE // 2 + REACH)
+    lane = iota((height, LANE), 1)
+    from_right = (lane >= LANE // 2) & (lane < LANE // 2 + REACH)
+    margin = from_right | (lane >= LANE - REACH)
+    plane = 0
+    for pad in (X, G, J, V):
+        for l in range(pad.shape[0]):
+            shift = (LANE // 2 - 8 * plane) % LANE
+            value = pltpu.roll(mixed, shift, 1) if shift else mixed
+            pad[l] = jnp.where(margin, value, strip_ref[plane])
+            plane += 1
+    groups = height // SUB
+    first_sweep(9, X, G, J, V, W0, XN, WN, D, DI, GD, JD, EH, EV)
+    later_sweeps(9, XN, V, WN, D, DI, GD, JD, G, W0, XL, DN)
+    power_rows(0, groups - 1, 17, XL, V, EH, EV, PA, PB, PD)
+    n, c = iota((LANE, cells), 0), iota((LANE, cells), 1)
+    near = lax.shift_right_logical(n, 2) == jnp.where(c < cells // 2, c, c - cells + LANE // 8)
+    before_it = n == (REFINE * jnp.where(c < cells // 2, c, c - cells + LANE // 8) - 1) % LANE
+    at_edge = (c < REACH) | (c >= cells - REACH)
+    heat = fold_power(
+        SUB, cell_rows, PA, PB, PD,
+        (near & at_edge).astype(jnp.float32), (before_it & at_edge).astype(jnp.float32),
+    )
+    lane = iota((rows, LANE), 1)
+    cell = iota((SUB, cells), 1)
+    edge = (cell < REACH - 1) | (cell > cells - REACH)
+    for l in range(layers):
+        hc_ref[l] = heat[l]
+        x = XL[l, SUB : SUB + rows, :]
+        xc_ref[l] = jnp.where(lane < LANE // 2, x, pltpu.roll(x, LANE // 2, 1))
+        own = jnp.concatenate([heat[l][:REACH], heat[l][cell_rows - REACH :]], 0)
+        hm_ref[l] = jnp.where(edge, own, hr_ref[l])
+
+
+def heat_rows(own, e_ref, o_ref, l):
     even, above, below = place("row")
     e, o = e_ref[l], o_ref[l]
     pick = uniform(even, e.shape)
     top = jnp.where(uniform(above, e.shape), jnp.where(pick, o, e), 0.0)
     bot = jnp.where(uniform(below, e.shape), jnp.where(pick, e, o), 0.0)
-    return jnp.concatenate([top, h_ref[l], bot], axis=0)
-
-
-def pack_heat_kernel(h_ref, re_ref, ro_ref, e_ref, o_ref):
+    return jnp.concatenate([top, own, bot], axis=0)
+
+
+def pack_heat_kernel(h_ref, re_ref, ro_ref, _, e_ref, o_ref):
     layers, cell_rows, cells = h_ref.shape
     height = cell_rows + 2 * SUB
     even, _, _ = place("col")
@@ -349,7 +523,7 @@
     slot, low = lax.shift_right_logical(lane, 3), lane % 8 < REACH
     left = right = jnp.zeros((height, LANE), jnp.float32)
     for l in range(layers):
-        value = heat_rows(h_ref, re_ref, ro_ref, l)
+        value = heat_rows(h_ref[l], re_ref, ro_ref, l)
         mine = (slot == l) & low
         left = jnp.where(mine, pltpu.roll(value[:, :LANE], 8 * l, 1) if l else value[:, :LANE], left)
         right = jnp.where(mine, pltpu.roll(value[:, cells - LANE :], 8 * l + REACH, 1), right)
@@ -359,13 +533,17 @@
 
 
 def warm_kernel(
-    w_ref, h_ref, re_ref, ro_ref, ce_ref, co_ref, hre_ref, hro_ref, hce_ref, hco_ref, out_ref
+    w_ref, h_ref, hm_ref, hc_ref, re_ref, ro_ref, ce_ref, co_ref,
+    hre_ref, hro_ref, hce_ref, hco_ref, out_ref,
 ):
     layers, cell_rows, cells = w_ref.shape
     half = 2 * layers
     height, width = cell_rows + 2 * SUB, cells + LANE
-    warm_mixed = col_margin(ce_ref[0:height, :], co_ref[0:height, :], True)
-    heat_mixed = col_margin(hce_ref[...], hco_ref[...], False)
+    warm_mixed = col_margin(ce_ref[0:height, :], co_ref[0:height, :], True, REACH)
+    heat_mixed = col_margin(hce_ref[...], hco_ref[...], False, REACH)
+    cell = iota((cell_rows, cells), 1)
+    edge = (cell < REACH - 1) | (cell > cells - REACH)
+    cell_row = iota((SUB, cells), 0)
     theta, heat = [], []
     for l in range(layers):
         top, bot = row_margin(
@@ -373,7 +551,12 @@
         )
         own = jnp.concatenate([top, w_ref[l], bot], axis=0)
         theta.append(jnp.concatenate([own, margin_tile(warm_mixed, 8 * l + REACH)], axis=1))
-        own = heat_rows(h_ref, hre_ref, hro_ref, l)
+        own = jnp.where(edge, hc_ref[l], h_ref[l])
+        first, final = own[:SUB], own[cell_rows - SUB :]
+        first = jnp.where(cell_row < REACH - 1, hm_ref[l], first)
+        final = jnp.where(cell_row > SUB - REACH, hm_ref[l], final)
+        own = jnp.concatenate([first, own[SUB : cell_rows - SUB], final], axis=0)
+        own = heat_rows(own, hre_ref, hro_ref, l)
         heat.append(jnp.concatenate([own, margin_tile(heat_mixed, 8 * l)], axis=1))
     _, above, below = place("row")
     _, before, after = place("col")
@@ -430,7 +613,7 @@
             lax.ppermute(m, BOTH, tables(mesh_rows, mesh_cols, first)) for first, m in enumerate((e, o))
         )
 
-    params = pltpu.CompilerParams(vmem_limit_bytes=40 * 1024 * 1024)
+    params = pltpu.CompilerParams(vmem_limit_bytes=24 * 1024 * 1024)
     row_args, row_specs = [], []
     for a in (x, base, warm, via, feeder, amps):
         end = last_cell_row if a is warm else last_row
@@ -443,23 +626,22 @@
         in_specs=row_specs,
         out_specs=(full(message), full(message)),
         out_shape=(message, message),
-        compiler_params=pltpu.CompilerParams(vmem_limit_bytes=60 * 1024 * 1024),
+        compiler_params=pltpu.CompilerParams(vmem_limit_bytes=58 * 1024 * 1024),
         name="pack_rows",
     )(*row_args)
     row_e, row_o = swap(e, o, row_swaps)
 
-    fine = pl.BlockSpec((1, rows, cols), lambda l: (l, 0, 0))
-    coarse = pl.BlockSpec((1, cell_rows, cells), lambda l: (l, 0, 0))
-    g, inject = pl.pallas_call(
-        fields_kernel,
-        grid=(layers,),
-        in_specs=[fine, coarse, fine, fine],
-        out_specs=(fine, fine),
-        out_shape=(shape(layers, rows, cols),) * 2,
+    fields = (shape(layers, rows, cols),) * 10
+    node_scratch = pltpu.VMEM((layers, rows, cols), f32)
+    g, inject, *mid = pl.pallas_call(
+        bulk_first_kernel,
+        out_shape=fields,
+        scratch_shapes=[node_scratch],
         compiler_params=params,
-        name="fields",
-        cost_estimate=pl.CostEstimate(flops=8 * x.size, bytes_accessed=20 * x.size, transcendentals=x.size),
-    )(base, warm, feeder, amps)
+        name="bulk_first",
+        cost_estimate=pl.CostEstimate(flops=40 * x.size, bytes_accessed=60 * x.size, transcendentals=0),
+    )(x, base, warm, via, feeder, amps)
+    x_mid, w_mid, d_mid, inv_diag, g_diag, j_diag, edge_h, edge_v = mid
 
     col_args, col_specs = [], []
     for a in (x, g, inject, via):
@@ -477,33 +659,77 @@
     )(*col_args, warm, row_e, row_o)
     col_e, col_o = swap(e, o, col_swaps)
 
-    pad = pltpu.VMEM((layers, rows + 4 * SUB, cols + LANE), f32)
-    pad_via = pltpu.VMEM((layers - 1, rows + 4 * SUB, cols + LANE), f32)
-    edge = shape(layers, SUB, cells)
-    voltage, heat, e, o = pl.pallas_call(
-        sweeps_kernel,
-        out_shape=(shape(layers, rows, cols), shape(layers, cell_rows, cells), edge, edge),
-        scratch_shapes=[pad, pad, pad, pad_via, pad, pad, pad, pad, pad, pltpu.VMEM((layers, rows, cols), f32)],
+    def strip_scratch(height, width):
+        node = pltpu.VMEM((layers, height, width), f32)
+        taller = pltpu.VMEM((layers, width // LANE, height + SUB, LANE), f32)
+        return [node] * 3 + [pltpu.VMEM((layers - 1, height, width), f32)] + [node] * 9 + [taller] * 3 + [node] * 2
+
+    def edge_deep(a, at):
+        return pl.BlockSpec((a.shape[0], 2 * SUB, a.shape[2]), lambda _, at=at: (0, at, 0))
+
+    deep_args, deep_specs = [], []
+    for a in (x, g, inject, via):
+        deep_args += [a, a]
+        deep_specs += [edge_deep(a, 0), edge_deep(a, rows // (2 * SUB) - 1)]
+    edge_x, edge_h2 = shape(layers, 2 * SUB, cols), shape(layers, SUB, cells)
+    strip = shape(4 * layers - 1, rows + 2 * SUB, LANE)
+    x_rows, heat_strip, strip = pl.pallas_call(
+        row_strip_kernel,
+        grid=(1,),
+        in_specs=deep_specs + col_specs + [full(row_e), full(row_o)],
+        out_specs=(full(edge_x), full(edge_h2), full(strip)),
+        out_shape=(edge_x, edge_h2, strip),
+        scratch_shapes=strip_scratch(6 * SUB, cols),
         compiler_params=params,
-        name="sweeps",
-    )(x, g, inject, via, row_e, row_o, col_e, col_o)
-    heat_row_e, heat_row_o = swap(e, o, row_swaps)
+        name="row_strip",
+        cost_estimate=pl.CostEstimate(flops=40 * x.size, bytes_accessed=20 * x.size, transcendentals=0),
+    )(*deep_args, *col_args, row_e, row_o)
+
+    x_cols, heat_cols, heat_edge = pl.pallas_call(
+        col_strip_kernel,
+        out_shape=(shape(layers, rows, LANE), shape(layers, cell_rows, cells), edge_h2),
+        scratch_shapes=strip_scratch(rows + 2 * SUB, LANE),
+        compiler_params=params,
+        name="col_strip",
+    )(strip, col_e, col_o, heat_strip)
+    heat_row_e, heat_row_o = swap(heat_edge, heat_edge, row_swaps)
+
+    assert SWEEPS == 3
+    x_next, w_next, d_next = pl.pallas_call(
+        bulk_mid_kernel,
+        out_shape=(shape(layers, rows, cols),) * 3,
+        compiler_params=params,
+        name="bulk_mid",
+        cost_estimate=pl.CostEstimate(flops=20 * x.size, bytes_accessed=20 * x.size, transcendentals=0),
+    )(x_mid, via, w_mid, d_mid, inv_diag, g_diag, j_diag, g)
 
     message = shape(cell_rows + 2 * SUB, LANE)
     e, o = pl.pallas_call(
         pack_heat_kernel,
+        in_specs=[pl.BlockSpec(memory_space=pltpu.VMEM)] * 3 + [pl.BlockSpec(memory_space=pl.ANY)],
         out_shape=(message, message),
         compiler_params=params,
         name="pack_heat",
-    )(heat, heat_row_e, heat_row_o)
+    )(heat_cols, heat_row_e, heat_row_o, x_next)
     heat_col_e, heat_col_o = swap(e, o, col_swaps)
+
+    tall = pltpu.VMEM((layers, cols // LANE, rows + SUB, LANE), f32)
+    voltage, heat = pl.pallas_call(
+        bulk_last_kernel,
+        out_shape=(shape(layers, rows, cols), shape(layers, cell_rows, cells)),
+        out_specs=(pl.BlockSpec(memory_space=pl.ANY), pl.BlockSpec(memory_space=pltpu.VMEM)),
+        scratch_shapes=[node_scratch] + [tall] * 3 + [node_scratch, pltpu.SemaphoreType.DMA],
+        compiler_params=params,
+        name="bulk_last",
+        cost_estimate=pl.CostEstimate(flops=40 * x.size, bytes_accessed=60 * x.size, transcendentals=0),
+    )(x_next, via, w_next, d_next, inv_diag, g_diag, j_diag, edge_h, edge_v, x_rows, x_cols)
 
     warmth = pl.pallas_call(
         warm_kernel,
         out_shape=shape(layers, cell_rows, cells),
         compiler_params=params,
         name="warm",
-    )(warm, heat, row_e, row_o, col_e, col_o, heat_row_e, heat_row_o, heat_col_e, heat_col_o)
+    )(warm, heat, heat_edge, heat_cols, row_e, row_o, col_e, col_o, heat_row_e, heat_row_o, heat_col_e, heat_col_o)
     return voltage, warmth
 
 

time: 37.5 us -> 29.6 us (0.79)
  waiting for transfers between devices: 6.49 us -> 1.05 us
  starting transfers between devices: 11.5 us -> 10.3 us
  Pallas kernels: 18.2 us -> 17.1 us
    ppermute x8, waiting for transfers between devices: 6.49 us -> 1.05 us  [swap(): lax.ppermute(m, BOTH, tables(mesh_rows, mesh_cols, first))]
    ppermute x8, starting transfers between devices: 11.5 us -> 10.3 us  [swap(): lax.ppermute(m, BOTH, tables(mesh_rows, mesh_cols, first))]
    pallas_call x3 -> x6, Pallas kernels: 13.6 us -> 12.5 us  [the longest x1 3.74 us: on_device(): pl.pallas_call(bulk_first_kernel, out_shape=fields, scratch_shapes=[node_...]
  transfers between devices with their start and end apart: 8 -> 8, of which waited for: 4 -> 2; matrix products, arithmetic and copies ran while one was open for 0% -> 0% of each run, Pallas kernels for 6% -> 35%
where the time goes in v2:
time: 29.6 us; the launch traced here: 29.3 us
  Pallas kernels  17.1 us (58%)
  starting transfers between devices  10.3 us (35%)
  waiting for transfers between devices  1.05 us (4%)
  between operations  0.8 us (3%)
    ppermute x8, starting transfers between devices, swap(): lax.ppermute(m, BOTH, tables(mesh_rows, mesh_cols, first))  10.3 us
    pallas_call x1, Pallas kernels, on_device(): pl.pallas_call(bulk_first_kernel, out_shape=fields, scratch_shapes=[node_...  3.74 us
    pallas_call x1, Pallas kernels, on_device(): pl.pallas_call(bulk_last_kernel, out_shape=(shape(layers, rows, cols), sh...  3.13 us
    pallas_call x1, Pallas kernels, on_device(): pl.pallas_call(pack_rows_kernel, grid=(1,), in_specs=row_specs, out_specs...  2.25 us
    pallas_call x1, Pallas kernels, on_device(): pl.pallas_call(col_strip_kernel, out_shape=(shape(layers, rows, LANE), sh...  2.17 us
    pallas_call x1, Pallas kernels, on_device(): pl.pallas_call(row_strip_kernel, grid=(1,), in_specs=deep_specs + col_spe...  2.13 us
    pallas_call x1, Pallas kernels, on_device(): pl.pallas_call(warm_kernel, out_shape=shape(layers, cell_rows, cells), co...  1.63 us
    pallas_call x1, Pallas kernels, on_device(): pl.pallas_call(bulk_mid_kernel, out_shape=(shape(layers, rows, cols),) *...  1.25 us
  transfers between devices with their start and end apart: 8, of which 2 were waited for; matrix products, arithmetic and copies ran while one was open for 0% of the time, Pallas kernels for 35%

profile of v2, /device:TPU:0, one launch (start us, length us, event | category | flops | bytes accessed | tf_op | source)
XLA Modules:
  0.0 29.3 jit_solution(11931316752602945012)
XLA Ops:
  0.6 0.0 copy-start.3
  0.6 0.0 copy-start.4
  0.7 0.0 copy-start.1
  0.7 0.0 copy-start.2
  0.7 0.0 copy-start.5
  0.7 0.0 copy-start
  0.7 2.2 %pack_rows.1 = (f32[8,8,512]{2,1,0:T(8,128)}, f32[8,8,512]{2,1,0:T(8,128)}) custom-call(f32[4,128,512]{2,1,0:T(8,128)} %x_r.3, f32[4,128,512]{2,1,0:T(8,128)} %x_r.3, f32[4,128,512]{2,1,0:T(8,128)} %b_b.1, f32[4,128,512]{2,1,0:T(8,128)} %b_b.1, f32[4,32,128]{2,1,0:T(8,128)} %w_ref.5, f32[4,32,128]{2,1,0:T(8,128)} %w_ref.5, s32[3,128,512]{2,1,0:T(8,128)} %V.3, ...), custom_call_target="tpu_custom_call" | custom-call | tf_op jit(solution)/shard_map/pack_rows/pallas_call | solution.py:623
  2.9 0.5 %collective-permute-start = (f32[8,8,512]{2,1,0:T(8,128)}, f32[8,8,512]{2,1,0:T(8,128)S(1)}, u32[]{:S(2)}, u32[]{:S(2)}) collective-permute-start(f32[8,8,512]{2,1,0:T(8,128)} %get-tuple-element.42), channel_id=1, source_target_pairs={{0,4},{1,5},{2,6},{3,7},{4,0},{5,1},{6,2},{7,3},{8,12},{9,13},{10,... | collective-permute-start | bytes 393224 | tf_op jit(solution)/shard_map/ppermute | solution.py:613
  3.4 2.6 %collective-permute-start.1 = (f32[8,8,512]{2,1,0:T(8,128)}, f32[8,8,512]{2,1,0:T(8,128)S(1)}, u32[]{:S(2)}, u32[]{:S(2)}) collective-permute-start(f32[8,8,512]{2,1,0:T(8,128)} %get-tuple-element.43), channel_id=1, source_target_pairs={{0,1},{1,0},{2,3},{3,2},{4,8},{5,9},{6,10},{7,11},{8,4},{9,5},{10,... | collective-permute-start | bytes 393224 | tf_op jit(solution)/shard_map/ppermute | solution.py:613
  6.0 0.0 copy-done.3
  6.0 0.0 copy-done.4
  6.0 0.0 copy-done.1
  6.0 0.0 copy-done.2
  6.0 0.0 copy-done.5
  6.0 0.0 copy-done
  6.1 3.7 %bulk_first.1 = (f32[4,128,512]{2,1,0:T(8,128)S(1)}, f32[4,128,512]{2,1,0:T(8,128)S(1)}, f32[4,128,512]{2,1,0:T(8,128)S(1)}, f32[4,128,512]{2,1,0:T(8,128)S(1)},...) custom-call(f32[4,128,512]{2,1,0:T(8,128)S(1)} %copy-done.1, ...), custom_call_target="tpu_custom_call" | custom-call | flops 10485760 | bytes 15728640 | tf_op jit(solution)/shard_map/bulk_first/pallas_call | solution.py:636
  9.8 0.0 collective-permute-done.re_ref
  9.8 0.0 collective-permute-done.1.ro_ref
  9.8 0.7 %pack_cols.1 = (f32[144,128]{1,0:T(8,128)S(1)}, f32[144,128]{1,0:T(8,128)S(1)}) custom-call(f32[4,128,512]{2,1,0:T(8,128)S(1)} %copy-done.1, f32[4,128,512]{2,1,0:T(8,128)S(1)} %copy-done.1, f32[4,128,512]{2,1,0:T(8,128)S(1)} %get-tuple-element.35.G.g_t.g_b.g_l.g_r, f32[4,128,512]{2,1,0:T(8,128)S(1)} %get-tuple-element.35.G.g_t.g_b.g_l.g_r, ...), custom_call_target="tpu_custom_call" | custom-call | tf_op jit(solution)/shard_map/pack_cols/pallas_call | solution.py:651
  10.5 1.4 %collective-permute-start.2 = (f32[144,128]{1,0:T(8,128)S(1)}, f32[144,128]{1,0:T(8,128)S(1)}, u32[]{:S(2)}, u32[]{:S(2)}) collective-permute-start(f32[144,128]{1,0:T(8,128)S(1)} %get-tuple-element.46), channel_id=1, source_target_pairs={{0,1},{1,0},{2,3},{3,2},{4,5},{5,4},{6,7},{7,6},{8,9},{9,8},{10,11... | collective-permute-start | bytes 221192 | tf_op jit(solution)/shard_map/ppermute | solution.py:613
  12.0 0.7 %collective-permute-start.3 = (f32[144,128]{1,0:T(8,128)S(1)}, f32[144,128]{1,0:T(8,128)S(1)}, u32[]{:S(2)}, u32[]{:S(2)}) collective-permute-start(f32[144,128]{1,0:T(8,128)S(1)} %get-tuple-element.47), channel_id=1, source_target_pairs={{0,4},{1,2},{2,1},{3,7},{4,0},{5,6},{6,5},{7,3},{8,12},{9,10},{10,... | collective-permute-start | bytes 221192 | tf_op jit(solution)/shard_map/ppermute | solution.py:613
  12.6 2.1 %row_strip.1 = (f32[4,16,512]{2,1,0:T(8,128)S(1)}, f32[4,8,128]{2,1,0:T(8,128)S(1)}, f32[15,144,128]{2,1,0:T(8,128)S(1)}) custom-call(f32[4,128,512]{2,1,0:T(8,128)S(1)} %copy-done.1, f32[4,128,512]{2,1,0:T(8,128)S(1)} %copy-done.1, f32[4,128,512]{2,1,0:T(8,128)S(1)} %get-tuple-element.35.G.g_t.g_b.g_l.g_r, ...), custom_call_target="tpu_custom_call" | custom-call | flops 10485760 | bytes 5242880 | tf_op jit(solution)/shard_map/row_strip/pallas_call | solution.py:676
  14.8 0.6 %collective-permute-done.2.ce_ref = f32[144,128]{1,0:T(8,128)S(1)} collective-permute-done((f32[144,128]{1,0:T(8,128)S(1)}, f32[144,128]{1,0:T(8,128)S(1)}, u32[]{:S(2)}, u32[]{:S(2)}) %collective-permute-start.2) | collective-permute-done | bytes 73760 | tf_op jit(solution)/shard_map/ppermute | solution.py:613
  15.3 0.0 collective-permute-done.3.co_ref
  15.4 2.2 %col_strip.1 = (f32[4,128,128]{2,1,0:T(8,128)S(1)}, f32[4,32,128]{2,1,0:T(8,128)S(1)}, f32[4,8,128]{2,1,0:T(8,128)S(1)}) custom-call(f32[15,144,128]{2,1,0:T(8,128)S(1)} %get-tuple-element.45.strip_ref, f32[144,128]{1,0:T(8,128)S(1)} %collective-permute-done.2.ce_ref, f32[144,128]{1,0:T(8,128)S(1)} %collective-permute-done.3.co_ref, ...), custom_call_target="tpu_custom_call" | custom-call | tf_op jit(solution)/shard_map/col_strip/pallas_call | solution.py:688
  17.5 0.1 collective-permute-start.4
  17.6 3.0 %collective-permute-start.5 = (f32[4,8,128]{2,1,0:T(8,128)S(1)}, f32[4,8,128]{2,1,0:T(8,128)S(1)}, u32[]{:S(2)}, u32[]{:S(2)}) collective-permute-start(f32[4,8,128]{2,1,0:T(8,128)S(1)} %get-tuple-element.52.hm_ref), channel_id=1, source_target_pairs={{0,1},{1,0},{2,3},{3,2},{4,8},{5,9},{6,10},{7,11},{8,4},{9,5},{10,... | collective-permute-start | bytes 49160 | tf_op jit(solution)/shard_map/ppermute | solution.py:613
  20.6 1.3 %bulk_mid.1 = (f32[4,128,512]{2,1,0:T(8,128)S(1)}, f32[4,128,512]{2,1,0:T(8,128)S(1)}, f32[4,128,512]{2,1,0:T(8,128)S(1)}) custom-call(f32[4,128,512]{2,1,0:T(8,128)S(1)} %get-tuple-element.29.X, s32[3,128,512]{2,1,0:T(8,128)S(1)} %copy-done, f32[4,128,512]{2,1,0:T(8,128)S(1)} %get-tuple-element.30.W, f32[4,128,512]{2,1,0:T(8,128)S(1)} %get-tuple-element.31.D, ...), custom_call_target="tpu_custom_call" | custom-call | flops 5242880 | bytes 5242880 | tf_op jit(solution)/shard_map/bulk_mid/pallas_call | solution.py:698
  21.8 0.0 collective-permute-done.4.re_ref.hre_ref
  21.8 0.4 %collective-permute-done.5.ro_ref.hro_ref = f32[4,8,128]{2,1,0:T(8,128)S(1)} collective-permute-done((f32[4,8,128]{2,1,0:T(8,128)S(1)}, f32[4,8,128]{2,1,0:T(8,128)S(1)}, u32[]{:S(2)}, u32[]{:S(2)}) %collective-permute-start.5) | collective-permute-done | bytes 16416 | tf_op jit(solution)/shard_map/ppermute | solution.py:613
  22.3 0.1 pack_heat.1
  22.4 2.1 %collective-permute-start.6 = (f32[48,128]{1,0:T(8,128)S(1)}, f32[48,128]{1,0:T(8,128)S(1)}, u32[]{:S(2)}, u32[]{:S(2)}) collective-permute-start(f32[48,128]{1,0:T(8,128)S(1)} %get-tuple-element.54), channel_id=1, source_target_pairs={{0,1},{1,0},{2,3},{3,2},{4,5},{5,4},{6,7},{7,6},{8,9},{9,8},{10,11... | collective-permute-start | bytes 73736 | tf_op jit(solution)/shard_map/ppermute | solution.py:613
  24.5 0.0 collective-permute-start.7
  24.5 3.1 %bulk_last.1 = (f32[4,128,512]{2,1,0:T(8,128)}, f32[4,32,128]{2,1,0:T(8,128)S(1)}) custom-call(f32[4,128,512]{2,1,0:T(8,128)S(1)} %get-tuple-element.36.X._, s32[3,128,512]{2,1,0:T(8,128)S(1)} %copy-done, f32[4,128,512]{2,1,0:T(8,128)S(1)} %get-tuple-element.37.W, f32[4,128,512]{2,1,0:T(8,128)S(1)} %get-tuple-element.38.D, ...), custom_call_target="tpu_custom_call" | custom-call | flops 10485760 | bytes 15728640 | tf_op jit(solution)/shard_map/bulk_last/pallas_call | solution.py:717
  27.6 0.0 collective-permute-done.6.hce_ref
  27.6 0.0 collective-permute-done.7.hco_ref
  27.7 1.6 %warm.1 = f32[4,32,128]{2,1,0:T(8,128)} custom-call(f32[4,32,128]{2,1,0:T(8,128)S(1)} %copy-done.5, f32[4,32,128]{2,1,0:T(8,128)S(1)} %get-tuple-element.51.h_ref, f32[4,8,128]{2,1,0:T(8,128)S(1)} %get-tuple-element.52.hm_ref, f32[4,32,128]{2,1,0:T(8,128)S(1)} %get-tuple-element.53.h_ref.hc_ref, f32[8,8,512]{2,1,0:T(8,128)S(1)} %collective-permute-done.re_ref, ...), custom_call_target="tpu_custom_call" | custom-call | tf_op jit(solution)/shard_map/warm/pallas_call | solution.py:727
Async XLA Ops:
  0.6 5.4 %copy-start.3 = (s32[4,128,512]{2,1,0:T(8,128)S(1)}, s32[4,128,512]{2,1,0:T(8,128)}, u32[]{:S(2)}) copy-start(s32[4,128,512]{2,1,0:T(8,128)} %f_b.1) | copy-start | bytes 3145732
  0.6 5.4 %copy-start.4 = (f32[4,128,512]{2,1,0:T(8,128)S(1)}, f32[4,128,512]{2,1,0:T(8,128)}, u32[]{:S(2)}) copy-start(f32[4,128,512]{2,1,0:T(8,128)} %a_b.1) | copy-start | bytes 3145732
  0.7 5.4 %copy-start.1 = (f32[4,128,512]{2,1,0:T(8,128)S(1)}, f32[4,128,512]{2,1,0:T(8,128)}, u32[]{:S(2)}) copy-start(f32[4,128,512]{2,1,0:T(8,128)} %x_r.3) | copy-start | bytes 3145732
  0.7 5.4 %copy-start.2 = (f32[4,128,512]{2,1,0:T(8,128)S(1)}, f32[4,128,512]{2,1,0:T(8,128)}, u32[]{:S(2)}) copy-start(f32[4,128,512]{2,1,0:T(8,128)} %b_b.1) | copy-start | bytes 3145732
  0.7 5.4 %copy-start.5 = (f32[4,32,128]{2,1,0:T(8,128)S(1)}, f32[4,32,128]{2,1,0:T(8,128)}, u32[]{:S(2)}) copy-start(f32[4,32,128]{2,1,0:T(8,128)} %w_ref.5) | copy-start | bytes 196612
  0.7 5.4 %copy-start = (s32[3,128,512]{2,1,0:T(8,128)S(1)}, s32[3,128,512]{2,1,0:T(8,128)}, u32[]{:S(2)}) copy-start(s32[3,128,512]{2,1,0:T(8,128)} %V.3) | copy-start | bytes 2359300
  2.9 6.9 %collective-permute-start = (f32[8,8,512]{2,1,0:T(8,128)}, f32[8,8,512]{2,1,0:T(8,128)S(1)}, u32[]{:S(2)}, u32[]{:S(2)}) collective-permute-start(f32[8,8,512]{2,1,0:T(8,128)} %get-tuple-element.42), channel_id=1, source_target_pairs={{0,4},{1,5},{2,6},{3,7},{4,0},{5,1},{6,2},{7,3},{8,12},{9,13},{10,... | collective-permute-start | bytes 393224 | tf_op jit(solution)/shard_map/ppermute | solution.py:613
  3.4 6.4 %collective-permute-start.1 = (f32[8,8,512]{2,1,0:T(8,128)}, f32[8,8,512]{2,1,0:T(8,128)S(1)}, u32[]{:S(2)}, u32[]{:S(2)}) collective-permute-start(f32[8,8,512]{2,1,0:T(8,128)} %get-tuple-element.43), channel_id=1, source_target_pairs={{0,1},{1,0},{2,3},{3,2},{4,8},{5,9},{6,10},{7,11},{8,4},{9,5},{10,... | collective-permute-start | bytes 393224 | tf_op jit(solution)/shard_map/ppermute | solution.py:613
  10.5 4.8 %collective-permute-start.2 = (f32[144,128]{1,0:T(8,128)S(1)}, f32[144,128]{1,0:T(8,128)S(1)}, u32[]{:S(2)}, u32[]{:S(2)}) collective-permute-start(f32[144,128]{1,0:T(8,128)S(1)} %get-tuple-element.46), channel_id=1, source_target_pairs={{0,1},{1,0},{2,3},{3,2},{4,5},{5,4},{6,7},{7,6},{8,9},{9,8},{10,11... | collective-permute-start | bytes 221192 | tf_op jit(solution)/shard_map/ppermute | solution.py:613
  12.0 3.4 %collective-permute-start.3 = (f32[144,128]{1,0:T(8,128)S(1)}, f32[144,128]{1,0:T(8,128)S(1)}, u32[]{:S(2)}, u32[]{:S(2)}) collective-permute-start(f32[144,128]{1,0:T(8,128)S(1)} %get-tuple-element.47), channel_id=1, source_target_pairs={{0,4},{1,2},{2,1},{3,7},{4,0},{5,6},{6,5},{7,3},{8,12},{9,10},{10,... | collective-permute-start | bytes 221192 | tf_op jit(solution)/shard_map/ppermute | solution.py:613
  17.5 4.3 %collective-permute-start.4 = (f32[4,8,128]{2,1,0:T(8,128)S(1)}, f32[4,8,128]{2,1,0:T(8,128)S(1)}, u32[]{:S(2)}, u32[]{:S(2)}) collective-permute-start(f32[4,8,128]{2,1,0:T(8,128)S(1)} %get-tuple-element.52.hm_ref), channel_id=1, source_target_pairs={{0,4},{1,5},{2,6},{3,7},{4,0},{5,1},{6,2},{7,3},{8,12},{9,13},{10,... | collective-permute-start | bytes 49160 | tf_op jit(solution)/shard_map/ppermute | solution.py:613
  17.6 4.7 %collective-permute-start.5 = (f32[4,8,128]{2,1,0:T(8,128)S(1)}, f32[4,8,128]{2,1,0:T(8,128)S(1)}, u32[]{:S(2)}, u32[]{:S(2)}) collective-permute-start(f32[4,8,128]{2,1,0:T(8,128)S(1)} %get-tuple-element.52.hm_ref), channel_id=1, source_target_pairs={{0,1},{1,0},{2,3},{3,2},{4,8},{5,9},{6,10},{7,11},{8,4},{9,5},{10,... | collective-permute-start | bytes 49160 | tf_op jit(solution)/shard_map/ppermute | solution.py:613
  22.4 5.2 %collective-permute-start.6 = (f32[48,128]{1,0:T(8,128)S(1)}, f32[48,128]{1,0:T(8,128)S(1)}, u32[]{:S(2)}, u32[]{:S(2)}) collective-permute-start(f32[48,128]{1,0:T(8,128)S(1)} %get-tuple-element.54), channel_id=1, source_target_pairs={{0,1},{1,0},{2,3},{3,2},{4,5},{5,4},{6,7},{7,6},{8,9},{9,8},{10,11... | collective-permute-start | bytes 73736 | tf_op jit(solution)/shard_map/ppermute | solution.py:613
  24.5 3.2 %collective-permute-start.7 = (f32[48,128]{1,0:T(8,128)S(1)}, f32[48,128]{1,0:T(8,128)S(1)}, u32[]{:S(2)}, u32[]{:S(2)}) collective-permute-start(f32[48,128]{1,0:T(8,128)S(1)} %get-tuple-element.55), channel_id=1, source_target_pairs={{0,4},{1,2},{2,1},{3,7},{4,0},{5,6},{6,5},{7,3},{8,12},{9,10},{10,... | collective-permute-start | bytes 73736 | tf_op jit(solution)/shard_map/ppermute | solution.py:613

commit v3 on v2

--- a/solution.py
+++ b/solution.py
@@ -118,41 +118,65 @@
     )
 
 
-def pack_cols_kernel(
-    x_l, x_r, g_l, g_r, j_l, j_r, v_l, v_r, w_ref, re_ref, ro_ref, e_ref, o_ref
-):
-    layers, rows, _ = x_l.shape
-    cols = re_ref.shape[2]
+def packed(values, side, high, out):
+    lane = iota(out.shape, 1)
+    slot, upper = lax.shift_right_logical(lane, 3), lane % 8 >= REACH
+    for p, value in enumerate(values):
+        shift = (8 * p + REACH * (side + high)) % LANE
+        value = pltpu.roll(value.astype(jnp.float32), shift, 1) if shift else value
+        out = jnp.where((slot == p) & (upper if high else ~upper), value, out)
+    return out
+
+
+def end_tiles(width):
+    return slice(0, LANE), slice(width - LANE, width)
+
+
+def pack_own_columns(fields, w_ref, e_ref, o_ref):
+    rows, cols = fields[0].shape[1:]
+    layers, cell_rows, cells = w_ref.shape
+    sides = []
+    for side in range(2):
+        tile, cell_tile = end_tiles(cols)[side], end_tiles(cells)[side]
+        values = [ref[l, :, tile] for ref in fields for l in range(ref.shape[0])]
+        out = packed(values, side, False, jnp.zeros((rows, LANE), jnp.float32))
+        head = packed([w_ref[l, :, cell_tile] for l in range(layers)], side, True, out[:cell_rows])
+        sides.append(jnp.concatenate([head, out[cell_rows:]], axis=0))
+    even, _, _ = place("col")
+    pick = uniform(even, (rows, LANE))
+    e_ref[...] = jnp.where(pick, sides[1], sides[0])
+    o_ref[...] = jnp.where(pick, sides[0], sides[1])
+
+
+def pack_cols_kernel(re_ref, ro_ref, own_e, own_o, w_ref, e_ref, o_ref):
+    rows, cols = own_e.shape[0], re_ref.shape[2]
+    layers, cell_rows, cells = w_ref.shape
     half = 2 * layers
-    cell_rows, cells = w_ref.shape[1:]
-    height, cell_height = rows + 2 * SUB, cell_rows + 2 * SUB
     even, _, _ = place("col")
-    lane = iota((height, LANE), 1)
-    slot, low = lax.shift_right_logical(lane, 3), lane % 8 < REACH
-    cell_lane = iota((cell_height, LANE), 1)
-    cell_slot, cell_high = lax.shift_right_logical(cell_lane, 3), cell_lane % 8 >= REACH
-    sides = []
-    for side, refs in enumerate(((x_l, g_l, j_l, v_l), (x_r, g_r, j_r, v_r))):
-        tile = slice(0, LANE) if side == 0 else slice(cols - LANE, cols)
-        own = [ref[l] for ref in refs for l in range(ref.shape[0])]
-        out = jnp.zeros((height, LANE), jnp.float32)
-        for p, value in enumerate(own):
-            top, bot = row_margin(re_ref, ro_ref, p, tile, half)
-            value = jnp.concatenate([top, value.astype(jnp.float32), bot], axis=0)
-            value = pltpu.roll(value, (8 * p + REACH * side) % LANE, 1)
-            out = jnp.where((slot == p) & low, value, out)
-        head = out[:cell_height]
-        for l in range(layers):
-            tile = slice(l * cells, (l + 1) * cells)
-            top, bot = row_margin(re_ref, ro_ref, 2 * half - 1, tile, half)
-            value = jnp.concatenate([top, w_ref[l], bot], axis=0)
-            value = pltpu.roll(value, (8 * l + REACH + REACH * side) % LANE, 1)
-            head = jnp.where((cell_slot == l) & cell_high, value, head)
-        sides.append(jnp.concatenate([head, out[cell_height:]], axis=0))
-    left, right = sides
-    pick = uniform(even, (height, LANE))
-    e_ref[...] = jnp.where(pick, right, left)
-    o_ref[...] = jnp.where(pick, left, right)
+    pick = uniform(even, (SUB, LANE))
+    zero = jnp.zeros((SUB, LANE), jnp.float32)
+    tops, bots, lows = [], [], []
+    for side in range(2):
+        tile, cell_tile = end_tiles(cols)[side], end_tiles(cells)[side]
+        margins = [row_margin(re_ref, ro_ref, p, tile, half) for p in range(2 * half - 1)]
+        warm = [
+            row_margin(
+                re_ref, ro_ref, 2 * half - 1,
+                slice(l * cells + cell_tile.start, l * cells + cell_tile.stop), half,
+            )
+            for l in range(layers)
+        ]
+        tops.append(packed([m[0] for m in warm], side, True, packed([m[0] for m in margins], side, False, zero)))
+        bots.append(packed([m[1] for m in margins], side, False, zero))
+        lows.append(packed([m[1] for m in warm], side, True, zero))
+    high = iota((SUB, LANE), 1) % 8 >= REACH
+    at = SUB + cell_rows
+    for ref, own, first in ((e_ref, own_e, 1), (o_ref, own_o, 0)):
+        ref[SUB : SUB + rows, :] = own[...]
+        ref[0:SUB, :] = jnp.where(pick, tops[first], tops[1 - first])
+        ref[SUB + rows : 2 * SUB + rows, :] = jnp.where(pick, bots[first], bots[1 - first])
+        low = jnp.where(pick, lows[first], lows[1 - first])
+        ref[at : at + SUB, :] = jnp.where(high, low, own[cell_rows : cell_rows + SUB, :])
 
 
 def col_margin(e, o, high, back):
@@ -241,7 +265,7 @@
     return [V[l, r, :].astype(jnp.float32) for l in range(V.shape[0])]
 
 
-def first_sweep(unroll, X, G, J, V, W0, XN, WN, D, DI, GD, JD, EH, EV):
+def first_sweep(unroll, skip, X, G, J, V, W0, XN, WN, D, DI, GD, JD, EH, EV):
     layers, height, _ = X.shape
     groups = height // SUB
 
@@ -275,10 +299,10 @@
             XN[l, r, :] = x
             WN[l, r, :] = g * x
 
-    each(0, groups, unroll, body)
-
-
-def next_sweep(unroll, keep, gain, X, V, W, D, DI, GD, JD, G, XN, WN=None, DN=None):
+    each(skip, groups - skip, unroll, body)
+
+
+def next_sweep(unroll, skip, keep, gain, X, V, W, D, DI, GD, JD, G, XN, WN=None, DN=None):
     layers, height, _ = X.shape
     groups = height // SUB
 
@@ -298,7 +322,7 @@
                 DN[l, r, :] = d
                 WN[l, r, :] = G[l, r, :] * x
 
-    each(0, groups, unroll, body)
+    each(skip, groups - skip, unroll, body)
 
 
 def later_sweeps(unroll, X, V, W, D, DI, GD, JD, G, WN, XN, DN):
@@ -306,9 +330,9 @@
     x, w, d, other = X, W, D, WN
     for at, (keep, gain) in enumerate(gains):
         if at == len(gains) - 1:
-            next_sweep(unroll, keep, gain, x, V, w, d, DI, GD, JD, G, XN)
+            next_sweep(unroll, 0, keep, gain, x, V, w, d, DI, GD, JD, G, XN)
         else:
-            next_sweep(unroll, keep, gain, x, V, w, d, DI, GD, JD, G, XN, other, DN)
+            next_sweep(unroll, 0, keep, gain, x, V, w, d, DI, GD, JD, G, XN, other, DN)
             assert len(gains) <= 2
             x, w, d = XN, other, DN
 
@@ -373,7 +397,7 @@
 
 def bulk_first_kernel(
     x_ref, b_ref, w_ref, v_ref, f_ref, a_ref,
-    g_ref, j_ref, XN, WN, D, DI, GD, JD, EH, EV,
+    g_ref, j_ref, XN, WN, D, DI, GD, JD, EH, EV, own_e, own_o,
     W0,
 ):
     layers, rows, cols = x_ref.shape
@@ -384,30 +408,42 @@
         warm = jnp.exp(-0.5 * warmth_sensitivity * w_ref[l])
         g_ref[l] = jnp.sqrt(b_ref[l]) * dot(spread_rows, dot(warm, spread))
         j_ref[l] = f_ref[l].astype(jnp.float32) * a_ref[l]
-    first_sweep(2, x_ref, g_ref, j_ref, v_ref, W0, XN, WN, D, DI, GD, JD, EH, EV)
-
-
-def bulk_mid_kernel(X, V, W, D, DI, GD, JD, G, XN, WN, DN):
-    keep, gain = sweep_gains()[0]
-    next_sweep(2, keep, gain, X, V, W, D, DI, GD, JD, G, XN, WN, DN)
+    pack_own_columns((x_ref, g_ref, j_ref, v_ref), w_ref, own_e, own_o)
+    first_sweep(2, 1, x_ref, g_ref, j_ref, v_ref, W0, XN, WN, D, DI, GD, JD, EH, EV)
+
+
+def bulk_mid_kernel(X, V, W, D, DI, GD, JD, G, XL, WN, XN, DN):
+    (keep, gain), (keep_last, gain_last) = sweep_gains()
+    next_sweep(2, 1, keep, gain, X, V, W, D, DI, GD, JD, G, XN, WN, DN)
+    next_sweep(2, 1, keep_last, gain_last, XN, V, WN, DN, DI, GD, JD, G, XL)
 
 
 def bulk_last_kernel(
-    X, V, W, D, DI, GD, JD, EH, EV, xr_ref, xc_ref,
+    XN, V, EH, EV, xr_ref, xc_ref,
     x_hbm, h_ref,
-    XN, PA, PB, PD, out, sem,
+    PA, PB, PD, out, sem,
 ):
-    layers, rows, cols = X.shape
+    layers, rows, cols = XN.shape
     cell_rows, cells = h_ref.shape[1:]
     groups = rows // SUB
-    keep, gain = sweep_gains()[-1]
-    next_sweep(2, keep, gain, X, V, W, D, DI, GD, JD, None, XN)
     lane = iota((rows, LANE), 1)
+    low = iota((SUB, LANE), 0) < REACH
     for l in range(layers):
         for t in range(cols // LANE):
             tile = slice(t * LANE, (t + 1) * LANE)
             x = jnp.concatenate(
-                [xr_ref[l, 0:SUB, tile], XN[l, SUB : rows - SUB, tile], xr_ref[l, SUB : 2 * SUB, tile]], 0
+                [
+                    xr_ref[l, 0:SUB, tile],
+                    jnp.where(low, xr_ref[l, SUB : 2 * SUB, tile], XN[l, SUB : 2 * SUB, tile]),
+                    XN[l, 2 * SUB : rows - 2 * SUB, tile],
+                    jnp.where(
+                        low,
+                        XN[l, rows - 2 * SUB : rows - SUB, tile],
+                        xr_ref[l, 2 * SUB : 3 * SUB, tile],
+                    ),
+                    xr_ref[l, 3 * SUB : 4 * SUB, tile],
+                ],
+                0,
             )
             if t == 0:
                 x = jnp.where(lane < SUB, xc_ref[l], x)
@@ -416,8 +452,7 @@
             out[l, :, tile] = x
     copy = pltpu.make_async_copy(out, x_hbm, sem)
     copy.start()
-    PD[:, :, 0:SUB, :] = jnp.zeros((layers, cols // LANE, SUB, LANE), jnp.float32)
-    power_rows(0, groups, 2, XN, V, EH, EV, PA, PB, PD)
+    power_rows(1, groups - 1, 2, XN, V, EH, EV, PA, PB, PD)
     heat = fold_power(0, cell_rows, PA, PB, PD, *fold_matrices(cols, cells))
     for l in range(layers):
         h_ref[l] = heat[l]
@@ -453,15 +488,14 @@
             )
             strip_ref[plane] = jnp.where(lane < LANE // 4, left, pltpu.roll(right, LANE // 2, 1))
             plane += 1
-    first_sweep(6, X, G, J, V, W0, XN, WN, D, DI, GD, JD, EH, EV)
+    first_sweep(6, 0, X, G, J, V, W0, XN, WN, D, DI, GD, JD, EH, EV)
     later_sweeps(6, XN, V, WN, D, DI, GD, JD, G, W0, XL, DN)
     groups = height // SUB
     power_rows(0, groups - 1, 6, XL, V, EH, EV, PA, PB, PD)
     heat = fold_power(SUB, 2 * SUB // 2, PA, PB, PD, *fold_matrices(cols, cells))
     for l in range(layers):
         h_ref[l] = heat[l]
-        xr_ref[l, 0:SUB, :] = XL[l, SUB : 2 * SUB, :]
-        xr_ref[l, SUB : 2 * SUB, :] = XL[l, height - 2 * SUB : height - SUB, :]
+        xr_ref[l] = XL[l, SUB : height - SUB, :]
 
 
 def col_strip_kernel(
@@ -484,7 +518,7 @@
             pad[l] = jnp.where(margin, value, strip_ref[plane])
             plane += 1
     groups = height // SUB
-    first_sweep(9, X, G, J, V, W0, XN, WN, D, DI, GD, JD, EH, EV)
+    first_sweep(9, 0, X, G, J, V, W0, XN, WN, D, DI, GD, JD, EH, EV)
     later_sweeps(9, XN, V, WN, D, DI, GD, JD, G, W0, XL, DN)
     power_rows(0, groups - 1, 17, XL, V, EH, EV, PA, PB, PD)
     n, c = iota((LANE, cells), 0), iota((LANE, cells), 1)
@@ -631,7 +665,7 @@
     )(*row_args)
     row_e, row_o = swap(e, o, row_swaps)
 
-    fields = (shape(layers, rows, cols),) * 10
+    fields = (shape(layers, rows, cols),) * 10 + (shape(rows, LANE),) * 2
     node_scratch = pltpu.VMEM((layers, rows, cols), f32)
     g, inject, *mid = pl.pallas_call(
         bulk_first_kernel,
@@ -641,7 +675,7 @@
         name="bulk_first",
         cost_estimate=pl.CostEstimate(flops=40 * x.size, bytes_accessed=60 * x.size, transcendentals=0),
     )(x, base, warm, via, feeder, amps)
-    x_mid, w_mid, d_mid, inv_diag, g_diag, j_diag, edge_h, edge_v = mid
+    x_mid, w_mid, d_mid, inv_diag, g_diag, j_diag, edge_h, edge_v, own_e, own_o = mid
 
     col_args, col_specs = [], []
     for a in (x, g, inject, via):
@@ -650,13 +684,10 @@
     message = shape(rows + 2 * SUB, LANE)
     e, o = pl.pallas_call(
         pack_cols_kernel,
-        grid=(1,),
-        in_specs=col_specs + [full(warm), full(row_e), full(row_o)],
-        out_specs=(full(message), full(message)),
         out_shape=(message, message),
         compiler_params=params,
         name="pack_cols",
-    )(*col_args, warm, row_e, row_o)
+    )(row_e, row_o, own_e, own_o, warm)
     col_e, col_o = swap(e, o, col_swaps)
 
     def strip_scratch(height, width):
@@ -671,7 +702,7 @@
     for a in (x, g, inject, via):
         deep_args += [a, a]
         deep_specs += [edge_deep(a, 0), edge_deep(a, rows // (2 * SUB) - 1)]
-    edge_x, edge_h2 = shape(layers, 2 * SUB, cols), shape(layers, SUB, cells)
+    edge_x, edge_h2 = shape(layers, 4 * SUB, cols), shape(layers, SUB, cells)
     strip = shape(4 * layers - 1, rows + 2 * SUB, LANE)
     x_rows, heat_strip, strip = pl.pallas_call(
         row_strip_kernel,
@@ -695,9 +726,10 @@
     heat_row_e, heat_row_o = swap(heat_edge, heat_edge, row_swaps)
 
     assert SWEEPS == 3
-    x_next, w_next, d_next = pl.pallas_call(
+    x_done = pl.pallas_call(
         bulk_mid_kernel,
-        out_shape=(shape(layers, rows, cols),) * 3,
+        out_shape=shape(layers, rows, cols),
+        scratch_shapes=[node_scratch] * 3,
         compiler_params=params,
         name="bulk_mid",
         cost_estimate=pl.CostEstimate(flops=20 * x.size, bytes_accessed=20 * x.size, transcendentals=0),
@@ -710,7 +742,7 @@
         out_shape=(message, message),
         compiler_params=params,
         name="pack_heat",
-    )(heat_cols, heat_row_e, heat_row_o, x_next)
+    )(heat_cols, heat_row_e, heat_row_o, x_done)
     heat_col_e, heat_col_o = swap(e, o, col_swaps)
 
     tall = pltpu.VMEM((layers, cols // LANE, rows + SUB, LANE), f32)
@@ -718,11 +750,11 @@
         bulk_last_kernel,
         out_shape=(shape(layers, rows, cols), shape(layers, cell_rows, cells)),
         out_specs=(pl.BlockSpec(memory_space=pl.ANY), pl.BlockSpec(memory_space=pltpu.VMEM)),
-        scratch_shapes=[node_scratch] + [tall] * 3 + [node_scratch, pltpu.SemaphoreType.DMA],
+        scratch_shapes=[tall] * 3 + [node_scratch, pltpu.SemaphoreType.DMA],
         compiler_params=params,
         name="bulk_last",
         cost_estimate=pl.CostEstimate(flops=40 * x.size, bytes_accessed=60 * x.size, transcendentals=0),
-    )(x_next, via, w_next, d_next, inv_diag, g_diag, j_diag, edge_h, edge_v, x_rows, x_cols)
+    )(x_done, via, edge_h, edge_v, x_rows, x_cols)
 
     warmth = pl.pallas_call(
         warm_kernel,

time: 29.6 us -> 28.1 us (0.949)
  Pallas kernels: 17.1 us -> 16.1 us
  starting transfers between devices: 10.3 us -> 9.82 us
    pallas_call x1, Pallas kernels: 3.13 us -> 1.76 us  [on_device(): pl.pallas_call(bulk_last_kernel, out_shape=(shape(layers, rows, cols), sh...]
    ppermute x8, starting transfers between devices: 10.3 us -> 9.82 us  [swap(): lax.ppermute(m, BOTH, tables(mesh_rows, mesh_cols, first))]
    pallas_call x2, Pallas kernels: 1.94 us -> 2.43 us  [the longest x1 2.27 us: on_device(): pl.pallas_call(bulk_mid_kernel, out_shape=shape(layers, rows, cols), scra...]
where the time goes in v3:
time: 28.1 us; the launch traced here: 28 us
  Pallas kernels  16.1 us (57%)
  starting transfers between devices  9.82 us (35%)
  waiting for transfers between devices  1.21 us (4%)
  between operations  0.79 us (3%)
    ppermute x8, starting transfers between devices, swap(): lax.ppermute(m, BOTH, tables(mesh_rows, mesh_cols, first))  9.82 us
    pallas_call x1, Pallas kernels, on_device(): pl.pallas_call(bulk_first_kernel, out_shape=fields, scratch_shapes=[node_...  3.65 us
    pallas_call x1, Pallas kernels, on_device(): pl.pallas_call(bulk_mid_kernel, out_shape=shape(layers, rows, cols), scra...  2.27 us
    pallas_call x1, Pallas kernels, on_device(): pl.pallas_call(pack_rows_kernel, grid=(1,), in_specs=row_specs, out_specs...  2.25 us
    pallas_call x1, Pallas kernels, on_device(): pl.pallas_call(col_strip_kernel, out_shape=(shape(layers, rows, LANE), sh...  2.17 us
    pallas_call x1, Pallas kernels, on_device(): pl.pallas_call(row_strip_kernel, grid=(1,), in_specs=deep_specs + col_spe...  2.13 us
    pallas_call x1, Pallas kernels, on_device(): pl.pallas_call(bulk_last_kernel, out_shape=(shape(layers, rows, cols), sh...  1.76 us
    pallas_call x1, Pallas kernels, on_device(): pl.pallas_call(warm_kernel, out_shape=shape(layers, cell_rows, cells), co...  1.62 us
  transfers between devices with their start and end apart: 8, of which 2 were waited for; matrix products, arithmetic and copies ran while one was open for 0% of the time, Pallas kernels for 35%

profile of v3, /device:TPU:0, one launch (start us, length us, event | category | flops | bytes accessed | tf_op | source)
XLA Modules:
  0.0 28.0 jit_solution(8188795384910091619)
XLA Ops:
  0.6 0.0 copy-start.1
  0.6 0.0 copy-start.2
  0.7 0.0 copy-start.5
  0.7 0.0 copy-start
  0.7 0.0 copy-start.3
  0.7 0.0 copy-start.4
  0.7 2.3 %pack_rows.1 = (f32[8,8,512]{2,1,0:T(8,128)}, f32[8,8,512]{2,1,0:T(8,128)}) custom-call(f32[4,128,512]{2,1,0:T(8,128)} %x_r.1, f32[4,128,512]{2,1,0:T(8,128)} %x_r.1, f32[4,128,512]{2,1,0:T(8,128)} %b_b.1, f32[4,128,512]{2,1,0:T(8,128)} %b_b.1, f32[4,32,128]{2,1,0:T(8,128)} %w_ref.5, f32[4,32,128]{2,1,0:T(8,128)} %w_ref.5, s32[3,128,512]{2,1,0:T(8,128)} %V.3, ...), custom_call_target="tpu_custom_call" | custom-call | tf_op jit(solution)/shard_map/pack_rows/pallas_call | solution.py:657
  2.9 0.5 %collective-permute-start = (f32[8,8,512]{2,1,0:T(8,128)}, f32[8,8,512]{2,1,0:T(8,128)S(1)}, u32[]{:S(2)}, u32[]{:S(2)}) collective-permute-start(f32[8,8,512]{2,1,0:T(8,128)} %get-tuple-element.38), channel_id=1, source_target_pairs={{0,4},{1,5},{2,6},{3,7},{4,0},{5,1},{6,2},{7,3},{8,12},{9,13},{10,... | collective-permute-start | bytes 393224 | tf_op jit(solution)/shard_map/ppermute | solution.py:647
  3.4 2.6 %collective-permute-start.1 = (f32[8,8,512]{2,1,0:T(8,128)}, f32[8,8,512]{2,1,0:T(8,128)S(1)}, u32[]{:S(2)}, u32[]{:S(2)}) collective-permute-start(f32[8,8,512]{2,1,0:T(8,128)} %get-tuple-element.39), channel_id=1, source_target_pairs={{0,1},{1,0},{2,3},{3,2},{4,8},{5,9},{6,10},{7,11},{8,4},{9,5},{10,... | collective-permute-start | bytes 393224 | tf_op jit(solution)/shard_map/ppermute | solution.py:647
  6.0 0.0 copy-done.1
  6.0 0.0 copy-done.2
  6.0 0.0 copy-done.5
  6.0 0.0 copy-done
  6.0 0.0 copy-done.3
  6.0 0.0 copy-done.4
  6.1 3.6 %bulk_first.1 = (f32[4,128,512]{2,1,0:T(8,128)S(1)}, f32[4,128,512]{2,1,0:T(8,128)S(1)}, f32[4,128,512]{2,1,0:T(8,128)S(1)}, f32[4,128,512]{2,1,0:T(8,128)S(1)},...) custom-call(f32[4,128,512]{2,1,0:T(8,128)S(1)} %copy-done.1, ...), custom_call_target="tpu_custom_call" | custom-call | flops 10485760 | bytes 15728640 | tf_op jit(solution)/shard_map/bulk_first/pallas_call | solution.py:670
  9.7 0.0 collective-permute-done.re_ref
  9.7 0.0 collective-permute-done.1.ro_ref
  9.7 0.2 pack_cols.1
  9.9 1.5 %collective-permute-start.2 = (f32[144,128]{1,0:T(8,128)S(1)}, f32[144,128]{1,0:T(8,128)S(1)}, u32[]{:S(2)}, u32[]{:S(2)}) collective-permute-start(f32[144,128]{1,0:T(8,128)S(1)} %get-tuple-element.44), channel_id=1, source_target_pairs={{0,1},{1,0},{2,3},{3,2},{4,5},{5,4},{6,7},{7,6},{8,9},{9,8},{10,11... | collective-permute-start | bytes 221192 | tf_op jit(solution)/shard_map/ppermute | solution.py:647
  11.4 0.7 %collective-permute-start.3 = (f32[144,128]{1,0:T(8,128)S(1)}, f32[144,128]{1,0:T(8,128)S(1)}, u32[]{:S(2)}, u32[]{:S(2)}) collective-permute-start(f32[144,128]{1,0:T(8,128)S(1)} %get-tuple-element.45), channel_id=1, source_target_pairs={{0,4},{1,2},{2,1},{3,7},{4,0},{5,6},{6,5},{7,3},{8,12},{9,10},{10,... | collective-permute-start | bytes 221192 | tf_op jit(solution)/shard_map/ppermute | solution.py:647
  12.1 2.1 %row_strip.1 = (f32[4,32,512]{2,1,0:T(8,128)S(1)}, f32[4,8,128]{2,1,0:T(8,128)S(1)}, f32[15,144,128]{2,1,0:T(8,128)S(1)}) custom-call(f32[4,128,512]{2,1,0:T(8,128)S(1)} %copy-done.1, f32[4,128,512]{2,1,0:T(8,128)S(1)} %copy-done.1, f32[4,128,512]{2,1,0:T(8,128)S(1)} %get-tuple-element.34.G.g_t.g_b.g_l.g_r, ...), custom_call_target="tpu_custom_call" | custom-call | flops 10485760 | bytes 5242880 | tf_op jit(solution)/shard_map/row_strip/pallas_call | solution.py:707
  14.2 0.6 %collective-permute-done.2.ce_ref = f32[144,128]{1,0:T(8,128)S(1)} collective-permute-done((f32[144,128]{1,0:T(8,128)S(1)}, f32[144,128]{1,0:T(8,128)S(1)}, u32[]{:S(2)}, u32[]{:S(2)}) %collective-permute-start.2) | collective-permute-done | bytes 73760 | tf_op jit(solution)/shard_map/ppermute | solution.py:647
  14.8 0.0 collective-permute-done.3.co_ref
  14.8 2.2 %col_strip.1 = (f32[4,128,128]{2,1,0:T(8,128)S(1)}, f32[4,32,128]{2,1,0:T(8,128)S(1)}, f32[4,8,128]{2,1,0:T(8,128)S(1)}) custom-call(f32[15,144,128]{2,1,0:T(8,128)S(1)} %get-tuple-element.41.strip_ref, f32[144,128]{1,0:T(8,128)S(1)} %collective-permute-done.2.ce_ref, f32[144,128]{1,0:T(8,128)S(1)} %collective-permute-done.3.co_ref, ...), custom_call_target="tpu_custom_call" | custom-call | tf_op jit(solution)/shard_map/col_strip/pallas_call | solution.py:719
  17.0 0.1 collective-permute-start.4
  17.1 3.0 %collective-permute-start.5 = (f32[4,8,128]{2,1,0:T(8,128)S(1)}, f32[4,8,128]{2,1,0:T(8,128)S(1)}, u32[]{:S(2)}, u32[]{:S(2)}) collective-permute-start(f32[4,8,128]{2,1,0:T(8,128)S(1)} %get-tuple-element.50.hm_ref), channel_id=1, source_target_pairs={{0,1},{1,0},{2,3},{3,2},{4,8},{5,9},{6,10},{7,11},{8,4},{9,5},{10,... | collective-permute-start | bytes 49160 | tf_op jit(solution)/shard_map/ppermute | solution.py:647
  20.0 2.3 %bulk_mid.1.XN._ = f32[4,128,512]{2,1,0:T(8,128)S(1)} custom-call(f32[4,128,512]{2,1,0:T(8,128)S(1)} %get-tuple-element.28.X, s32[3,128,512]{2,1,0:T(8,128)S(1)} %copy-done, f32[4,128,512]{2,1,0:T(8,128)S(1)} %get-tuple-element.29.W, f32[4,128,512]{2,1,0:T(8,128)S(1)} %get-tuple-element.30.D, f32[4,128,512]{2,1,0:T(8,128)S(1)} %get-tuple-element.31.DI, ...), custom_call_target="tpu_custom_call" | custom-call | flops 5242880 | bytes 5242880 | tf_op jit(solution)/shard_map/bulk_mid/pallas_call | solution.py:729
  22.3 0.0 collective-permute-done.4.re_ref.hre_ref
  22.3 0.0 collective-permute-done.5.ro_ref.hro_ref
  22.3 0.1 pack_heat.1
  22.5 1.5 %collective-permute-start.6 = (f32[48,128]{1,0:T(8,128)S(1)}, f32[48,128]{1,0:T(8,128)S(1)}, u32[]{:S(2)}, u32[]{:S(2)}) collective-permute-start(f32[48,128]{1,0:T(8,128)S(1)} %get-tuple-element.52), channel_id=1, source_target_pairs={{0,1},{1,0},{2,3},{3,2},{4,5},{5,4},{6,7},{7,6},{8,9},{9,8},{10,11... | collective-permute-start | bytes 73736 | tf_op jit(solution)/shard_map/ppermute | solution.py:647
  24.0 0.0 collective-permute-start.7
  24.0 1.8 %bulk_last.1 = (f32[4,128,512]{2,1,0:T(8,128)}, f32[4,32,128]{2,1,0:T(8,128)S(1)}) custom-call(f32[4,128,512]{2,1,0:T(8,128)S(1)} %bulk_mid.1.XN._, s32[3,128,512]{2,1,0:T(8,128)S(1)} %copy-done, f32[4,128,512]{2,1,0:T(8,128)S(1)} %get-tuple-element.35.EH, f32[4,128,512]{2,1,0:T(8,128)S(1)} %get-tuple-element.36.EV, ...), custom_call_target="tpu_custom_call" | custom-call | flops 10485760 | bytes 15728640 | tf_op jit(solution)/shard_map/bulk_last/pallas_call | solution.py:749
  25.7 0.6 %collective-permute-done.6.hce_ref = f32[48,128]{1,0:T(8,128)S(1)} collective-permute-done((f32[48,128]{1,0:T(8,128)S(1)}, f32[48,128]{1,0:T(8,128)S(1)}, u32[]{:S(2)}, u32[]{:S(2)}) %collective-permute-start.6) | collective-permute-done | bytes 24608 | tf_op jit(solution)/shard_map/ppermute | solution.py:647
  26.4 0.0 collective-permute-done.7.hco_ref
  26.4 1.6 %warm.1 = f32[4,32,128]{2,1,0:T(8,128)} custom-call(f32[4,32,128]{2,1,0:T(8,128)S(1)} %copy-done.5, f32[4,32,128]{2,1,0:T(8,128)S(1)} %get-tuple-element.49.h_ref, f32[4,8,128]{2,1,0:T(8,128)S(1)} %get-tuple-element.50.hm_ref, f32[4,32,128]{2,1,0:T(8,128)S(1)} %get-tuple-element.51.h_ref.hc_ref, f32[8,8,512]{2,1,0:T(8,128)S(1)} %collective-permute-done.re_ref, ...), custom_call_target="tpu_custom_call" | custom-call | tf_op jit(solution)/shard_map/warm/pallas_call | solution.py:759
Async XLA Ops:
  0.6 5.4 %copy-start.1 = (f32[4,128,512]{2,1,0:T(8,128)S(1)}, f32[4,128,512]{2,1,0:T(8,128)}, u32[]{:S(2)}) copy-start(f32[4,128,512]{2,1,0:T(8,128)} %x_r.1) | copy-start | bytes 3145732
  0.6 5.4 %copy-start.2 = (f32[4,128,512]{2,1,0:T(8,128)S(1)}, f32[4,128,512]{2,1,0:T(8,128)}, u32[]{:S(2)}) copy-start(f32[4,128,512]{2,1,0:T(8,128)} %b_b.1) | copy-start | bytes 3145732
  0.7 5.4 %copy-start.5 = (f32[4,32,128]{2,1,0:T(8,128)S(1)}, f32[4,32,128]{2,1,0:T(8,128)}, u32[]{:S(2)}) copy-start(f32[4,32,128]{2,1,0:T(8,128)} %w_ref.5) | copy-start | bytes 196612
  0.7 5.4 %copy-start = (s32[3,128,512]{2,1,0:T(8,128)S(1)}, s32[3,128,512]{2,1,0:T(8,128)}, u32[]{:S(2)}) copy-start(s32[3,128,512]{2,1,0:T(8,128)} %V.3) | copy-start | bytes 2359300
  0.7 5.4 %copy-start.3 = (s32[4,128,512]{2,1,0:T(8,128)S(1)}, s32[4,128,512]{2,1,0:T(8,128)}, u32[]{:S(2)}) copy-start(s32[4,128,512]{2,1,0:T(8,128)} %f_b.1) | copy-start | bytes 3145732
  0.7 5.4 %copy-start.4 = (f32[4,128,512]{2,1,0:T(8,128)S(1)}, f32[4,128,512]{2,1,0:T(8,128)}, u32[]{:S(2)}) copy-start(f32[4,128,512]{2,1,0:T(8,128)} %a_b.1) | copy-start | bytes 3145732
  2.9 6.8 %collective-permute-start = (f32[8,8,512]{2,1,0:T(8,128)}, f32[8,8,512]{2,1,0:T(8,128)S(1)}, u32[]{:S(2)}, u32[]{:S(2)}) collective-permute-start(f32[8,8,512]{2,1,0:T(8,128)} %get-tuple-element.38), channel_id=1, source_target_pairs={{0,4},{1,5},{2,6},{3,7},{4,0},{5,1},{6,2},{7,3},{8,12},{9,13},{10,... | collective-permute-start | bytes 393224 | tf_op jit(solution)/shard_map/ppermute | solution.py:647
  3.4 6.3 %collective-permute-start.1 = (f32[8,8,512]{2,1,0:T(8,128)}, f32[8,8,512]{2,1,0:T(8,128)S(1)}, u32[]{:S(2)}, u32[]{:S(2)}) collective-permute-start(f32[8,8,512]{2,1,0:T(8,128)} %get-tuple-element.39), channel_id=1, source_target_pairs={{0,1},{1,0},{2,3},{3,2},{4,8},{5,9},{6,10},{7,11},{8,4},{9,5},{10,... | collective-permute-start | bytes 393224 | tf_op jit(solution)/shard_map/ppermute | solution.py:647
  9.9 4.9 %collective-permute-start.2 = (f32[144,128]{1,0:T(8,128)S(1)}, f32[144,128]{1,0:T(8,128)S(1)}, u32[]{:S(2)}, u32[]{:S(2)}) collective-permute-start(f32[144,128]{1,0:T(8,128)S(1)} %get-tuple-element.44), channel_id=1, source_target_pairs={{0,1},{1,0},{2,3},{3,2},{4,5},{5,4},{6,7},{7,6},{8,9},{9,8},{10,11... | collective-permute-start | bytes 221192 | tf_op jit(solution)/shard_map/ppermute | solution.py:647
  11.4 3.4 %collective-permute-start.3 = (f32[144,128]{1,0:T(8,128)S(1)}, f32[144,128]{1,0:T(8,128)S(1)}, u32[]{:S(2)}, u32[]{:S(2)}) collective-permute-start(f32[144,128]{1,0:T(8,128)S(1)} %get-tuple-element.45), channel_id=1, source_target_pairs={{0,4},{1,2},{2,1},{3,7},{4,0},{5,6},{6,5},{7,3},{8,12},{9,10},{10,... | collective-permute-start | bytes 221192 | tf_op jit(solution)/shard_map/ppermute | solution.py:647
  17.0 5.3 %collective-permute-start.4 = (f32[4,8,128]{2,1,0:T(8,128)S(1)}, f32[4,8,128]{2,1,0:T(8,128)S(1)}, u32[]{:S(2)}, u32[]{:S(2)}) collective-permute-start(f32[4,8,128]{2,1,0:T(8,128)S(1)} %get-tuple-element.50.hm_ref), channel_id=1, source_target_pairs={{0,4},{1,5},{2,6},{3,7},{4,0},{5,1},{6,2},{7,3},{8,12},{9,13},{10,... | collective-permute-start | bytes 49160 | tf_op jit(solution)/shard_map/ppermute | solution.py:647
  17.1 5.3 %collective-permute-start.5 = (f32[4,8,128]{2,1,0:T(8,128)S(1)}, f32[4,8,128]{2,1,0:T(8,128)S(1)}, u32[]{:S(2)}, u32[]{:S(2)}) collective-permute-start(f32[4,8,128]{2,1,0:T(8,128)S(1)} %get-tuple-element.50.hm_ref), channel_id=1, source_target_pairs={{0,1},{1,0},{2,3},{3,2},{4,8},{5,9},{6,10},{7,11},{8,4},{9,5},{10,... | collective-permute-start | bytes 49160 | tf_op jit(solution)/shard_map/ppermute | solution.py:647
  22.5 3.9 %collective-permute-start.6 = (f32[48,128]{1,0:T(8,128)S(1)}, f32[48,128]{1,0:T(8,128)S(1)}, u32[]{:S(2)}, u32[]{:S(2)}) collective-permute-start(f32[48,128]{1,0:T(8,128)S(1)} %get-tuple-element.52), channel_id=1, source_target_pairs={{0,1},{1,0},{2,3},{3,2},{4,5},{5,4},{6,7},{7,6},{8,9},{9,8},{10,11... | collective-permute-start | bytes 73736 | tf_op jit(solution)/shard_map/ppermute | solution.py:647
  24.0 2.4 %collective-permute-start.7 = (f32[48,128]{1,0:T(8,128)S(1)}, f32[48,128]{1,0:T(8,128)S(1)}, u32[]{:S(2)}, u32[]{:S(2)}) collective-permute-start(f32[48,128]{1,0:T(8,128)S(1)} %get-tuple-element.53), channel_id=1, source_target_pairs={{0,4},{1,2},{2,1},{3,7},{4,0},{5,6},{6,5},{7,3},{8,12},{9,10},{10,... | collective-permute-start | bytes 73736 | tf_op jit(solution)/shard_map/ppermute | solution.py:647

commit v4 on v3

--- a/solution.py
+++ b/solution.py
@@ -472,7 +472,8 @@
     half = 2 * layers
     height = 2 * (SUB + deep)
     plane = 0
-    lane = iota((rows + 2 * SUB, LANE), 1)
+    tall = strip_ref.shape[1]
+    lane = iota((tall, LANE), 1)
     for top_ref, bot_ref, left_ref, right_ref, pad in (
         (x_t, x_b, x_l, x_r, X), (g_t, g_b, g_l, g_r, G), (j_t, j_b, j_l, j_r, J), (v_t, v_b, v_l, v_r, V),
     ):
@@ -486,7 +487,15 @@
             right = jnp.concatenate(
                 [top[:, cols - LANE :], right_ref[l].astype(jnp.float32), bot[:, cols - LANE :]], 0
             )
-            strip_ref[plane] = jnp.where(lane < LANE // 4, left, pltpu.roll(right, LANE // 2, 1))
+            strip_ref[plane] = jnp.where(
+                lane < LANE // 2,
+                jnp.where(lane < LANE // 4, left[:tall], pltpu.roll(right[:tall], 48, 1)),
+                jnp.where(
+                    lane < 3 * LANE // 4,
+                    pltpu.roll(left[rows + 2 * SUB - tall :], 64, 1),
+                    pltpu.roll(right[rows + 2 * SUB - tall :], 112, 1),
+                ),
+            )
             plane += 1
     first_sweep(6, 0, X, G, J, V, W0, XN, WN, D, DI, GD, JD, EH, EV)
     later_sweeps(6, XN, V, WN, D, DI, GD, JD, G, W0, XL, DN)
@@ -505,38 +514,50 @@
 ):
     layers, rows, _ = xc_ref.shape
     cell_rows, cells = hc_ref.shape[1:]
-    height = rows + 2 * SUB
-    mixed = col_margin(ce_ref[...], co_ref[...], False, LANE // 2 + REACH)
-    lane = iota((height, LANE), 1)
-    from_right = (lane >= LANE // 2) & (lane < LANE // 2 + REACH)
-    margin = from_right | (lane >= LANE - REACH)
+    tall = strip_ref.shape[1]
+    mixed = col_margin(ce_ref[...], co_ref[...], False, 52)
+    upper, lower = mixed[:tall], mixed[rows + 2 * SUB - tall :]
+    lane = iota((tall, LANE), 1)
+    in_upper = ((lane >= 48) & (lane < 48 + REACH)) | (lane >= LANE - REACH)
+    in_lower = ((lane >= 112) & (lane < 112 + REACH)) | ((lane >= 64 - REACH) & (lane < 64))
     plane = 0
     for pad in (X, G, J, V):
         for l in range(pad.shape[0]):
-            shift = (LANE // 2 - 8 * plane) % LANE
-            value = pltpu.roll(mixed, shift, 1) if shift else mixed
-            pad[l] = jnp.where(margin, value, strip_ref[plane])
+            shift = (48 - 8 * plane) % LANE
+            value = pltpu.roll(upper, shift, 1) if shift else upper
+            shift = (112 - 8 * plane) % LANE
+            other = pltpu.roll(lower, shift, 1) if shift else lower
+            value = jnp.where(in_upper, value, strip_ref[plane])
+            pad[l] = jnp.where(in_lower, other, value)
             plane += 1
-    groups = height // SUB
-    first_sweep(9, 0, X, G, J, V, W0, XN, WN, D, DI, GD, JD, EH, EV)
-    later_sweeps(9, XN, V, WN, D, DI, GD, JD, G, W0, XL, DN)
-    power_rows(0, groups - 1, 17, XL, V, EH, EV, PA, PB, PD)
+    groups = tall // SUB
+    first_sweep(groups, 0, X, G, J, V, W0, XN, WN, D, DI, GD, JD, EH, EV)
+    later_sweeps(groups, XN, V, WN, D, DI, GD, JD, G, W0, XL, DN)
+    power_rows(0, groups - 1, groups, XL, V, EH, EV, PA, PB, PD)
     n, c = iota((LANE, cells), 0), iota((LANE, cells), 1)
-    near = lax.shift_right_logical(n, 2) == jnp.where(c < cells // 2, c, c - cells + LANE // 8)
-    before_it = n == (REFINE * jnp.where(c < cells // 2, c, c - cells + LANE // 8) - 1) % LANE
     at_edge = (c < REACH) | (c >= cells - REACH)
-    heat = fold_power(
-        SUB, cell_rows, PA, PB, PD,
-        (near & at_edge).astype(jnp.float32), (before_it & at_edge).astype(jnp.float32),
-    )
-    lane = iota((rows, LANE), 1)
+    halves = []
+    for part in range(2):
+        slot = jnp.where(c < cells // 2, c, c - cells + 12) + 16 * part
+        same = at_edge & (lax.shift_right_logical(n, 2) == slot)
+        left = at_edge & (n == jnp.where(slot == 0, LANE - 1, REFINE * slot - 1))
+        halves.append(
+            fold_power(
+                SUB, cell_rows // 2, PA, PB, PD, same.astype(jnp.float32), left.astype(jnp.float32)
+            )
+        )
+    lane = iota((rows // 2, LANE), 1)
     cell = iota((SUB, cells), 1)
     edge = (cell < REACH - 1) | (cell > cells - REACH)
+    low = lane < LANE // 2
     for l in range(layers):
-        hc_ref[l] = heat[l]
-        x = XL[l, SUB : SUB + rows, :]
-        xc_ref[l] = jnp.where(lane < LANE // 2, x, pltpu.roll(x, LANE // 2, 1))
-        own = jnp.concatenate([heat[l][:REACH], heat[l][cell_rows - REACH :]], 0)
+        first, final = halves[0][l], halves[1][l]
+        hc_ref[l, 0 : cell_rows // 2, :] = first
+        hc_ref[l, cell_rows // 2 : cell_rows, :] = final
+        x = XL[l, SUB : SUB + rows // 2, :]
+        xc_ref[l, 0 : rows // 2, :] = jnp.where(low, x, pltpu.roll(x, 80, 1))
+        xc_ref[l, rows // 2 : rows, :] = jnp.where(low, pltpu.roll(x, 64, 1), pltpu.roll(x, 16, 1))
+        own = jnp.concatenate([first[:REACH], final[cell_rows // 2 - REACH :]], 0)
         hm_ref[l] = jnp.where(edge, own, hr_ref[l])
 
 
@@ -703,7 +724,7 @@
         deep_args += [a, a]
         deep_specs += [edge_deep(a, 0), edge_deep(a, rows // (2 * SUB) - 1)]
     edge_x, edge_h2 = shape(layers, 4 * SUB, cols), shape(layers, SUB, cells)
-    strip = shape(4 * layers - 1, rows + 2 * SUB, LANE)
+    strip = shape(4 * layers - 1, rows // 2 + 2 * SUB, LANE)
     x_rows, heat_strip, strip = pl.pallas_call(
         row_strip_kernel,
         grid=(1,),
@@ -719,7 +740,7 @@
     x_cols, heat_cols, heat_edge = pl.pallas_call(
         col_strip_kernel,
         out_shape=(shape(layers, rows, LANE), shape(layers, cell_rows, cells), edge_h2),
-        scratch_shapes=strip_scratch(rows + 2 * SUB, LANE),
+        scratch_shapes=strip_scratch(rows // 2 + 2 * SUB, LANE),
         compiler_params=params,
         name="col_strip",
     )(strip, col_e, col_o, heat_strip)

time: 28.1 us -> 27.2 us (0.968)
  Pallas kernels: 16.1 us -> 15.4 us
    pallas_call x1, Pallas kernels: 2.17 us -> 1.27 us  [on_device(): pl.pallas_call(col_strip_kernel, out_shape=(shape(layers, rows, LANE), sh...]
  transfers between devices with their start and end apart: 8 -> 8, of which waited for: 2 -> 2; matrix products, arithmetic and copies ran while one was open for 0% -> 0% of each run, Pallas kernels for 35% -> 37%
where the time goes in v4:
time: 27.2 us; the launch traced here: 27 us
  Pallas kernels  15.4 us (57%)
  starting transfers between devices  9.89 us (36%)
  waiting for transfers between devices  0.95 us (3%)
  between operations  0.79 us (3%)
    ppermute x8, starting transfers between devices, swap(): lax.ppermute(m, BOTH, tables(mesh_rows, mesh_cols, first))  9.89 us
    pallas_call x1, Pallas kernels, on_device(): pl.pallas_call(bulk_first_kernel, out_shape=fields, scratch_shapes=[node_...  3.65 us
    pallas_call x1, Pallas kernels, on_device(): pl.pallas_call(row_strip_kernel, grid=(1,), in_specs=deep_specs + col_spe...  2.32 us
    pallas_call x1, Pallas kernels, on_device(): pl.pallas_call(pack_rows_kernel, grid=(1,), in_specs=row_specs, out_specs...  2.25 us
    pallas_call x1, Pallas kernels, on_device(): pl.pallas_call(bulk_mid_kernel, out_shape=shape(layers, rows, cols), scra...  2.21 us
    pallas_call x1, Pallas kernels, on_device(): pl.pallas_call(bulk_last_kernel, out_shape=(shape(layers, rows, cols), sh...  1.77 us
    pallas_call x1, Pallas kernels, on_device(): pl.pallas_call(warm_kernel, out_shape=shape(layers, cell_rows, cells), co...  1.62 us
    pallas_call x1, Pallas kernels, on_device(): pl.pallas_call(col_strip_kernel, out_shape=(shape(layers, rows, LANE), sh...  1.27 us
  transfers between devices with their start and end apart: 8, of which 2 were waited for; matrix products, arithmetic and copies ran while one was open for 0% of the time, Pallas kernels for 37%

profile of v4, /device:TPU:0, one launch (start us, length us, event | category | flops | bytes accessed | tf_op | source)
XLA Modules:
  0.0 27.0 jit_solution(16997711016888558062)
XLA Ops:
  0.6 0.0 copy-start.1
  0.6 0.0 copy-start.2
  0.7 0.0 copy-start.5
  0.7 0.0 copy-start
  0.7 0.0 copy-start.3
  0.7 0.0 copy-start.4
  0.7 2.3 %pack_rows.1 = (f32[8,8,512]{2,1,0:T(8,128)}, f32[8,8,512]{2,1,0:T(8,128)}) custom-call(f32[4,128,512]{2,1,0:T(8,128)} %x_r.1, f32[4,128,512]{2,1,0:T(8,128)} %x_r.1, f32[4,128,512]{2,1,0:T(8,128)} %b_b.1, f32[4,128,512]{2,1,0:T(8,128)} %b_b.1, f32[4,32,128]{2,1,0:T(8,128)} %w_ref.5, f32[4,32,128]{2,1,0:T(8,128)} %w_ref.5, s32[3,128,512]{2,1,0:T(8,128)} %V.3, ...), custom_call_target="tpu_custom_call" | custom-call | tf_op jit(solution)/shard_map/pack_rows/pallas_call | solution.py:678
  2.9 0.5 %collective-permute-start = (f32[8,8,512]{2,1,0:T(8,128)}, f32[8,8,512]{2,1,0:T(8,128)S(1)}, u32[]{:S(2)}, u32[]{:S(2)}) collective-permute-start(f32[8,8,512]{2,1,0:T(8,128)} %get-tuple-element.38), channel_id=1, source_target_pairs={{0,4},{1,5},{2,6},{3,7},{4,0},{5,1},{6,2},{7,3},{8,12},{9,13},{10,... | collective-permute-start | bytes 393224 | tf_op jit(solution)/shard_map/ppermute | solution.py:668
  3.4 2.6 %collective-permute-start.1 = (f32[8,8,512]{2,1,0:T(8,128)}, f32[8,8,512]{2,1,0:T(8,128)S(1)}, u32[]{:S(2)}, u32[]{:S(2)}) collective-permute-start(f32[8,8,512]{2,1,0:T(8,128)} %get-tuple-element.39), channel_id=1, source_target_pairs={{0,1},{1,0},{2,3},{3,2},{4,8},{5,9},{6,10},{7,11},{8,4},{9,5},{10,... | collective-permute-start | bytes 393224 | tf_op jit(solution)/shard_map/ppermute | solution.py:668
  6.0 0.0 copy-done.1
  6.0 0.0 copy-done.2
  6.0 0.0 copy-done.5
  6.0 0.0 copy-done
  6.0 0.0 copy-done.3
  6.0 0.0 copy-done.4
  6.1 3.6 %bulk_first.1 = (f32[4,128,512]{2,1,0:T(8,128)S(1)}, f32[4,128,512]{2,1,0:T(8,128)S(1)}, f32[4,128,512]{2,1,0:T(8,128)S(1)}, f32[4,128,512]{2,1,0:T(8,128)S(1)},...) custom-call(f32[4,128,512]{2,1,0:T(8,128)S(1)} %copy-done.1, ...), custom_call_target="tpu_custom_call" | custom-call | flops 10485760 | bytes 15728640 | tf_op jit(solution)/shard_map/bulk_first/pallas_call | solution.py:691
  9.7 0.0 collective-permute-done.re_ref
  9.7 0.0 collective-permute-done.1.ro_ref
  9.7 0.2 pack_cols.1
  9.9 1.5 %collective-permute-start.2 = (f32[144,128]{1,0:T(8,128)S(1)}, f32[144,128]{1,0:T(8,128)S(1)}, u32[]{:S(2)}, u32[]{:S(2)}) collective-permute-start(f32[144,128]{1,0:T(8,128)S(1)} %get-tuple-element.44), channel_id=1, source_target_pairs={{0,1},{1,0},{2,3},{3,2},{4,5},{5,4},{6,7},{7,6},{8,9},{9,8},{10,11... | collective-permute-start | bytes 221192 | tf_op jit(solution)/shard_map/ppermute | solution.py:668
  11.4 0.7 %collective-permute-start.3 = (f32[144,128]{1,0:T(8,128)S(1)}, f32[144,128]{1,0:T(8,128)S(1)}, u32[]{:S(2)}, u32[]{:S(2)}) collective-permute-start(f32[144,128]{1,0:T(8,128)S(1)} %get-tuple-element.45), channel_id=1, source_target_pairs={{0,4},{1,2},{2,1},{3,7},{4,0},{5,6},{6,5},{7,3},{8,12},{9,10},{10,... | collective-permute-start | bytes 221192 | tf_op jit(solution)/shard_map/ppermute | solution.py:668
  12.1 2.3 %row_strip.1 = (f32[4,32,512]{2,1,0:T(8,128)S(1)}, f32[4,8,128]{2,1,0:T(8,128)S(1)}, f32[15,80,128]{2,1,0:T(8,128)S(1)}) custom-call(f32[4,128,512]{2,1,0:T(8,128)S(1)} %copy-done.1, f32[4,128,512]{2,1,0:T(8,128)S(1)} %copy-done.1, f32[4,128,512]{2,1,0:T(8,128)S(1)} %get-tuple-element.34.G.g_t.g_b.g_l.g_r, ...), custom_call_target="tpu_custom_call" | custom-call | flops 10485760 | bytes 5242880 | tf_op jit(solution)/shard_map/row_strip/pallas_call | solution.py:728
  14.4 0.4 %collective-permute-done.2.ce_ref = f32[144,128]{1,0:T(8,128)S(1)} collective-permute-done((f32[144,128]{1,0:T(8,128)S(1)}, f32[144,128]{1,0:T(8,128)S(1)}, u32[]{:S(2)}, u32[]{:S(2)}) %collective-permute-start.2) | collective-permute-done | bytes 73760 | tf_op jit(solution)/shard_map/ppermute | solution.py:668
  14.8 0.0 collective-permute-done.3.co_ref
  14.8 1.3 %col_strip.1 = (f32[4,128,128]{2,1,0:T(8,128)S(1)}, f32[4,32,128]{2,1,0:T(8,128)S(1)}, f32[4,8,128]{2,1,0:T(8,128)S(1)}) custom-call(f32[15,80,128]{2,1,0:T(8,128)S(1)} %get-tuple-element.41.strip_ref, f32[144,128]{1,0:T(8,128)S(1)} %collective-permute-done.2.ce_ref, f32[144,128]{1,0:T(8,128)S(1)} %collective-permute-done.3.co_ref, ...), custom_call_target="tpu_custom_call" | custom-call | tf_op jit(solution)/shard_map/col_strip/pallas_call | solution.py:740
  16.1 0.1 collective-permute-start.4
  16.2 3.0 %collective-permute-start.5 = (f32[4,8,128]{2,1,0:T(8,128)S(1)}, f32[4,8,128]{2,1,0:T(8,128)S(1)}, u32[]{:S(2)}, u32[]{:S(2)}) collective-permute-start(f32[4,8,128]{2,1,0:T(8,128)S(1)} %get-tuple-element.50.hm_ref), channel_id=1, source_target_pairs={{0,1},{1,0},{2,3},{3,2},{4,8},{5,9},{6,10},{7,11},{8,4},{9,5},{10,... | collective-permute-start | bytes 49160 | tf_op jit(solution)/shard_map/ppermute | solution.py:668
  19.1 2.2 %bulk_mid.1.XN._ = f32[4,128,512]{2,1,0:T(8,128)S(1)} custom-call(f32[4,128,512]{2,1,0:T(8,128)S(1)} %get-tuple-element.28.X, s32[3,128,512]{2,1,0:T(8,128)S(1)} %copy-done, f32[4,128,512]{2,1,0:T(8,128)S(1)} %get-tuple-element.29.W, f32[4,128,512]{2,1,0:T(8,128)S(1)} %get-tuple-element.30.D, f32[4,128,512]{2,1,0:T(8,128)S(1)} %get-tuple-element.31.DI, ...), custom_call_target="tpu_custom_call" | custom-call | flops 5242880 | bytes 5242880 | tf_op jit(solution)/shard_map/bulk_mid/pallas_call | solution.py:750
  21.4 0.0 collective-permute-done.4.re_ref.hre_ref
  21.4 0.0 collective-permute-done.5.ro_ref.hro_ref
  21.4 0.1 pack_heat.1
  21.5 1.6 %collective-permute-start.6 = (f32[48,128]{1,0:T(8,128)S(1)}, f32[48,128]{1,0:T(8,128)S(1)}, u32[]{:S(2)}, u32[]{:S(2)}) collective-permute-start(f32[48,128]{1,0:T(8,128)S(1)} %get-tuple-element.52), channel_id=1, source_target_pairs={{0,1},{1,0},{2,3},{3,2},{4,5},{5,4},{6,7},{7,6},{8,9},{9,8},{10,11... | collective-permute-start | bytes 73736 | tf_op jit(solution)/shard_map/ppermute | solution.py:668
  23.1 0.0 collective-permute-start.7
  23.1 1.8 %bulk_last.1 = (f32[4,128,512]{2,1,0:T(8,128)}, f32[4,32,128]{2,1,0:T(8,128)S(1)}) custom-call(f32[4,128,512]{2,1,0:T(8,128)S(1)} %bulk_mid.1.XN._, s32[3,128,512]{2,1,0:T(8,128)S(1)} %copy-done, f32[4,128,512]{2,1,0:T(8,128)S(1)} %get-tuple-element.35.EH, f32[4,128,512]{2,1,0:T(8,128)S(1)} %get-tuple-element.36.EV, ...), custom_call_target="tpu_custom_call" | custom-call | flops 10485760 | bytes 15728640 | tf_op jit(solution)/shard_map/bulk_last/pallas_call | solution.py:770
  24.8 0.5 %collective-permute-done.6.hce_ref = f32[48,128]{1,0:T(8,128)S(1)} collective-permute-done((f32[48,128]{1,0:T(8,128)S(1)}, f32[48,128]{1,0:T(8,128)S(1)}, u32[]{:S(2)}, u32[]{:S(2)}) %collective-permute-start.6) | collective-permute-done | bytes 24608 | tf_op jit(solution)/shard_map/ppermute | solution.py:668
  25.4 0.0 collective-permute-done.7.hco_ref
  25.4 1.6 %warm.1 = f32[4,32,128]{2,1,0:T(8,128)} custom-call(f32[4,32,128]{2,1,0:T(8,128)S(1)} %copy-done.5, f32[4,32,128]{2,1,0:T(8,128)S(1)} %get-tuple-element.49.h_ref, f32[4,8,128]{2,1,0:T(8,128)S(1)} %get-tuple-element.50.hm_ref, f32[4,32,128]{2,1,0:T(8,128)S(1)} %get-tuple-element.51.h_ref.hc_ref, f32[8,8,512]{2,1,0:T(8,128)S(1)} %collective-permute-done.re_ref, ...), custom_call_target="tpu_custom_call" | custom-call | tf_op jit(solution)/shard_map/warm/pallas_call | solution.py:780
Async XLA Ops:
  0.6 5.4 %copy-start.1 = (f32[4,128,512]{2,1,0:T(8,128)S(1)}, f32[4,128,512]{2,1,0:T(8,128)}, u32[]{:S(2)}) copy-start(f32[4,128,512]{2,1,0:T(8,128)} %x_r.1) | copy-start | bytes 3145732
  0.6 5.4 %copy-start.2 = (f32[4,128,512]{2,1,0:T(8,128)S(1)}, f32[4,128,512]{2,1,0:T(8,128)}, u32[]{:S(2)}) copy-start(f32[4,128,512]{2,1,0:T(8,128)} %b_b.1) | copy-start | bytes 3145732
  0.7 5.4 %copy-start.5 = (f32[4,32,128]{2,1,0:T(8,128)S(1)}, f32[4,32,128]{2,1,0:T(8,128)}, u32[]{:S(2)}) copy-start(f32[4,32,128]{2,1,0:T(8,128)} %w_ref.5) | copy-start | bytes 196612
  0.7 5.4 %copy-start = (s32[3,128,512]{2,1,0:T(8,128)S(1)}, s32[3,128,512]{2,1,0:T(8,128)}, u32[]{:S(2)}) copy-start(s32[3,128,512]{2,1,0:T(8,128)} %V.3) | copy-start | bytes 2359300
  0.7 5.4 %copy-start.3 = (s32[4,128,512]{2,1,0:T(8,128)S(1)}, s32[4,128,512]{2,1,0:T(8,128)}, u32[]{:S(2)}) copy-start(s32[4,128,512]{2,1,0:T(8,128)} %f_b.1) | copy-start | bytes 3145732
  0.7 5.4 %copy-start.4 = (f32[4,128,512]{2,1,0:T(8,128)S(1)}, f32[4,128,512]{2,1,0:T(8,128)}, u32[]{:S(2)}) copy-start(f32[4,128,512]{2,1,0:T(8,128)} %a_b.1) | copy-start | bytes 3145732
  2.9 6.8 %collective-permute-start = (f32[8,8,512]{2,1,0:T(8,128)}, f32[8,8,512]{2,1,0:T(8,128)S(1)}, u32[]{:S(2)}, u32[]{:S(2)}) collective-permute-start(f32[8,8,512]{2,1,0:T(8,128)} %get-tuple-element.38), channel_id=1, source_target_pairs={{0,4},{1,5},{2,6},{3,7},{4,0},{5,1},{6,2},{7,3},{8,12},{9,13},{10,... | collective-permute-start | bytes 393224 | tf_op jit(solution)/shard_map/ppermute | solution.py:668
  3.4 6.3 %collective-permute-start.1 = (f32[8,8,512]{2,1,0:T(8,128)}, f32[8,8,512]{2,1,0:T(8,128)S(1)}, u32[]{:S(2)}, u32[]{:S(2)}) collective-permute-start(f32[8,8,512]{2,1,0:T(8,128)} %get-tuple-element.39), channel_id=1, source_target_pairs={{0,1},{1,0},{2,3},{3,2},{4,8},{5,9},{6,10},{7,11},{8,4},{9,5},{10,... | collective-permute-start | bytes 393224 | tf_op jit(solution)/shard_map/ppermute | solution.py:668
  9.9 4.9 %collective-permute-start.2 = (f32[144,128]{1,0:T(8,128)S(1)}, f32[144,128]{1,0:T(8,128)S(1)}, u32[]{:S(2)}, u32[]{:S(2)}) collective-permute-start(f32[144,128]{1,0:T(8,128)S(1)} %get-tuple-element.44), channel_id=1, source_target_pairs={{0,1},{1,0},{2,3},{3,2},{4,5},{5,4},{6,7},{7,6},{8,9},{9,8},{10,11... | collective-permute-start | bytes 221192 | tf_op jit(solution)/shard_map/ppermute | solution.py:668
  11.4 3.4 %collective-permute-start.3 = (f32[144,128]{1,0:T(8,128)S(1)}, f32[144,128]{1,0:T(8,128)S(1)}, u32[]{:S(2)}, u32[]{:S(2)}) collective-permute-start(f32[144,128]{1,0:T(8,128)S(1)} %get-tuple-element.45), channel_id=1, source_target_pairs={{0,4},{1,2},{2,1},{3,7},{4,0},{5,6},{6,5},{7,3},{8,12},{9,10},{10,... | collective-permute-start | bytes 221192 | tf_op jit(solution)/shard_map/ppermute | solution.py:668
  16.1 5.3 %collective-permute-start.4 = (f32[4,8,128]{2,1,0:T(8,128)S(1)}, f32[4,8,128]{2,1,0:T(8,128)S(1)}, u32[]{:S(2)}, u32[]{:S(2)}) collective-permute-start(f32[4,8,128]{2,1,0:T(8,128)S(1)} %get-tuple-element.50.hm_ref), channel_id=1, source_target_pairs={{0,4},{1,5},{2,6},{3,7},{4,0},{5,1},{6,2},{7,3},{8,12},{9,13},{10,... | collective-permute-start | bytes 49160 | tf_op jit(solution)/shard_map/ppermute | solution.py:668
  16.2 5.2 %collective-permute-start.5 = (f32[4,8,128]{2,1,0:T(8,128)S(1)}, f32[4,8,128]{2,1,0:T(8,128)S(1)}, u32[]{:S(2)}, u32[]{:S(2)}) collective-permute-start(f32[4,8,128]{2,1,0:T(8,128)S(1)} %get-tuple-element.50.hm_ref), channel_id=1, source_target_pairs={{0,1},{1,0},{2,3},{3,2},{4,8},{5,9},{6,10},{7,11},{8,4},{9,5},{10,... | collective-permute-start | bytes 49160 | tf_op jit(solution)/shard_map/ppermute | solution.py:668
  21.5 3.9 %collective-permute-start.6 = (f32[48,128]{1,0:T(8,128)S(1)}, f32[48,128]{1,0:T(8,128)S(1)}, u32[]{:S(2)}, u32[]{:S(2)}) collective-permute-start(f32[48,128]{1,0:T(8,128)S(1)} %get-tuple-element.52), channel_id=1, source_target_pairs={{0,1},{1,0},{2,3},{3,2},{4,5},{5,4},{6,7},{7,6},{8,9},{9,8},{10,11... | collective-permute-start | bytes 73736 | tf_op jit(solution)/shard_map/ppermute | solution.py:668
  23.1 2.3 %collective-permute-start.7 = (f32[48,128]{1,0:T(8,128)S(1)}, f32[48,128]{1,0:T(8,128)S(1)}, u32[]{:S(2)}, u32[]{:S(2)}) collective-permute-start(f32[48,128]{1,0:T(8,128)S(1)} %get-tuple-element.53), channel_id=1, source_target_pairs={{0,4},{1,2},{2,1},{3,7},{4,0},{5,6},{6,5},{7,3},{8,12},{9,10},{10,... | collective-permute-start | bytes 73736 | tf_op jit(solution)/shard_map/ppermute | solution.py:668

commit v5 on v4

--- a/solution.py
+++ b/solution.py
@@ -118,65 +118,93 @@
     )
 
 
-def packed(values, side, high, out):
-    lane = iota(out.shape, 1)
-    slot, upper = lax.shift_right_logical(lane, 3), lane % 8 >= REACH
-    for p, value in enumerate(values):
-        shift = (8 * p + REACH * (side + high)) % LANE
-        value = pltpu.roll(value.astype(jnp.float32), shift, 1) if shift else value
-        out = jnp.where((slot == p) & (upper if high else ~upper), value, out)
-    return out
+def put(out, value, at, side):
+    at = at % LANE
+    shift = (at + REACH * side) % LANE
+    lane, value = iota(out.shape, 1), value.astype(jnp.float32)
+    value = pltpu.roll(value, shift, 1) if shift else value
+    return jnp.where((lane >= at) & (lane < at + REACH), value, out)
 
 
 def end_tiles(width):
     return slice(0, LANE), slice(width - LANE, width)
+
+
+LOWER = LANE // 2 + REACH
 
 
 def pack_own_columns(fields, w_ref, e_ref, o_ref):
     rows, cols = fields[0].shape[1:]
     layers, cell_rows, cells = w_ref.shape
+    part = rows // 2 + SUB
+    zero = jnp.zeros((SUB, LANE), jnp.float32)
     sides = []
     for side in range(2):
         tile, cell_tile = end_tiles(cols)[side], end_tiles(cells)[side]
         values = [ref[l, :, tile] for ref in fields for l in range(ref.shape[0])]
-        out = packed(values, side, False, jnp.zeros((rows, LANE), jnp.float32))
-        head = packed([w_ref[l, :, cell_tile] for l in range(layers)], side, True, out[:cell_rows])
-        sides.append(jnp.concatenate([head, out[cell_rows:]], axis=0))
+        out = jnp.zeros((part + SUB, LANE), jnp.float32)
+        for p, value in enumerate(values):
+            value = value.astype(jnp.float32)
+            out = put(out, jnp.concatenate([zero, value[:part]], 0), 8 * p, side)
+            out = put(out, jnp.concatenate([value[rows - part :], zero], 0), 8 * p + LOWER, side)
+        warm = zero
+        for l in range(layers):
+            for k in range(cell_rows // SUB):
+                value = w_ref[l, k * SUB : (k + 1) * SUB, cell_tile]
+                warm = put(warm, value, 16 * (k + 1) + REACH * l, side)
+        sides.append(jnp.concatenate([out, warm], axis=0))
     even, _, _ = place("col")
-    pick = uniform(even, (rows, LANE))
+    pick = uniform(even, sides[0].shape)
     e_ref[...] = jnp.where(pick, sides[1], sides[0])
     o_ref[...] = jnp.where(pick, sides[0], sides[1])
 
 
 def pack_cols_kernel(re_ref, ro_ref, own_e, own_o, w_ref, e_ref, o_ref):
-    rows, cols = own_e.shape[0], re_ref.shape[2]
+    cols = re_ref.shape[2]
+    tall = own_e.shape[0] - SUB
     layers, cell_rows, cells = w_ref.shape
     half = 2 * layers
+    final = 16 * (cell_rows // SUB + 1)
     even, _, _ = place("col")
     pick = uniform(even, (SUB, LANE))
     zero = jnp.zeros((SUB, LANE), jnp.float32)
-    tops, bots, lows = [], [], []
+    parts = []
     for side in range(2):
         tile, cell_tile = end_tiles(cols)[side], end_tiles(cells)[side]
-        margins = [row_margin(re_ref, ro_ref, p, tile, half) for p in range(2 * half - 1)]
-        warm = [
-            row_margin(
-                re_ref, ro_ref, 2 * half - 1,
-                slice(l * cells + cell_tile.start, l * cells + cell_tile.stop), half,
-            )
-            for l in range(layers)
-        ]
-        tops.append(packed([m[0] for m in warm], side, True, packed([m[0] for m in margins], side, False, zero)))
-        bots.append(packed([m[1] for m in margins], side, False, zero))
-        lows.append(packed([m[1] for m in warm], side, True, zero))
-    high = iota((SUB, LANE), 1) % 8 >= REACH
-    at = SUB + cell_rows
+        above = below = warm = zero
+        for p in range(2 * half - 1):
+            top, bot = row_margin(re_ref, ro_ref, p, tile, half)
+            above = put(above, top, 8 * p, side)
+            below = put(below, bot, 8 * p + LOWER, side)
+        for l in range(layers):
+            at = slice(l * cells + cell_tile.start, l * cells + cell_tile.stop)
+            top, bot = row_margin(re_ref, ro_ref, 2 * half - 1, at, half)
+            warm = put(put(warm, top, REACH * l, side), bot, final + REACH * l, side)
+        parts.append((above, below, warm))
+    lane = iota((SUB, LANE), 1)
+    low = lane % 8 < REACH
+    ends = (lane < 16) | ((lane >= final) & (lane < final + 16))
     for ref, own, first in ((e_ref, own_e, 1), (o_ref, own_o, 0)):
-        ref[SUB : SUB + rows, :] = own[...]
-        ref[0:SUB, :] = jnp.where(pick, tops[first], tops[1 - first])
-        ref[SUB + rows : 2 * SUB + rows, :] = jnp.where(pick, bots[first], bots[1 - first])
-        low = jnp.where(pick, lows[first], lows[1 - first])
-        ref[at : at + SUB, :] = jnp.where(high, low, own[cell_rows : cell_rows + SUB, :])
+        above, below, warm = (jnp.where(pick, a, b) for a, b in zip(parts[first], parts[1 - first]))
+        ref[SUB : tall - SUB, :] = own[SUB : tall - SUB, :]
+        ref[0:SUB, :] = jnp.where(low, above, own[0:SUB, :])
+        ref[tall - SUB : tall, :] = jnp.where(low, own[tall - SUB : tall, :], below)
+        ref[tall : tall + SUB, :] = jnp.where(ends, warm, own[tall : tall + SUB, :])
+
+
+def col_sides(e, o):
+    even, before, after = place("col")
+    pick = uniform(even, e.shape)
+    right, left = jnp.where(pick, e, o), jnp.where(pick, o, e)
+    return (
+        jnp.where(uniform(after, e.shape), right, 0.0),
+        jnp.where(uniform(before, e.shape), left, 0.0),
+    )
+
+
+def turned(value, shift):
+    shift = shift % LANE
+    return pltpu.roll(value, shift, 1) if shift else value
 
 
 def col_margin(e, o, high, back):
@@ -492,8 +520,8 @@
                 jnp.where(lane < LANE // 4, left[:tall], pltpu.roll(right[:tall], 48, 1)),
                 jnp.where(
                     lane < 3 * LANE // 4,
-                    pltpu.roll(left[rows + 2 * SUB - tall :], 64, 1),
-                    pltpu.roll(right[rows + 2 * SUB - tall :], 112, 1),
+                    pltpu.roll(left[rows + 2 * SUB - tall :], LOWER, 1),
+                    pltpu.roll(right[rows + 2 * SUB - tall :], 48 + LOWER, 1),
                 ),
             )
             plane += 1
@@ -515,20 +543,15 @@
     layers, rows, _ = xc_ref.shape
     cell_rows, cells = hc_ref.shape[1:]
     tall = strip_ref.shape[1]
-    mixed = col_margin(ce_ref[...], co_ref[...], False, 52)
-    upper, lower = mixed[:tall], mixed[rows + 2 * SUB - tall :]
+    right, left = col_sides(ce_ref[0:tall, :], co_ref[0:tall, :])
     lane = iota((tall, LANE), 1)
-    in_upper = ((lane >= 48) & (lane < 48 + REACH)) | (lane >= LANE - REACH)
-    in_lower = ((lane >= 112) & (lane < 112 + REACH)) | ((lane >= 64 - REACH) & (lane < 64))
+    in_right = ((lane >= 48) & (lane < 48 + REACH)) | ((lane >= 48 + LOWER) & (lane < 48 + LOWER + REACH))
+    in_left = (lane >= LANE - REACH) | ((lane >= LOWER - REACH) & (lane < LOWER))
     plane = 0
     for pad in (X, G, J, V):
         for l in range(pad.shape[0]):
-            shift = (48 - 8 * plane) % LANE
-            value = pltpu.roll(upper, shift, 1) if shift else upper
-            shift = (112 - 8 * plane) % LANE
-            other = pltpu.roll(lower, shift, 1) if shift else lower
-            value = jnp.where(in_upper, value, strip_ref[plane])
-            pad[l] = jnp.where(in_lower, other, value)
+            value = jnp.where(in_right, turned(right, 48 - 8 * plane), strip_ref[plane])
+            pad[l] = jnp.where(in_left, turned(left, LANE - REACH - 8 * plane), value)
             plane += 1
     groups = tall // SUB
     first_sweep(groups, 0, X, G, J, V, W0, XN, WN, D, DI, GD, JD, EH, EV)
@@ -538,7 +561,7 @@
     at_edge = (c < REACH) | (c >= cells - REACH)
     halves = []
     for part in range(2):
-        slot = jnp.where(c < cells // 2, c, c - cells + 12) + 16 * part
+        slot = jnp.where(c < cells // 2, c, c - cells + 12) + LOWER // REFINE * part
         same = at_edge & (lax.shift_right_logical(n, 2) == slot)
         left = at_edge & (n == jnp.where(slot == 0, LANE - 1, REFINE * slot - 1))
         halves.append(
@@ -556,7 +579,7 @@
         hc_ref[l, cell_rows // 2 : cell_rows, :] = final
         x = XL[l, SUB : SUB + rows // 2, :]
         xc_ref[l, 0 : rows // 2, :] = jnp.where(low, x, pltpu.roll(x, 80, 1))
-        xc_ref[l, rows // 2 : rows, :] = jnp.where(low, pltpu.roll(x, 64, 1), pltpu.roll(x, 16, 1))
+        xc_ref[l, rows // 2 : rows, :] = jnp.where(low, turned(x, -LOWER), turned(x, 80 - LOWER))
         own = jnp.concatenate([first[:REACH], final[cell_rows // 2 - REACH :]], 0)
         hm_ref[l] = jnp.where(edge, own, hr_ref[l])
 
@@ -594,7 +617,9 @@
     layers, cell_rows, cells = w_ref.shape
     half = 2 * layers
     height, width = cell_rows + 2 * SUB, cells + LANE
-    warm_mixed = col_margin(ce_ref[0:height, :], co_ref[0:height, :], True, REACH)
+    tall = ce_ref.shape[0]
+    right, left = col_sides(ce_ref[tall - SUB : tall, :], co_ref[tall - SUB : tall, :])
+    lane = iota((SUB, LANE), 1)
     heat_mixed = col_margin(hce_ref[...], hco_ref[...], False, REACH)
     cell = iota((cell_rows, cells), 1)
     edge = (cell < REACH - 1) | (cell > cells - REACH)
@@ -605,7 +630,12 @@
             re_ref, ro_ref, 2 * half - 1, slice(l * cells, (l + 1) * cells), half
         )
         own = jnp.concatenate([top, w_ref[l], bot], axis=0)
-        theta.append(jnp.concatenate([own, margin_tile(warm_mixed, 8 * l + REACH)], axis=1))
+        pieces = []
+        for k in range(height // SUB):
+            at = 16 * k + REACH * l
+            value = jnp.where(lane < REACH, turned(right, -at), 0.0)
+            pieces.append(jnp.where(lane >= LANE - REACH, turned(left, -REACH - at), value))
+        theta.append(jnp.concatenate([own, jnp.concatenate(pieces, axis=0)], axis=1))
         own = jnp.where(edge, hc_ref[l], h_ref[l])
         first, final = own[:SUB], own[cell_rows - SUB :]
         first = jnp.where(cell_row < REACH - 1, hm_ref[l], first)
@@ -686,7 +716,7 @@
     )(*row_args)
     row_e, row_o = swap(e, o, row_swaps)
 
-    fields = (shape(layers, rows, cols),) * 10 + (shape(rows, LANE),) * 2
+    fields = (shape(layers, rows, cols),) * 10 + (shape(rows // 2 + 3 * SUB, LANE),) * 2
     node_scratch = pltpu.VMEM((layers, rows, cols), f32)
     g, inject, *mid = pl.pallas_call(
         bulk_first_kernel,
@@ -702,7 +732,7 @@
     for a in (x, g, inject, via):
         col_args += [a, a]
         col_specs += [edge_cols(a, 0), edge_cols(a, last_col)]
-    message = shape(rows + 2 * SUB, LANE)
+    message = shape(rows // 2 + 3 * SUB, LANE)
     e, o = pl.pallas_call(
         pack_cols_kernel,
         out_shape=(message, message),

time: 27.2 us -> 26.8 us (0.985)
  waiting for transfers between devices: 0.95 us -> 0.11 us
  starting transfers between devices: 9.89 us -> 10.2 us
    ppermute x8, waiting for transfers between devices: 0.95 us -> 0.11 us  [swap(): lax.ppermute(m, BOTH, tables(mesh_rows, mesh_cols, first))]
    ppermute x8, starting transfers between devices: 9.89 us -> 10.2 us  [swap(): lax.ppermute(m, BOTH, tables(mesh_rows, mesh_cols, first))]
  transfers between devices with their start and end apart: 8 -> 8, of which waited for: 2 -> 1; matrix products, arithmetic and copies ran while one was open for 0% -> 0% of each run, Pallas kernels for 37% -> 38%
where the time goes in v5:
time: 26.8 us; the launch traced here: 26.5 us
  Pallas kernels  15.4 us (57%)
  starting transfers between devices  10.2 us (38%)
  between operations  0.81 us (3%)
    ppermute x8, starting transfers between devices, swap(): lax.ppermute(m, BOTH, tables(mesh_rows, mesh_cols, first))  10.2 us
    pallas_call x1, Pallas kernels, on_device(): pl.pallas_call(bulk_first_kernel, out_shape=fields, scratch_shapes=[node_...  3.73 us
    pallas_call x1, Pallas kernels, on_device(): pl.pallas_call(row_strip_kernel, grid=(1,), in_specs=deep_specs + col_spe...  2.35 us
    pallas_call x1, Pallas kernels, on_device(): pl.pallas_call(pack_rows_kernel, grid=(1,), in_specs=row_specs, out_specs...  2.25 us
    pallas_call x1, Pallas kernels, on_device(): pl.pallas_call(bulk_mid_kernel, out_shape=shape(layers, rows, cols), scra...  2.18 us
    pallas_call x1, Pallas kernels, on_device(): pl.pallas_call(bulk_last_kernel, out_shape=(shape(layers, rows, cols), sh...  1.76 us
    pallas_call x1, Pallas kernels, on_device(): pl.pallas_call(warm_kernel, out_shape=shape(layers, cell_rows, cells), co...  1.6 us
    pallas_call x1, Pallas kernels, on_device(): pl.pallas_call(col_strip_kernel, out_shape=(shape(layers, rows, LANE), sh...  1.25 us
  transfers between devices with their start and end apart: 8, of which 1 were waited for; matrix products, arithmetic and copies ran while one was open for 0% of the time, Pallas kernels for 38%

profile of v5, /device:TPU:0, one launch (start us, length us, event | category | flops | bytes accessed | tf_op | source)
XLA Modules:
  0.0 26.5 jit_solution(10553322106667202105)
XLA Ops:
  0.6 0.0 copy-start.1
  0.6 0.0 copy-start.2
  0.7 0.0 copy-start.5
  0.7 0.0 copy-start
  0.7 0.0 copy-start.3
  0.7 0.0 copy-start.4
  0.7 2.3 %pack_rows.1 = (f32[8,8,512]{2,1,0:T(8,128)}, f32[8,8,512]{2,1,0:T(8,128)}) custom-call(f32[4,128,512]{2,1,0:T(8,128)} %x_r.1, f32[4,128,512]{2,1,0:T(8,128)} %x_r.1, f32[4,128,512]{2,1,0:T(8,128)} %b_b.1, f32[4,128,512]{2,1,0:T(8,128)} %b_b.1, f32[4,32,128]{2,1,0:T(8,128)} %w_ref.5, f32[4,32,128]{2,1,0:T(8,128)} %w_ref.5, s32[3,128,512]{2,1,0:T(8,128)} %V.3, ...), custom_call_target="tpu_custom_call" | custom-call | tf_op jit(solution)/shard_map/pack_rows/pallas_call | solution.py:708
  2.9 0.5 %collective-permute-start = (f32[8,8,512]{2,1,0:T(8,128)}, f32[8,8,512]{2,1,0:T(8,128)S(1)}, u32[]{:S(2)}, u32[]{:S(2)}) collective-permute-start(f32[8,8,512]{2,1,0:T(8,128)} %get-tuple-element.38), channel_id=1, source_target_pairs={{0,4},{1,5},{2,6},{3,7},{4,0},{5,1},{6,2},{7,3},{8,12},{9,13},{10,... | collective-permute-start | bytes 393224 | tf_op jit(solution)/shard_map/ppermute | solution.py:698
  3.4 2.6 %collective-permute-start.1 = (f32[8,8,512]{2,1,0:T(8,128)}, f32[8,8,512]{2,1,0:T(8,128)S(1)}, u32[]{:S(2)}, u32[]{:S(2)}) collective-permute-start(f32[8,8,512]{2,1,0:T(8,128)} %get-tuple-element.39), channel_id=1, source_target_pairs={{0,1},{1,0},{2,3},{3,2},{4,8},{5,9},{6,10},{7,11},{8,4},{9,5},{10,... | collective-permute-start | bytes 393224 | tf_op jit(solution)/shard_map/ppermute | solution.py:698
  6.0 0.0 copy-done.1
  6.0 0.0 copy-done.2
  6.0 0.0 copy-done.5
  6.0 0.0 copy-done
  6.0 0.0 copy-done.3
  6.0 0.0 copy-done.4
  6.1 3.7 %bulk_first.1 = (f32[4,128,512]{2,1,0:T(8,128)S(1)}, f32[4,128,512]{2,1,0:T(8,128)S(1)}, f32[4,128,512]{2,1,0:T(8,128)S(1)}, f32[4,128,512]{2,1,0:T(8,128)S(1)},...) custom-call(f32[4,128,512]{2,1,0:T(8,128)S(1)} %copy-done.1, ...), custom_call_target="tpu_custom_call" | custom-call | flops 10485760 | bytes 15728640 | tf_op jit(solution)/shard_map/bulk_first/pallas_call | solution.py:721
  9.8 0.0 collective-permute-done.re_ref
  9.8 0.0 collective-permute-done.1.ro_ref
  9.8 0.2 pack_cols.1
  10.0 1.4 %collective-permute-start.2 = (f32[88,128]{1,0:T(8,128)S(1)}, f32[88,128]{1,0:T(8,128)S(1)}, u32[]{:S(2)}, u32[]{:S(2)}) collective-permute-start(f32[88,128]{1,0:T(8,128)S(1)} %get-tuple-element.44), channel_id=1, source_target_pairs={{0,1},{1,0},{2,3},{3,2},{4,5},{5,4},{6,7},{7,6},{8,9},{9,8},{10,11... | collective-permute-start | bytes 135176 | tf_op jit(solution)/shard_map/ppermute | solution.py:698
  11.4 0.7 %collective-permute-start.3 = (f32[88,128]{1,0:T(8,128)S(1)}, f32[88,128]{1,0:T(8,128)S(1)}, u32[]{:S(2)}, u32[]{:S(2)}) collective-permute-start(f32[88,128]{1,0:T(8,128)S(1)} %get-tuple-element.45), channel_id=1, source_target_pairs={{0,4},{1,2},{2,1},{3,7},{4,0},{5,6},{6,5},{7,3},{8,12},{9,10},{10,... | collective-permute-start | bytes 135176 | tf_op jit(solution)/shard_map/ppermute | solution.py:698
  12.1 2.3 %row_strip.1 = (f32[4,32,512]{2,1,0:T(8,128)S(1)}, f32[4,8,128]{2,1,0:T(8,128)S(1)}, f32[15,80,128]{2,1,0:T(8,128)S(1)}) custom-call(f32[4,128,512]{2,1,0:T(8,128)S(1)} %copy-done.1, f32[4,128,512]{2,1,0:T(8,128)S(1)} %copy-done.1, f32[4,128,512]{2,1,0:T(8,128)S(1)} %get-tuple-element.34.G.g_t.g_b.g_l.g_r, ...), custom_call_target="tpu_custom_call" | custom-call | flops 10485760 | bytes 5242880 | tf_op jit(solution)/shard_map/row_strip/pallas_call | solution.py:758
  14.5 0.0 collective-permute-done.2.ce_ref
  14.5 0.0 collective-permute-done.3.co_ref
  14.5 1.3 %col_strip.1 = (f32[4,128,128]{2,1,0:T(8,128)S(1)}, f32[4,32,128]{2,1,0:T(8,128)S(1)}, f32[4,8,128]{2,1,0:T(8,128)S(1)}) custom-call(f32[15,80,128]{2,1,0:T(8,128)S(1)} %get-tuple-element.41.strip_ref, f32[88,128]{1,0:T(8,128)S(1)} %collective-permute-done.2.ce_ref, f32[88,128]{1,0:T(8,128)S(1)} %collective-permute-done.3.co_ref, ...), custom_call_target="tpu_custom_call" | custom-call | tf_op jit(solution)/shard_map/col_strip/pallas_call | solution.py:770
  15.7 0.1 collective-permute-start.4
  15.8 2.9 %collective-permute-start.5 = (f32[4,8,128]{2,1,0:T(8,128)S(1)}, f32[4,8,128]{2,1,0:T(8,128)S(1)}, u32[]{:S(2)}, u32[]{:S(2)}) collective-permute-start(f32[4,8,128]{2,1,0:T(8,128)S(1)} %get-tuple-element.50.hm_ref), channel_id=1, source_target_pairs={{0,1},{1,0},{2,3},{3,2},{4,8},{5,9},{6,10},{7,11},{8,4},{9,5},{10,... | collective-permute-start | bytes 49160 | tf_op jit(solution)/shard_map/ppermute | solution.py:698
  18.7 2.2 %bulk_mid.1.XN._ = f32[4,128,512]{2,1,0:T(8,128)S(1)} custom-call(f32[4,128,512]{2,1,0:T(8,128)S(1)} %get-tuple-element.28.X, s32[3,128,512]{2,1,0:T(8,128)S(1)} %copy-done, f32[4,128,512]{2,1,0:T(8,128)S(1)} %get-tuple-element.29.W, f32[4,128,512]{2,1,0:T(8,128)S(1)} %get-tuple-element.30.D, f32[4,128,512]{2,1,0:T(8,128)S(1)} %get-tuple-element.31.DI, ...), custom_call_target="tpu_custom_call" | custom-call | flops 5242880 | bytes 5242880 | tf_op jit(solution)/shard_map/bulk_mid/pallas_call | solution.py:780
  20.9 0.0 collective-permute-done.4.re_ref.hre_ref
  20.9 0.0 collective-permute-done.5.ro_ref.hro_ref
  20.9 0.1 pack_heat.1
  21.0 1.6 %collective-permute-start.6 = (f32[48,128]{1,0:T(8,128)S(1)}, f32[48,128]{1,0:T(8,128)S(1)}, u32[]{:S(2)}, u32[]{:S(2)}) collective-permute-start(f32[48,128]{1,0:T(8,128)S(1)} %get-tuple-element.52), channel_id=1, source_target_pairs={{0,1},{1,0},{2,3},{3,2},{4,5},{5,4},{6,7},{7,6},{8,9},{9,8},{10,11... | collective-permute-start | bytes 73736 | tf_op jit(solution)/shard_map/ppermute | solution.py:698
  22.6 0.4 %collective-permute-start.7 = (f32[48,128]{1,0:T(8,128)S(1)}, f32[48,128]{1,0:T(8,128)S(1)}, u32[]{:S(2)}, u32[]{:S(2)}) collective-permute-start(f32[48,128]{1,0:T(8,128)S(1)} %get-tuple-element.53), channel_id=1, source_target_pairs={{0,4},{1,2},{2,1},{3,7},{4,0},{5,6},{6,5},{7,3},{8,12},{9,10},{10,... | collective-permute-start | bytes 73736 | tf_op jit(solution)/shard_map/ppermute | solution.py:698
  23.0 1.8 %bulk_last.1 = (f32[4,128,512]{2,1,0:T(8,128)}, f32[4,32,128]{2,1,0:T(8,128)S(1)}) custom-call(f32[4,128,512]{2,1,0:T(8,128)S(1)} %bulk_mid.1.XN._, s32[3,128,512]{2,1,0:T(8,128)S(1)} %copy-done, f32[4,128,512]{2,1,0:T(8,128)S(1)} %get-tuple-element.35.EH, f32[4,128,512]{2,1,0:T(8,128)S(1)} %get-tuple-element.36.EV, ...), custom_call_target="tpu_custom_call" | custom-call | flops 10485760 | bytes 15728640 | tf_op jit(solution)/shard_map/bulk_last/pallas_call | solution.py:800
  24.8 0.1 collective-permute-done.6.hce_ref
  24.9 0.0 collective-permute-done.7.hco_ref
  24.9 1.6 %warm.1 = f32[4,32,128]{2,1,0:T(8,128)} custom-call(f32[4,32,128]{2,1,0:T(8,128)S(1)} %copy-done.5, f32[4,32,128]{2,1,0:T(8,128)S(1)} %get-tuple-element.49.h_ref, f32[4,8,128]{2,1,0:T(8,128)S(1)} %get-tuple-element.50.hm_ref, f32[4,32,128]{2,1,0:T(8,128)S(1)} %get-tuple-element.51.h_ref.hc_ref, f32[8,8,512]{2,1,0:T(8,128)S(1)} %collective-permute-done.re_ref, ...), custom_call_target="tpu_custom_call" | custom-call | tf_op jit(solution)/shard_map/warm/pallas_call | solution.py:810
Async XLA Ops:
  0.6 5.4 %copy-start.1 = (f32[4,128,512]{2,1,0:T(8,128)S(1)}, f32[4,128,512]{2,1,0:T(8,128)}, u32[]{:S(2)}) copy-start(f32[4,128,512]{2,1,0:T(8,128)} %x_r.1) | copy-start | bytes 3145732
  0.6 5.4 %copy-start.2 = (f32[4,128,512]{2,1,0:T(8,128)S(1)}, f32[4,128,512]{2,1,0:T(8,128)}, u32[]{:S(2)}) copy-start(f32[4,128,512]{2,1,0:T(8,128)} %b_b.1) | copy-start | bytes 3145732
  0.7 5.4 %copy-start.5 = (f32[4,32,128]{2,1,0:T(8,128)S(1)}, f32[4,32,128]{2,1,0:T(8,128)}, u32[]{:S(2)}) copy-start(f32[4,32,128]{2,1,0:T(8,128)} %w_ref.5) | copy-start | bytes 196612
  0.7 5.4 %copy-start = (s32[3,128,512]{2,1,0:T(8,128)S(1)}, s32[3,128,512]{2,1,0:T(8,128)}, u32[]{:S(2)}) copy-start(s32[3,128,512]{2,1,0:T(8,128)} %V.3) | copy-start | bytes 2359300
  0.7 5.4 %copy-start.3 = (s32[4,128,512]{2,1,0:T(8,128)S(1)}, s32[4,128,512]{2,1,0:T(8,128)}, u32[]{:S(2)}) copy-start(s32[4,128,512]{2,1,0:T(8,128)} %f_b.1) | copy-start | bytes 3145732
  0.7 5.4 %copy-start.4 = (f32[4,128,512]{2,1,0:T(8,128)S(1)}, f32[4,128,512]{2,1,0:T(8,128)}, u32[]{:S(2)}) copy-start(f32[4,128,512]{2,1,0:T(8,128)} %a_b.1) | copy-start | bytes 3145732
  2.9 6.8 %collective-permute-start = (f32[8,8,512]{2,1,0:T(8,128)}, f32[8,8,512]{2,1,0:T(8,128)S(1)}, u32[]{:S(2)}, u32[]{:S(2)}) collective-permute-start(f32[8,8,512]{2,1,0:T(8,128)} %get-tuple-element.38), channel_id=1, source_target_pairs={{0,4},{1,5},{2,6},{3,7},{4,0},{5,1},{6,2},{7,3},{8,12},{9,13},{10,... | collective-permute-start | bytes 393224 | tf_op jit(solution)/shard_map/ppermute | solution.py:698
  3.4 6.4 %collective-permute-start.1 = (f32[8,8,512]{2,1,0:T(8,128)}, f32[8,8,512]{2,1,0:T(8,128)S(1)}, u32[]{:S(2)}, u32[]{:S(2)}) collective-permute-start(f32[8,8,512]{2,1,0:T(8,128)} %get-tuple-element.39), channel_id=1, source_target_pairs={{0,1},{1,0},{2,3},{3,2},{4,8},{5,9},{6,10},{7,11},{8,4},{9,5},{10,... | collective-permute-start | bytes 393224 | tf_op jit(solution)/shard_map/ppermute | solution.py:698
  10.0 4.5 %collective-permute-start.2 = (f32[88,128]{1,0:T(8,128)S(1)}, f32[88,128]{1,0:T(8,128)S(1)}, u32[]{:S(2)}, u32[]{:S(2)}) collective-permute-start(f32[88,128]{1,0:T(8,128)S(1)} %get-tuple-element.44), channel_id=1, source_target_pairs={{0,1},{1,0},{2,3},{3,2},{4,5},{5,4},{6,7},{7,6},{8,9},{9,8},{10,11... | collective-permute-start | bytes 135176 | tf_op jit(solution)/shard_map/ppermute | solution.py:698
  11.4 3.0 %collective-permute-start.3 = (f32[88,128]{1,0:T(8,128)S(1)}, f32[88,128]{1,0:T(8,128)S(1)}, u32[]{:S(2)}, u32[]{:S(2)}) collective-permute-start(f32[88,128]{1,0:T(8,128)S(1)} %get-tuple-element.45), channel_id=1, source_target_pairs={{0,4},{1,2},{2,1},{3,7},{4,0},{5,6},{6,5},{7,3},{8,12},{9,10},{10,... | collective-permute-start | bytes 135176 | tf_op jit(solution)/shard_map/ppermute | solution.py:698
  15.7 5.1 %collective-permute-start.4 = (f32[4,8,128]{2,1,0:T(8,128)S(1)}, f32[4,8,128]{2,1,0:T(8,128)S(1)}, u32[]{:S(2)}, u32[]{:S(2)}) collective-permute-start(f32[4,8,128]{2,1,0:T(8,128)S(1)} %get-tuple-element.50.hm_ref), channel_id=1, source_target_pairs={{0,4},{1,5},{2,6},{3,7},{4,0},{5,1},{6,2},{7,3},{8,12},{9,13},{10,... | collective-permute-start | bytes 49160 | tf_op jit(solution)/shard_map/ppermute | solution.py:698
  15.8 5.1 %collective-permute-start.5 = (f32[4,8,128]{2,1,0:T(8,128)S(1)}, f32[4,8,128]{2,1,0:T(8,128)S(1)}, u32[]{:S(2)}, u32[]{:S(2)}) collective-permute-start(f32[4,8,128]{2,1,0:T(8,128)S(1)} %get-tuple-element.50.hm_ref), channel_id=1, source_target_pairs={{0,1},{1,0},{2,3},{3,2},{4,8},{5,9},{6,10},{7,11},{8,4},{9,5},{10,... | collective-permute-start | bytes 49160 | tf_op jit(solution)/shard_map/ppermute | solution.py:698
  21.0 3.9 %collective-permute-start.6 = (f32[48,128]{1,0:T(8,128)S(1)}, f32[48,128]{1,0:T(8,128)S(1)}, u32[]{:S(2)}, u32[]{:S(2)}) collective-permute-start(f32[48,128]{1,0:T(8,128)S(1)} %get-tuple-element.52), channel_id=1, source_target_pairs={{0,1},{1,0},{2,3},{3,2},{4,5},{5,4},{6,7},{7,6},{8,9},{9,8},{10,11... | collective-permute-start | bytes 73736 | tf_op jit(solution)/shard_map/ppermute | solution.py:698
  22.6 2.3 %collective-permute-start.7 = (f32[48,128]{1,0:T(8,128)S(1)}, f32[48,128]{1,0:T(8,128)S(1)}, u32[]{:S(2)}, u32[]{:S(2)}) collective-permute-start(f32[48,128]{1,0:T(8,128)S(1)} %get-tuple-element.53), channel_id=1, source_target_pairs={{0,4},{1,2},{2,1},{3,7},{4,0},{5,6},{6,5},{7,3},{8,12},{9,10},{10,... | collective-permute-start | bytes 73736 | tf_op jit(solution)/shard_map/ppermute | solution.py:698

commit v6 on v5

--- a/solution.py
+++ b/solution.py
@@ -437,13 +437,13 @@
         g_ref[l] = jnp.sqrt(b_ref[l]) * dot(spread_rows, dot(warm, spread))
         j_ref[l] = f_ref[l].astype(jnp.float32) * a_ref[l]
     pack_own_columns((x_ref, g_ref, j_ref, v_ref), w_ref, own_e, own_o)
-    first_sweep(2, 1, x_ref, g_ref, j_ref, v_ref, W0, XN, WN, D, DI, GD, JD, EH, EV)
+    first_sweep(7, 1, x_ref, g_ref, j_ref, v_ref, W0, XN, WN, D, DI, GD, JD, EH, EV)
 
 
 def bulk_mid_kernel(X, V, W, D, DI, GD, JD, G, XL, WN, XN, DN):
     (keep, gain), (keep_last, gain_last) = sweep_gains()
-    next_sweep(2, 1, keep, gain, X, V, W, D, DI, GD, JD, G, XN, WN, DN)
-    next_sweep(2, 1, keep_last, gain_last, XN, V, WN, DN, DI, GD, JD, G, XL)
+    next_sweep(7, 1, keep, gain, X, V, W, D, DI, GD, JD, G, XN, WN, DN)
+    next_sweep(7, 1, keep_last, gain_last, XN, V, WN, DN, DI, GD, JD, G, XL)
 
 
 def bulk_last_kernel(
@@ -480,7 +480,7 @@
             out[l, :, tile] = x
     copy = pltpu.make_async_copy(out, x_hbm, sem)
     copy.start()
-    power_rows(1, groups - 1, 2, XN, V, EH, EV, PA, PB, PD)
+    power_rows(1, groups - 1, 7, XN, V, EH, EV, PA, PB, PD)
     heat = fold_power(0, cell_rows, PA, PB, PD, *fold_matrices(cols, cells))
     for l in range(layers):
         h_ref[l] = heat[l]

time: 26.8 us -> 26.7 us (level)
  the two profiles are of different devices: /device:TPU:0 before, /device:TPU:20 now
where the time goes in v6:
time: 26.7 us; the launch traced here: 26.6 us
  Pallas kernels  14.4 us (54%)
  waiting for transfers between devices  7.5 us (28%)
  starting transfers between devices  3.83 us (14%)
  between operations  0.79 us (3%)
    ppermute x8, waiting for transfers between devices, swap(): lax.ppermute(m, BOTH, tables(mesh_rows, mesh_cols, first))  7.5 us
    ppermute x8, starting transfers between devices, swap(): lax.ppermute(m, BOTH, tables(mesh_rows, mesh_cols, first))  3.83 us
    pallas_call x1, Pallas kernels, on_device(): pl.pallas_call(bulk_first_kernel, out_shape=fields, scratch_shapes=[node_...  3.44 us
    pallas_call x1, Pallas kernels, on_device(): pl.pallas_call(row_strip_kernel, grid=(1,), in_specs=deep_specs + col_spe...  2.35 us
    pallas_call x1, Pallas kernels, on_device(): pl.pallas_call(pack_rows_kernel, grid=(1,), in_specs=row_specs, out_specs...  2.25 us
    pallas_call x1, Pallas kernels, on_device(): pl.pallas_call(bulk_last_kernel, out_shape=(shape(layers, rows, cols), sh...  1.66 us
    pallas_call x1, Pallas kernels, on_device(): pl.pallas_call(bulk_mid_kernel, out_shape=shape(layers, rows, cols), scra...  1.63 us
    pallas_call x1, Pallas kernels, on_device(): pl.pallas_call(warm_kernel, out_shape=shape(layers, cell_rows, cells), co...  1.6 us
  transfers between devices with their start and end apart: 8, of which 6 were waited for; matrix products, arithmetic and copies ran while one was open for 0% of the time, Pallas kernels for 34%

profile of v6, /device:TPU:20, one launch (start us, length us, event | category | flops | bytes accessed | tf_op | source)
XLA Modules:
  0.0 26.6 jit_solution(8265796705746014269)
XLA Ops:
  0.6 0.0 copy-start.1
  0.6 0.0 copy-start.2
  0.7 0.0 copy-start.5
  0.7 0.0 copy-start
  0.7 0.0 copy-start.3
  0.7 0.0 copy-start.4
  0.7 2.3 %pack_rows.1 = (f32[8,8,512]{2,1,0:T(8,128)}, f32[8,8,512]{2,1,0:T(8,128)}) custom-call(f32[4,128,512]{2,1,0:T(8,128)} %x_r.1, f32[4,128,512]{2,1,0:T(8,128)} %x_r.1, f32[4,128,512]{2,1,0:T(8,128)} %b_b.1, f32[4,128,512]{2,1,0:T(8,128)} %b_b.1, f32[4,32,128]{2,1,0:T(8,128)} %w_ref.5, f32[4,32,128]{2,1,0:T(8,128)} %w_ref.5, s32[3,128,512]{2,1,0:T(8,128)} %V.3, ...), custom_call_target="tpu_custom_call" | custom-call | tf_op jit(solution)/shard_map/pack_rows/pallas_call | solution.py:708
  2.9 0.0 collective-permute-start
  2.9 1.5 %collective-permute-start.1 = (f32[8,8,512]{2,1,0:T(8,128)}, f32[8,8,512]{2,1,0:T(8,128)S(1)}, u32[]{:S(2)}, u32[]{:S(2)}) collective-permute-start(f32[8,8,512]{2,1,0:T(8,128)} %get-tuple-element.39), channel_id=1, source_target_pairs={{0,1},{1,0},{2,3},{3,2},{4,8},{5,9},{6,10},{7,11},{8,4},{9,5},{10,... | collective-permute-start | bytes 393224 | tf_op jit(solution)/shard_map/ppermute | solution.py:698
  4.5 0.0 copy-done.1
  4.5 0.0 copy-done.2
  4.5 0.0 copy-done.5
  4.5 0.0 copy-done
  4.5 0.0 copy-done.3
  4.5 0.0 copy-done.4
  4.5 3.4 %bulk_first.1 = (f32[4,128,512]{2,1,0:T(8,128)S(1)}, f32[4,128,512]{2,1,0:T(8,128)S(1)}, f32[4,128,512]{2,1,0:T(8,128)S(1)}, f32[4,128,512]{2,1,0:T(8,128)S(1)},...) custom-call(f32[4,128,512]{2,1,0:T(8,128)S(1)} %copy-done.1, ...), custom_call_target="tpu_custom_call" | custom-call | flops 10485760 | bytes 15728640 | tf_op jit(solution)/shard_map/bulk_first/pallas_call | solution.py:721
  8.0 0.0 collective-permute-done.re_ref
  8.0 1.6 %collective-permute-done.1.ro_ref = f32[8,8,512]{2,1,0:T(8,128)S(1)} collective-permute-done((f32[8,8,512]{2,1,0:T(8,128)}, f32[8,8,512]{2,1,0:T(8,128)S(1)}, u32[]{:S(2)}, u32[]{:S(2)}) %collective-permute-start.1) | collective-permute-done | bytes 131104 | tf_op jit(solution)/shard_map/ppermute | solution.py:698
  9.6 0.2 pack_cols.1
  9.7 1.6 %collective-permute-start.2 = (f32[88,128]{1,0:T(8,128)S(1)}, f32[88,128]{1,0:T(8,128)S(1)}, u32[]{:S(2)}, u32[]{:S(2)}) collective-permute-start(f32[88,128]{1,0:T(8,128)S(1)} %get-tuple-element.44), channel_id=1, source_target_pairs={{0,1},{1,0},{2,3},{3,2},{4,5},{5,4},{6,7},{7,6},{8,9},{9,8},{10,11... | collective-permute-start | bytes 135176 | tf_op jit(solution)/shard_map/ppermute | solution.py:698
  11.4 0.0 collective-permute-start.3
  11.4 2.3 %row_strip.1 = (f32[4,32,512]{2,1,0:T(8,128)S(1)}, f32[4,8,128]{2,1,0:T(8,128)S(1)}, f32[15,80,128]{2,1,0:T(8,128)S(1)}) custom-call(f32[4,128,512]{2,1,0:T(8,128)S(1)} %copy-done.1, f32[4,128,512]{2,1,0:T(8,128)S(1)} %copy-done.1, f32[4,128,512]{2,1,0:T(8,128)S(1)} %get-tuple-element.34.G.g_t.g_b.g_l.g_r, ...), custom_call_target="tpu_custom_call" | custom-call | flops 10485760 | bytes 5242880 | tf_op jit(solution)/shard_map/row_strip/pallas_call | solution.py:758
  13.7 0.1 collective-permute-done.2.ce_ref
  13.9 1.6 %collective-permute-done.3.co_ref = f32[88,128]{1,0:T(8,128)S(1)} collective-permute-done((f32[88,128]{1,0:T(8,128)S(1)}, f32[88,128]{1,0:T(8,128)S(1)}, u32[]{:S(2)}, u32[]{:S(2)}) %collective-permute-start.3) | collective-permute-done | bytes 45088 | tf_op jit(solution)/shard_map/ppermute | solution.py:698
  15.4 1.2 %col_strip.1 = (f32[4,128,128]{2,1,0:T(8,128)S(1)}, f32[4,32,128]{2,1,0:T(8,128)S(1)}, f32[4,8,128]{2,1,0:T(8,128)S(1)}) custom-call(f32[15,80,128]{2,1,0:T(8,128)S(1)} %get-tuple-element.41.strip_ref, f32[88,128]{1,0:T(8,128)S(1)} %collective-permute-done.2.ce_ref, f32[88,128]{1,0:T(8,128)S(1)} %collective-permute-done.3.co_ref, ...), custom_call_target="tpu_custom_call" | custom-call | tf_op jit(solution)/shard_map/col_strip/pallas_call | solution.py:770
  16.7 0.1 collective-permute-start.4
  16.8 0.1 collective-permute-start.5
  16.8 1.6 %bulk_mid.1.XN._ = f32[4,128,512]{2,1,0:T(8,128)S(1)} custom-call(f32[4,128,512]{2,1,0:T(8,128)S(1)} %get-tuple-element.28.X, s32[3,128,512]{2,1,0:T(8,128)S(1)} %copy-done, f32[4,128,512]{2,1,0:T(8,128)S(1)} %get-tuple-element.29.W, f32[4,128,512]{2,1,0:T(8,128)S(1)} %get-tuple-element.30.D, f32[4,128,512]{2,1,0:T(8,128)S(1)} %get-tuple-element.31.DI, ...), custom_call_target="tpu_custom_call" | custom-call | flops 5242880 | bytes 5242880 | tf_op jit(solution)/shard_map/bulk_mid/pallas_call | solution.py:780
  18.5 0.0 collective-permute-done.4.re_ref.hre_ref
  18.5 2.4 %collective-permute-done.5.ro_ref.hro_ref = f32[4,8,128]{2,1,0:T(8,128)S(1)} collective-permute-done((f32[4,8,128]{2,1,0:T(8,128)S(1)}, f32[4,8,128]{2,1,0:T(8,128)S(1)}, u32[]{:S(2)}, u32[]{:S(2)}) %collective-permute-start.5) | collective-permute-done | bytes 16416 | tf_op jit(solution)/shard_map/ppermute | solution.py:698
  20.9 0.1 pack_heat.1
  21.0 0.1 collective-permute-start.6
  21.1 0.4 %collective-permute-start.7 = (f32[48,128]{1,0:T(8,128)S(1)}, f32[48,128]{1,0:T(8,128)S(1)}, u32[]{:S(2)}, u32[]{:S(2)}) collective-permute-start(f32[48,128]{1,0:T(8,128)S(1)} %get-tuple-element.53), channel_id=1, source_target_pairs={{0,4},{1,2},{2,1},{3,7},{4,0},{5,6},{6,5},{7,3},{8,12},{9,10},{10,... | collective-permute-start | bytes 73736 | tf_op jit(solution)/shard_map/ppermute | solution.py:698
  21.5 1.7 %bulk_last.1 = (f32[4,128,512]{2,1,0:T(8,128)}, f32[4,32,128]{2,1,0:T(8,128)S(1)}) custom-call(f32[4,128,512]{2,1,0:T(8,128)S(1)} %bulk_mid.1.XN._, s32[3,128,512]{2,1,0:T(8,128)S(1)} %copy-done, f32[4,128,512]{2,1,0:T(8,128)S(1)} %get-tuple-element.35.EH, f32[4,128,512]{2,1,0:T(8,128)S(1)} %get-tuple-element.36.EV, ...), custom_call_target="tpu_custom_call" | custom-call | flops 10485760 | bytes 15728640 | tf_op jit(solution)/shard_map/bulk_last/pallas_call | solution.py:800
  23.2 1.7 %collective-permute-done.6.hce_ref = f32[48,128]{1,0:T(8,128)S(1)} collective-permute-done((f32[48,128]{1,0:T(8,128)S(1)}, f32[48,128]{1,0:T(8,128)S(1)}, u32[]{:S(2)}, u32[]{:S(2)}) %collective-permute-start.6) | collective-permute-done | bytes 24608 | tf_op jit(solution)/shard_map/ppermute | solution.py:698
  24.9 0.1 collective-permute-done.7.hco_ref
  25.0 1.6 %warm.1 = f32[4,32,128]{2,1,0:T(8,128)} custom-call(f32[4,32,128]{2,1,0:T(8,128)S(1)} %copy-done.5, f32[4,32,128]{2,1,0:T(8,128)S(1)} %get-tuple-element.49.h_ref, f32[4,8,128]{2,1,0:T(8,128)S(1)} %get-tuple-element.50.hm_ref, f32[4,32,128]{2,1,0:T(8,128)S(1)} %get-tuple-element.51.h_ref.hc_ref, f32[8,8,512]{2,1,0:T(8,128)S(1)} %collective-permute-done.re_ref, ...), custom_call_target="tpu_custom_call" | custom-call | tf_op jit(solution)/shard_map/warm/pallas_call | solution.py:810
Async XLA Ops:
  0.6 3.9 %copy-start.1 = (f32[4,128,512]{2,1,0:T(8,128)S(1)}, f32[4,128,512]{2,1,0:T(8,128)}, u32[]{:S(2)}) copy-start(f32[4,128,512]{2,1,0:T(8,128)} %x_r.1) | copy-start | bytes 3145732
  0.6 3.9 %copy-start.2 = (f32[4,128,512]{2,1,0:T(8,128)S(1)}, f32[4,128,512]{2,1,0:T(8,128)}, u32[]{:S(2)}) copy-start(f32[4,128,512]{2,1,0:T(8,128)} %b_b.1) | copy-start | bytes 3145732
  0.7 3.8 %copy-start.5 = (f32[4,32,128]{2,1,0:T(8,128)S(1)}, f32[4,32,128]{2,1,0:T(8,128)}, u32[]{:S(2)}) copy-start(f32[4,32,128]{2,1,0:T(8,128)} %w_ref.5) | copy-start | bytes 196612
  0.7 3.8 %copy-start = (s32[3,128,512]{2,1,0:T(8,128)S(1)}, s32[3,128,512]{2,1,0:T(8,128)}, u32[]{:S(2)}) copy-start(s32[3,128,512]{2,1,0:T(8,128)} %V.3) | copy-start | bytes 2359300
  0.7 3.8 %copy-start.3 = (s32[4,128,512]{2,1,0:T(8,128)S(1)}, s32[4,128,512]{2,1,0:T(8,128)}, u32[]{:S(2)}) copy-start(s32[4,128,512]{2,1,0:T(8,128)} %f_b.1) | copy-start | bytes 3145732
  0.7 3.8 %copy-start.4 = (f32[4,128,512]{2,1,0:T(8,128)S(1)}, f32[4,128,512]{2,1,0:T(8,128)}, u32[]{:S(2)}) copy-start(f32[4,128,512]{2,1,0:T(8,128)} %a_b.1) | copy-start | bytes 3145732
  2.9 5.0 %collective-permute-start = (f32[8,8,512]{2,1,0:T(8,128)}, f32[8,8,512]{2,1,0:T(8,128)S(1)}, u32[]{:S(2)}, u32[]{:S(2)}) collective-permute-start(f32[8,8,512]{2,1,0:T(8,128)} %get-tuple-element.38), channel_id=1, source_target_pairs={{0,4},{1,5},{2,6},{3,7},{4,0},{5,1},{6,2},{7,3},{8,12},{9,13},{10,... | collective-permute-start | bytes 393224 | tf_op jit(solution)/shard_map/ppermute | solution.py:698
  2.9 6.6 %collective-permute-start.1 = (f32[8,8,512]{2,1,0:T(8,128)}, f32[8,8,512]{2,1,0:T(8,128)S(1)}, u32[]{:S(2)}, u32[]{:S(2)}) collective-permute-start(f32[8,8,512]{2,1,0:T(8,128)} %get-tuple-element.39), channel_id=1, source_target_pairs={{0,1},{1,0},{2,3},{3,2},{4,8},{5,9},{6,10},{7,11},{8,4},{9,5},{10,... | collective-permute-start | bytes 393224 | tf_op jit(solution)/shard_map/ppermute | solution.py:698
  9.7 4.1 %collective-permute-start.2 = (f32[88,128]{1,0:T(8,128)S(1)}, f32[88,128]{1,0:T(8,128)S(1)}, u32[]{:S(2)}, u32[]{:S(2)}) collective-permute-start(f32[88,128]{1,0:T(8,128)S(1)} %get-tuple-element.44), channel_id=1, source_target_pairs={{0,1},{1,0},{2,3},{3,2},{4,5},{5,4},{6,7},{7,6},{8,9},{9,8},{10,11... | collective-permute-start | bytes 135176 | tf_op jit(solution)/shard_map/ppermute | solution.py:698
  11.4 4.0 %collective-permute-start.3 = (f32[88,128]{1,0:T(8,128)S(1)}, f32[88,128]{1,0:T(8,128)S(1)}, u32[]{:S(2)}, u32[]{:S(2)}) collective-permute-start(f32[88,128]{1,0:T(8,128)S(1)} %get-tuple-element.45), channel_id=1, source_target_pairs={{0,4},{1,2},{2,1},{3,7},{4,0},{5,6},{6,5},{7,3},{8,12},{9,10},{10,... | collective-permute-start | bytes 135176 | tf_op jit(solution)/shard_map/ppermute | solution.py:698
  16.7 1.8 %collective-permute-start.4 = (f32[4,8,128]{2,1,0:T(8,128)S(1)}, f32[4,8,128]{2,1,0:T(8,128)S(1)}, u32[]{:S(2)}, u32[]{:S(2)}) collective-permute-start(f32[4,8,128]{2,1,0:T(8,128)S(1)} %get-tuple-element.50.hm_ref), channel_id=1, source_target_pairs={{0,4},{1,5},{2,6},{3,7},{4,0},{5,1},{6,2},{7,3},{8,12},{9,13},{10,... | collective-permute-start | bytes 49160 | tf_op jit(solution)/shard_map/ppermute | solution.py:698
  16.8 4.1 %collective-permute-start.5 = (f32[4,8,128]{2,1,0:T(8,128)S(1)}, f32[4,8,128]{2,1,0:T(8,128)S(1)}, u32[]{:S(2)}, u32[]{:S(2)}) collective-permute-start(f32[4,8,128]{2,1,0:T(8,128)S(1)} %get-tuple-element.50.hm_ref), channel_id=1, source_target_pairs={{0,1},{1,0},{2,3},{3,2},{4,8},{5,9},{6,10},{7,11},{8,4},{9,5},{10,... | collective-permute-start | bytes 49160 | tf_op jit(solution)/shard_map/ppermute | solution.py:698
  21.0 3.9 %collective-permute-start.6 = (f32[48,128]{1,0:T(8,128)S(1)}, f32[48,128]{1,0:T(8,128)S(1)}, u32[]{:S(2)}, u32[]{:S(2)}) collective-permute-start(f32[48,128]{1,0:T(8,128)S(1)} %get-tuple-element.52), channel_id=1, source_target_pairs={{0,1},{1,0},{2,3},{3,2},{4,5},{5,4},{6,7},{7,6},{8,9},{9,8},{10,11... | collective-permute-start | bytes 73736 | tf_op jit(solution)/shard_map/ppermute | solution.py:698
  21.1 3.9 %collective-permute-start.7 = (f32[48,128]{1,0:T(8,128)S(1)}, f32[48,128]{1,0:T(8,128)S(1)}, u32[]{:S(2)}, u32[]{:S(2)}) collective-permute-start(f32[48,128]{1,0:T(8,128)S(1)} %get-tuple-element.53), channel_id=1, source_target_pairs={{0,4},{1,2},{2,1},{3,7},{4,0},{5,6},{6,5},{7,3},{8,12},{9,10},{10,... | collective-permute-start | bytes 73736 | tf_op jit(solution)/shard_map/ppermute | solution.py:698
